TPU v7x, 32 devices: a whole 2x2x4 slice. The times are simulated.
32 devices in a mesh: dp: 4 (over y, core), blk: 8 (over z, x).
Axes of the slice: x: 2, y: 2, z: 4, core: 2. Of those that a mesh axis runs over, the one named last changes fastest.
Arguments:
- counts: int32 [8, 512, 1024], P('dp', 'blk'), may hold values from 0 to 15
- coords: int32 [2, 8, 512], P(None, 'dp', 'blk'), may hold values from 0 to 1023
- segment_ids: int32 [8, 512], P('dp', 'blk'), may hold values from 0 to 511, as said below
- logit_grad: bfloat16 [8, 512, 1024], P('dp', 'blk'), may hold values from -5 to 5
- enc_weight: bfloat16 [1024, 1024], P('blk'), may hold values from -0.09375 to 0.09375
- qkv_weight: bfloat16 [1024, 3072], P('blk'), may hold values from -0.1875 to 0.1875
- out_weight: bfloat16 [1024, 1024], P('blk'), may hold values from -0.75 to 0.75
- up_weight: bfloat16 [1024, 4096], P('blk'), may hold values from -0.1875 to 0.1875
- down_weight: bfloat16 [4096, 1024], P('blk'), may hold values from -0.09375 to 0.09375
- dec_weight: bfloat16 [1024, 1024], P('blk'), may hold values from -0.1875 to 0.1875
- dec_bias: bfloat16 [1024], P('blk'), may hold values from -4 to 4
- norm1_gain: bfloat16 [1024], P('blk'), may hold values from 0.5 to 1.5
- norm1_shift: bfloat16 [1024], P('blk'), may hold values from -3 to 3
- norm2_gain: bfloat16 [1024], P('blk'), may hold values from 0.5 to 1.5
- norm2_shift: bfloat16 [1024], P('blk'), may hold values from -3 to 3
Outputs:
- logits: bfloat16 [8, 512, 1024], P('dp', 'blk')
- input_grad: bfloat16 [8, 512, 1024], P('dp', 'blk')
- grad_enc_weight: float32 [1024, 1024], P('blk')
- grad_qkv_weight: float32 [1024, 3072], P('blk')
- grad_out_weight: float32 [1024, 1024], P('blk')
- grad_up_weight: float32 [1024, 4096], P('blk')
- grad_down_weight: float32 [4096, 1024], P('blk')
- grad_dec_weight: float32 [1024, 1024], P('blk')
- grad_dec_bias: float32 [1024], P('blk')
- grad_norm1_gain: float32 [1024], P('blk')
- grad_norm1_shift: float32 [1024], P('blk')
- grad_norm2_gain: float32 [1024], P('blk')
- grad_norm2_shift: float32 [1024], P('blk')
Inputs may be any that keep to these rules, and one draw needn't show every extreme that they name: `segment_ids`: Non-decreasing along each sequence; in each group of 2 sequences on one index of dp, one sequence is a single segment, and in every other sequence the last cell is a segment of its own with id 512 - 1.
All inputs are finite; a program needn't handle non-finite values.
Results may differ from a plain program's by a relative error of at most 0.02.
Values may be sent and summed in bfloat16 or wider, within the bound.
No kernel may reach another device: no remote copies, remote signals or barrier semaphores. Data moves between devices by JAX's collectives and lax.ppermute only.
A program may use at most 448 MiB of HBM per device.

v0:
```python
import math

import jax
import jax.numpy as jnp
from jax import lax
from jax.sharding import PartitionSpec as P

HEADS = 16


NEGATIVE = -1e30
EPSILON = 1e-05


def layer_norm(inputs, gain_vec, shift_vec):
    centre = inputs - jnp.mean(inputs, axis=-1, keepdims=True)
    spread = jnp.mean(centre * centre, axis=-1, keepdims=True)
    return centre * lax.rsqrt(spread + EPSILON) * gain_vec + shift_vec


def sinusoids(coords, width):
    quarter = width // 4
    frequency = jnp.exp(jnp.arange(quarter, dtype=jnp.float32) * (-math.log(10000.0) / quarter))
    first_angle = coords[0].astype(jnp.float32)[..., None] * frequency
    second_angle = coords[1].astype(jnp.float32)[..., None] * frequency
    return jnp.concatenate(
        [jnp.sin(first_angle), jnp.cos(first_angle), jnp.sin(second_angle), jnp.cos(second_angle)],
        axis=-1,
    )


def inner(left, right):
    return lax.dot_general(
        left, right, (((0,), (0,)), ((), ())), preferred_element_type=jnp.float32
    )


def times_t(left, right):
    return lax.dot_general(
        left, right, (((1,), (1,)), ((), ())), preferred_element_type=jnp.float32
    )


def local(
    counts,
    coords,
    segment_ids,
    logit_grad,
    enc_weight,
    qkv_weight,
    out_weight,
    up_weight,
    down_weight,
    dec_weight,
    dec_bias,
    norm1_gain,
    norm1_shift,
    norm2_gain,
    norm2_shift,
):
    gathered = (
        lax.all_gather(enc_weight, "blk", axis=0, tiled=True),
        lax.all_gather(qkv_weight, "blk", axis=0, tiled=True),
        lax.all_gather(out_weight, "blk", axis=0, tiled=True),
        lax.all_gather(up_weight, "blk", axis=0, tiled=True),
        lax.all_gather(down_weight, "blk", axis=0, tiled=True),
        lax.all_gather(dec_weight, "blk", axis=0, tiled=True),
        lax.all_gather(dec_bias, "blk", axis=0, tiled=True),
        lax.all_gather(norm1_gain, "blk", axis=0, tiled=True),
        lax.all_gather(norm1_shift, "blk", axis=0, tiled=True),
        lax.all_gather(norm2_gain, "blk", axis=0, tiled=True),
        lax.all_gather(norm2_shift, "blk", axis=0, tiled=True),
    )
    w_enc, w_qkv, w_out, w_up, w_down, w_dec, b_dec, gain_one, shift_one, gain_two, shift_two = (
        gathered
    )
    seg_all = lax.all_gather(segment_ids, "blk", axis=1, tiled=True)
    seq_count, cell_count, gene_count = counts.shape
    width = w_enc.shape[1]
    head_count = HEADS
    head_size = width // head_count
    scaling = head_size ** (-0.5)
    row_count = seq_count * cell_count
    express = (
        jnp.log1p(counts.astype(jnp.float32)).astype(jnp.bfloat16).reshape(row_count, gene_count)
    )
    embed = sinusoids(coords, width).reshape(row_count, width)
    hidden0 = jnp.dot(express, w_enc, preferred_element_type=jnp.float32) + embed
    gain_one32 = gain_one.astype(jnp.float32)
    shift_one32 = shift_one.astype(jnp.float32)
    gain_two32 = gain_two.astype(jnp.float32)
    shift_two32 = shift_two.astype(jnp.float32)
    normed1 = layer_norm(hidden0, gain_one32, shift_one32).astype(jnp.bfloat16)
    qkv = jnp.dot(normed1, w_qkv, preferred_element_type=jnp.float32).astype(jnp.bfloat16)
    queries = qkv[:, :width].reshape(seq_count, cell_count, head_count, head_size)
    key_rows = qkv[:, width : 2 * width].reshape(seq_count, cell_count, head_count, head_size)
    values = qkv[:, 2 * width :].reshape(seq_count, cell_count, head_count, head_size)

    def masked_scores(query_part, key_part, seg_query, seg_key):
        scores = (
            jnp.einsum("sqhe,skhe->shqk", query_part, key_part, preferred_element_type=jnp.float32)
            * scaling
        )
        return jnp.where(seg_query[:, None, :, None] == seg_key[:, None, None, :], scores, NEGATIVE)

    start_max = jnp.full((seq_count, head_count, cell_count), NEGATIVE, jnp.float32)
    piece = (
        lax.all_gather(key_rows, "blk", axis=1, tiled=True),
        lax.all_gather(values, "blk", axis=1, tiled=True),
    )
    seg_part = seg_all
    incoming = (piece[0], piece[1], seg_part)
    running_max = start_max
    key_part, value_part, context_seg_part = incoming
    query_part = queries
    scores = masked_scores(query_part, key_part, segment_ids, context_seg_part)
    newest = jnp.maximum(running_max, jnp.max(scores, axis=-1))
    expo = jnp.exp(scores - newest[..., None])
    running_sum = jnp.sum(expo, axis=-1)
    update = jnp.einsum(
        "shqk,skhe->sqhe", expo.astype(jnp.bfloat16), value_part, preferred_element_type=jnp.float32
    )
    weighted = update
    running_max, running_sum, weighted = (newest, running_sum, weighted)
    context32 = weighted / jnp.transpose(running_sum, (0, 2, 1))[..., None]
    logsum = jnp.transpose(running_max + jnp.log(running_sum), (0, 2, 1))
    context = context32.astype(jnp.bfloat16).reshape(row_count, width)
    hidden1 = hidden0 + jnp.dot(context, w_out, preferred_element_type=jnp.float32)
    normed2 = layer_norm(hidden1, gain_two32, shift_two32).astype(jnp.bfloat16)
    up_value = jnp.dot(normed2, w_up, preferred_element_type=jnp.float32)
    active = jax.nn.gelu(up_value).astype(jnp.bfloat16)
    hidden2 = hidden1 + jnp.dot(active, w_down, preferred_element_type=jnp.float32)
    hidden2_low = hidden2.astype(jnp.bfloat16)
    logits = (
        jnp.dot(hidden2_low, w_dec, preferred_element_type=jnp.float32) + b_dec.astype(jnp.float32)
    ).astype(jnp.bfloat16)
    regathered = (
        lax.all_gather(enc_weight, "blk", axis=0, tiled=True),
        lax.all_gather(qkv_weight, "blk", axis=0, tiled=True),
        lax.all_gather(out_weight, "blk", axis=0, tiled=True),
        lax.all_gather(up_weight, "blk", axis=0, tiled=True),
        lax.all_gather(down_weight, "blk", axis=0, tiled=True),
        lax.all_gather(dec_weight, "blk", axis=0, tiled=True),
        lax.all_gather(dec_bias, "blk", axis=0, tiled=True),
        lax.all_gather(norm1_gain, "blk", axis=0, tiled=True),
        lax.all_gather(norm1_shift, "blk", axis=0, tiled=True),
        lax.all_gather(norm2_gain, "blk", axis=0, tiled=True),
        lax.all_gather(norm2_shift, "blk", axis=0, tiled=True),
    )
    w_enc, w_qkv, w_out, w_up, w_down, w_dec = regathered[:6]
    cotangent = logit_grad.reshape(row_count, gene_count)
    grad_dec = inner(hidden2_low, cotangent)
    grad_bias = jnp.sum(cotangent.astype(jnp.float32), axis=0)
    grad_h2 = times_t(cotangent, w_dec)
    grad_down = grad_h2.astype(jnp.bfloat16)
    grad_w_down = inner(active, grad_down)
    grad_active = times_t(grad_down, w_down)
    gelu_pull = jax.vjp(jax.nn.gelu, up_value)[1]
    grad_up = gelu_pull(grad_active)[0].astype(jnp.bfloat16)
    grad_w_up = inner(normed2, grad_up)
    grad_normed2 = times_t(grad_up, w_up)
    norm_pull_two = jax.vjp(layer_norm, hidden1, gain_two32, shift_two32)[1]
    part_two, grad_gain_two, grad_shift_two = norm_pull_two(grad_normed2)
    grad_h1 = grad_h2 + part_two
    grad_attn = grad_h1.astype(jnp.bfloat16)
    grad_w_out = inner(context, grad_attn)
    grad_context = (
        times_t(grad_attn, w_out)
        .astype(jnp.bfloat16)
        .reshape(seq_count, cell_count, head_count, head_size)
    )
    delta = jnp.sum(grad_context.astype(jnp.float32) * context32, axis=-1)
    logsum_all, delta_all = (
        lax.all_gather(logsum, "blk", axis=1, tiled=True),
        lax.all_gather(delta, "blk", axis=1, tiled=True),
    )
    piece = (
        lax.all_gather(key_rows, "blk", axis=1, tiled=True),
        lax.all_gather(values, "blk", axis=1, tiled=True),
    )
    seg_part = seg_all
    incoming = (piece[0], piece[1], seg_part)
    key_part, value_part, query_seg_part = incoming
    query_part = queries
    gradout_part = grad_context
    logsum_part = logsum
    delta_part = delta
    scores = masked_scores(query_part, key_part, segment_ids, query_seg_part)
    probs = jnp.exp(scores - jnp.transpose(logsum_part, (0, 2, 1))[..., None])
    dprob = jnp.einsum(
        "sqhe,skhe->shqk", gradout_part, value_part, preferred_element_type=jnp.float32
    )
    dscore = (probs * (dprob - jnp.transpose(delta_part, (0, 2, 1))[..., None])).astype(
        jnp.bfloat16
    )
    grad_queries = (
        jnp.einsum("shqk,skhe->sqhe", dscore, key_part, preferred_element_type=jnp.float32)
        * scaling
    )
    piece = (
        lax.all_gather(queries, "blk", axis=1, tiled=True),
        lax.all_gather(grad_context, "blk", axis=1, tiled=True),
    )
    seg_part = seg_all
    logsum_part = logsum_all
    delta_part = delta_all
    incoming = (piece[0], piece[1], logsum_part, delta_part, seg_part)
    query_part, gradout_part, key_logsum_part, key_delta_part, key_seg_part = incoming
    key_part = key_rows
    scores = masked_scores(query_part, key_part, key_seg_part, segment_ids)
    probs = jnp.exp(scores - jnp.transpose(key_logsum_part, (0, 2, 1))[..., None])
    grad_values = jnp.einsum(
        "shqk,sqhe->skhe",
        probs.astype(jnp.bfloat16),
        gradout_part,
        preferred_element_type=jnp.float32,
    )
    dprob = jnp.einsum("sqhe,skhe->shqk", gradout_part, values, preferred_element_type=jnp.float32)
    dscore = (probs * (dprob - jnp.transpose(key_delta_part, (0, 2, 1))[..., None])).astype(
        jnp.bfloat16
    )
    grad_keys = (
        jnp.einsum("shqk,sqhe->skhe", dscore, query_part, preferred_element_type=jnp.float32)
        * scaling
    )
    grad_keys, grad_values = (grad_keys, grad_values)
    grad_qkv = jnp.concatenate(
        [
            grad_queries.reshape(row_count, width),
            grad_keys.reshape(row_count, width),
            grad_values.reshape(row_count, width),
        ],
        axis=1,
    ).astype(jnp.bfloat16)
    grad_w_qkv = inner(normed1, grad_qkv)
    grad_normed1 = times_t(grad_qkv, w_qkv)
    norm_pull_one = jax.vjp(layer_norm, hidden0, gain_one32, shift_one32)[1]
    part_one, grad_gain_one, grad_shift_one = norm_pull_one(grad_normed1)
    grad_h0 = (grad_h1 + part_one).astype(jnp.bfloat16)
    input_grad = (
        times_t(grad_h0, w_enc).astype(jnp.bfloat16).reshape(seq_count, cell_count, gene_count)
    )
    enc_share = lax.psum_scatter(inner(express, grad_h0), "blk", scatter_dimension=0, tiled=True)
    shares = (
        lax.psum_scatter(grad_w_qkv, "blk", scatter_dimension=0, tiled=True),
        lax.psum_scatter(grad_w_out, "blk", scatter_dimension=0, tiled=True),
        lax.psum_scatter(grad_w_up, "blk", scatter_dimension=0, tiled=True),
        lax.psum_scatter(grad_w_down, "blk", scatter_dimension=0, tiled=True),
        lax.psum_scatter(grad_dec, "blk", scatter_dimension=0, tiled=True),
        lax.psum_scatter(grad_bias, "blk", scatter_dimension=0, tiled=True),
        lax.psum_scatter(grad_gain_one, "blk", scatter_dimension=0, tiled=True),
        lax.psum_scatter(grad_shift_one, "blk", scatter_dimension=0, tiled=True),
        lax.psum_scatter(grad_gain_two, "blk", scatter_dimension=0, tiled=True),
        lax.psum_scatter(grad_shift_two, "blk", scatter_dimension=0, tiled=True),
    )
    summed = (
        lax.psum(enc_share.astype(jnp.bfloat16), "dp").astype(jnp.float32),
        lax.psum(shares[0].astype(jnp.bfloat16), "dp").astype(jnp.float32),
        lax.psum(shares[1].astype(jnp.bfloat16), "dp").astype(jnp.float32),
        lax.psum(shares[2].astype(jnp.bfloat16), "dp").astype(jnp.float32),
        lax.psum(shares[3].astype(jnp.bfloat16), "dp").astype(jnp.float32),
        lax.psum(shares[4].astype(jnp.bfloat16), "dp").astype(jnp.float32),
        lax.psum(shares[5].astype(jnp.bfloat16), "dp").astype(jnp.float32),
        lax.psum(shares[6].astype(jnp.bfloat16), "dp").astype(jnp.float32),
        lax.psum(shares[7].astype(jnp.bfloat16), "dp").astype(jnp.float32),
        lax.psum(shares[8].astype(jnp.bfloat16), "dp").astype(jnp.float32),
        lax.psum(shares[9].astype(jnp.bfloat16), "dp").astype(jnp.float32),
    )
    return (
        logits.reshape(seq_count, cell_count, gene_count),
        input_grad,
        summed[0],
        summed[1],
        summed[2],
        summed[3],
        summed[4],
        summed[5],
        summed[6],
        summed[7],
        summed[8],
        summed[9],
        summed[10],
    )


def solution(mesh):
    in_specs = (
        P("dp", "blk", None),
        P(None, "dp", "blk"),
        P("dp", "blk"),
        P("dp", "blk", None),
        P("blk", None),
        P("blk", None),
        P("blk", None),
        P("blk", None),
        P("blk", None),
        P("blk", None),
        P("blk"),
        P("blk"),
        P("blk"),
        P("blk"),
        P("blk"),
    )
    out_specs = (
        P("dp", "blk", None),
        P("dp", "blk", None),
        P("blk", None),
        P("blk", None),
        P("blk", None),
        P("blk", None),
        P("blk", None),
        P("blk", None),
        P("blk"),
        P("blk"),
        P("blk"),
        P("blk"),
        P("blk"),
    )
    return jax.shard_map(local, mesh=mesh, in_specs=in_specs, out_specs=out_specs, check_vma=False)
```

profile of v0, /device:TPU:1, one launch (start us, length us, event | category | flops | bytes accessed | tf_op | source)
XLA Modules:
  0.0 1968.9 jit_solution(17997505387084995258)
XLA Ops:
  10.3 17.9 all-gather.1
  28.2 12.9 all-gather
  43.4 17.1 all-gather.17.cloned.1.call-done
  62.8 98.0 %all-gather.19.cloned.1.call-done = bf16[1024,3072]{1,0:T(8,128)(2,1)} async-done(((bf16[128,3072]{1,0:T(8,128)(2,1)}), bf16[1024,3072]{1,0:T(8,128)(2,1)}) %all-gather.19.cloned.1.call-update) | async-done | bytes 6291472 | tf_op jit(solution)/shard_map/all_gather | solution.py:63
  169.6 14.7 all-gather.2
  184.4 13.2 all-gather.4
  197.6 14.7 all-gather.3
  217.3 67.2 %all-gather.23.cloned.1.call-done = bf16[2,512,16,64]{3,1,2,0:T(8,128)(2,1)} async-done(((bf16[2,64,16,64]{3,1,2,0:T(8,128)(2,1)}), bf16[2,512,16,64]{3,1,2,0:T(8,128)(2,1)}) %all-gather.23.cloned.1.call-update) | async-done | bytes 2097168 | tf_op jit(solution)/shard_map/all_gather | solution.py:108
  291.6 67.1 %all-gather.21.cloned.1.call-done = bf16[2,512,16,64]{3,2,0,1:T(8,128)(2,1)} async-done(((bf16[2,64,16,64]{3,2,0,1:T(8,128)(2,1)}), bf16[2,512,16,64]{3,2,0,1:T(8,128)(2,1)}) %all-gather.21.cloned.1.call-update) | async-done | bytes 2097168 | tf_op jit(solution)/shard_map/all_gather | solution.py:109
  358.8 9.4 fusion.97
  369.0 39.5 %all-gather.25.cloned.1.call-done = bf16[1024,1024]{1,0:T(8,128)(2,1)} async-done(((bf16[128,1024]{1,0:T(8,128)(2,1)}), bf16[1024,1024]{1,0:T(8,128)(2,1)}) %all-gather.25.cloned.1.call-update) | async-done | bytes 2097168 | tf_op jit(solution)/shard_map/all_gather | solution.py:64
  410.8 123.9 %all-gather.27.cloned.1.call-done = bf16[1024,4096]{1,0:T(8,128)(2,1)} async-done(((bf16[128,4096]{1,0:T(8,128)(2,1)}), bf16[1024,4096]{1,0:T(8,128)(2,1)}) %all-gather.27.cloned.1.call-update) | async-done | bytes 8388624 | tf_op jit(solution)/shard_map/all_gather | solution.py:65
  539.5 120.5 %all-gather.29.cloned.1.call-done = bf16[4096,1024]{1,0:T(8,128)(2,1)} async-done(((bf16[512,1024]{1,0:T(8,128)(2,1)}), bf16[4096,1024]{1,0:T(8,128)(2,1)}) %all-gather.29.cloned.1.call-update) | async-done | bytes 8388624 | tf_op jit(solution)/shard_map/all_gather | solution.py:66
  660.0 7.5 fusion.14
  696.8 12.1 fusion.51
  713.3 29.1 %all_gather.79 = f32[2,512,16]{2,0,1:T(2,128)} all-gather(f32[2,64,16]{2,0,1:T(2,128)} %copy.96), channel_id=1, replica_groups=mesh['dp'=4,'blk'=8] {'blk'}, dimensions={1}, use_global_device_ids=true | all-gather | bytes 73728 | tf_op jit(solution)/shard_map/all_gather | solution.py:175
  744.4 29.4 %all_gather.77 = f32[2,512,16]{2,0,1:T(2,128)} all-gather(f32[2,64,16]{2,0,1:T(2,128)S(1)} %copy.91), channel_id=1, replica_groups=mesh['dp'=4,'blk'=8] {'blk'}, dimensions={1}, use_global_device_ids=true | all-gather | bytes 73728 | tf_op jit(solution)/shard_map/all_gather | solution.py:174
  783.1 32.1 %all-gather.35.cloned.1.call-done = bf16[2,512,16,64]{3,2,0,1:T(8,128)(2,1)} async-done(((bf16[2,64,16,64]{3,2,0,1:T(8,128)(2,1)}), bf16[2,512,16,64]{3,2,0,1:T(8,128)(2,1)}) %all-gather.35.cloned.1.call-update) | async-done | bytes 2097168 | tf_op jit(solution)/shard_map/all_gather | solution.py:202
  820.7 7.1 fusion.57
  854.5 7.5 fusion.90
  862.3 9.6 fusion.91
  873.0 8.1 fusion.70
  881.2 25.5 %reduce-scatter.11.cloned.1.call-done = f32[128,1024]{1,0:T(8,128)} async-done(((f32[1024,1024]{1,0:T(8,128)}), f32[128,1024]{1,0:T(8,128)}) %reduce-scatter.11.cloned.1.call-update) | async-done | bytes 524304 | tf_op jit(solution)/shard_map/reduce_scatter | solution.py:246
  908.5 89.8 %reduce-scatter.17.cloned.1.call-done = f32[128,1024]{1,0:T(8,128)} async-done(((f32[1024,1024]{1,0:T(8,128)}), f32[128,1024]{1,0:T(8,128)}) %reduce-scatter.17.cloned.1.call-update) | async-done | bytes 524304 | tf_op jit(solution)/shard_map/reduce_scatter | solution.py:249
  1000.0 90.1 %reduce-scatter.7.cloned.1.call-done = f32[128,1024]{0,1:T(8,128)} async-done(((f32[1024,1024]{0,1:T(8,128)}), f32[128,1024]{0,1:T(8,128)}) %reduce-scatter.7.cloned.1.call-update) | async-done | bytes 524304 | tf_op jit(solution)/shard_map/reduce_scatter | solution.py:243
  1091.9 209.3 %reduce-scatter.9.cloned.1.call-done = f32[128,3072]{1,0:T(8,128)} async-done(((f32[1024,3072]{1,0:T(8,128)}), f32[128,3072]{1,0:T(8,128)}) %reduce-scatter.9.cloned.1.call-update) | async-done | bytes 1572880 | tf_op jit(solution)/shard_map/reduce_scatter | solution.py:245
  1303.6 283.1 %reduce-scatter.13.cloned.1.call-done = f32[128,4096]{1,0:T(8,128)} async-done(((f32[1024,4096]{1,0:T(8,128)}), f32[128,4096]{1,0:T(8,128)}) %reduce-scatter.13.cloned.1.call-update) | async-done | bytes 2097168 | tf_op jit(solution)/shard_map/reduce_scatter | solution.py:247
  1589.4 282.3 %reduce-scatter.15.cloned.1.call-done = f32[512,1024]{1,0:T(8,128)} async-done(((f32[4096,1024]{1,0:T(8,128)}), f32[512,1024]{1,0:T(8,128)}) %reduce-scatter.15.cloned.1.call-update) | async-done | bytes 2097168 | tf_op jit(solution)/shard_map/reduce_scatter | solution.py:248
  1874.5 14.9 all-gather.5
  1893.5 26.3 %all-reduce.5 = (bf16[1024]{0:T(1024)(128)(2,1)S(1)}, bf16[1024]{0:T(1024)(128)(2,1)S(1)}, bf16[1024]{0:T(1024)(128)(2,1)S(1)}, bf16[1024]{0:T(1024)(128)(2,1)S(1)}, bf16[1024]{0:T(1024)(128)(2,1)S(1)}) all-reduce(f32[1024]{0:T(1024)S(1)} %convert_reduce_fusion, ...), channel_id=8, replica_groups=mesh['dp'=4,'blk'=8] {'blk'}, use_global_device_ids=true, to_apply=%region_24.25.clone | all-reduce | flops 5120 | bytes 30720
  1920.2 16.0 all-reduce.6
  1940.3 11.6 all-reduce.10.cloned.1.call-done
  (207 shorter events, 145.7 us)
Async XLA Ops:
  7.2 53.3 %all-gather.17.cloned.1.call-start = ((), (), s32[]{:S(2)}) async-start(), calls=%async_computation.6 | async-start | bytes 2359296 | tf_op jit(solution)/shard_map/all_gather | solution.py:62
  7.9 152.9 %all-gather.19.cloned.1.call-start = ((), (), s32[]{:S(2)}) async-start(), calls=%async_computation.7 | async-start | bytes 7077888 | tf_op jit(solution)/shard_map/all_gather | solution.py:63
  8.7 203.8 %all-gather.31.cloned.1.call-start = ((), (), s32[]{:S(2)}) async-start(), calls=%async_computation.13 | async-start | bytes 2359296 | tf_op jit(solution)/shard_map/all_gather | solution.py:67
  9.4 275.1 %all-gather.23.cloned.1.call-start = ((), (), s32[]{:S(2)}) async-start(), calls=%async_computation.9 | async-start | bytes 4718592 | tf_op jit(solution)/shard_map/all_gather | solution.py:108
  62.8 102.0 %copy-start.30 = (f32[128]{0:T(128)}, f32[128]{0:T(128)S(1)}, u32[]{:S(2)}) copy-start(f32[128]{0:T(128)S(1)} %multiply_reduce_fusion.6) | copy-start | bytes 1540
  62.8 101.9 %copy-start.24 = (f32[128]{0:T(128)}, f32[128]{0:T(128)S(1)}, u32[]{:S(2)}) copy-start(f32[128]{0:T(128)S(1)} %fusion.76) | copy-start | bytes 1540
  164.7 47.8 %copy-start.13 = (bf16[2,64,1024]{2,1,0:T(8,128)(2,1)S(1)}, bf16[2,64,1024]{2,1,0:T(8,128)(2,1)}, u32[]{:S(2)}) copy-start(bf16[2,64,1024]{2,1,0:T(8,128)(2,1)} %param.18) | copy-start | bytes 786436
  165.1 50.6 %copy-start.6 = (bf16[2,64,16,64]{3,2,1,0:T(8,128)(2,1)}, bf16[2,64,16,64]{3,2,1,0:T(8,128)(2,1)S(1)}, u32[]{:S(2)}) copy-start(bf16[2,64,16,64]{3,2,1,0:T(8,128)(2,1)S(1)} %reshape.192) | copy-start | bytes 786436
  166.1 192.7 %all-gather.21.cloned.1.call-start = ((), (), s32[]{:S(2)}) async-start(), calls=%async_computation.8 | async-start | bytes 4718592 | tf_op jit(solution)/shard_map/all_gather | solution.py:109
  166.5 50.5 %copy-start.16 = (bf16[2,64,16,64]{3,2,1,0:T(8,128)(2,1)}, bf16[2,64,16,64]{3,2,1,0:T(8,128)(2,1)S(1)}, u32[]{:S(2)}) copy-start(bf16[2,64,16,64]{3,2,1,0:T(8,128)(2,1)S(1)} %reshape.190) | copy-start | bytes 786436
  167.4 241.0 %all-gather.25.cloned.1.call-start = ((), (), s32[]{:S(2)}) async-start(), calls=%async_computation.10 | async-start | bytes 2359296 | tf_op jit(solution)/shard_map/all_gather | solution.py:64
  168.0 366.7 %all-gather.27.cloned.1.call-start = ((), (), s32[]{:S(2)}) async-start(), calls=%async_computation.11 | async-start | bytes 9437184 | tf_op jit(solution)/shard_map/all_gather | solution.py:65
  168.8 491.3 %all-gather.29.cloned.1.call-start = ((), (), s32[]{:S(2)}) async-start(), calls=%async_computation.12 | async-start | bytes 9437184 | tf_op jit(solution)/shard_map/all_gather | solution.py:66
  169.5 607.8 %all-gather.33.cloned.1.call-start = ((), (), s32[]{:S(2)}) async-start(), calls=%async_computation.14 | async-start | bytes 4718592 | tf_op jit(solution)/shard_map/all_gather | solution.py:201
  217.1 598.2 %all-gather.35.cloned.1.call-start = ((), (), s32[]{:S(2)}) async-start(), calls=%async_computation.15 | async-start | bytes 4718592 | tf_op jit(solution)/shard_map/all_gather | solution.py:202
  369.0 165.8 %copy-start.12 = (bf16[128,1024]{1,0:T(8,128)(2,1)}, bf16[128,1024]{1,0:T(8,128)(2,1)S(1)}, u32[]{:S(2)}) copy-start(bf16[128,1024]{1,0:T(8,128)(2,1)S(1)} %reshape.193) | copy-start | bytes 786436
  410.8 128.7 %copy-start.32 = (f32[128]{0:T(128)}, f32[128]{0:T(128)S(1)}, u32[]{:S(2)}) copy-start(f32[128]{0:T(128)S(1)} %multiply_reduce_fusion.5) | copy-start | bytes 1540
  677.9 228.7 %reduce-scatter.11.cloned.1.call-start = ((), (), s32[]{:S(2)}) async-start(), calls=%async_computation.18 | async-start | bytes 4718592 | tf_op jit(solution)/shard_map/reduce_scatter | solution.py:246
  681.8 316.4 %reduce-scatter.17.cloned.1.call-start = ((), (), s32[]{:S(2)}) async-start(), calls=%async_computation.21 | async-start | bytes 4718592 | tf_op jit(solution)/shard_map/reduce_scatter | solution.py:249
  690.4 399.7 %reduce-scatter.7.cloned.1.call-start = ((), (), s32[]{:S(2)}) async-start(), calls=%async_computation.16 | async-start | bytes 4718592 | tf_op jit(solution)/shard_map/reduce_scatter | solution.py:243
  783.1 37.6 %copy-start.22 = (f32[2,16,512]{2,1,0:T(8,128)S(1)}, f32[2,16,512]{2,1,0:T(8,128)}, u32[]{:S(2)}) copy-start(f32[2,16,512]{2,1,0:T(8,128)} %copy.97) | copy-start | bytes 196612
  854.5 446.7 %reduce-scatter.9.cloned.1.call-start = ((), (), s32[]{:S(2)}) async-start(), calls=%async_computation.17 | async-start | bytes 14155776 | tf_op jit(solution)/shard_map/reduce_scatter | solution.py:245
  862.1 724.6 %reduce-scatter.13.cloned.1.call-start = ((), (), s32[]{:S(2)}) async-start(), calls=%async_computation.19 | async-start | bytes 18874368 | tf_op jit(solution)/shard_map/reduce_scatter | solution.py:247
  871.9 999.7 %reduce-scatter.15.cloned.1.call-start = ((), (), s32[]{:S(2)}) async-start(), calls=%async_computation.20 | async-start | bytes 18874368 | tf_op jit(solution)/shard_map/reduce_scatter | solution.py:248
  881.1 1070.8 %all-reduce.10.cloned.1.call-start = ((), (), s32[]{:S(2)}) async-start(), calls=%async_computation.22 | async-start | bytes 7340032 | tf_op jit(solution)/shard_map/psum | solution.py:257
  1589.4 285.1 %copy-start.29 = (bf16[128]{0:T(256)(128)(2,1)S(1)}, bf16[128]{0:T(256)(128)(2,1)}, u32[]{:S(2)}) copy-start(bf16[128]{0:T(256)(128)(2,1)} %param.25) | copy-start | bytes 772
  1589.4 300.0 %copy-start.34 = (u32[32]{0:T(128)S(1)}, u32[32]{0:T(128)}, u32[]{:S(2)}) copy-start(u32[32]{0:T(128)} %constant.45) | copy-start | bytes 388
  1589.4 301.3 %copy-start.15 = (bf16[2,64,1024]{2,1,0:T(8,128)(2,1)S(1)}, bf16[2,64,1024]{2,1,0:T(8,128)(2,1)}, u32[]{:S(2)}) copy-start(bf16[2,64,1024]{2,1,0:T(8,128)(2,1)} %param.18) | copy-start | bytes 786436
  1589.4 301.4 %copy-start.20 = (bf16[128,1024]{1,0:T(8,128)(2,1)S(1)}, bf16[128,1024]{1,0:T(8,128)(2,1)}, u32[]{:S(2)}) copy-start(bf16[128,1024]{1,0:T(8,128)(2,1)} %copy-done.19) | copy-start | bytes 786436
  1589.4 304.1 %copy-start.23 = (f32[1024]{0:T(1024)S(1)}, f32[1024]{0:T(1024)}, u32[]{:S(2)}) copy-start(f32[1024]{0:T(1024)} %get-tuple-element.69) | copy-start | bytes 12292
  1589.4 349.4 %copy-start.2 = (bf16[1024,1024]{1,0:T(8,128)(2,1)S(1)}, bf16[1024,1024]{1,0:T(8,128)(2,1)}, u32[]{:S(2)}) copy-start(bf16[1024,1024]{1,0:T(8,128)(2,1)} %all-gather.17.cloned.1.call-done) | copy-start | bytes 6291460
  1589.4 349.4 %copy-start.11 = (bf16[128,1024]{1,0:T(8,128)(2,1)S(1)}, bf16[128,1024]{1,0:T(8,128)(2,1)}, u32[]{:S(2)}) copy-start(bf16[128,1024]{1,0:T(8,128)(2,1)} %copy-done.10) | copy-start | bytes 786436
  (20 other events, 137.7 us)
Sparse Core Ops, SparseCore 0:
  10.1 50.2 all-gather.16
  62.6 98.0 all-gather.18
  162.9 47.1 all-gather.30
  212.7 71.7 all-gather.22
  287.1 71.6 all-gather.20
  360.8 47.6 all-gather.24
  410.6 124.1 all-gather.26
  536.9 123.1 all-gather.28
  662.2 75.4 all-gather.32
  739.6 75.5 all-gather.34
  818.9 87.7 reduce-scatter.10
  910.6 87.6 reduce-scatter.16
  1001.9 88.2 reduce-scatter.6
  1094.0 207.1 reduce-scatter.8
  1305.3 281.3 reduce-scatter.12
  1590.3 281.3 reduce-scatter.14
  1875.1 76.7 all-reduce.9
where the time goes:
time: 1980 us; the launch traced here: 1970 us
  waiting for transfers between devices  1560 us (79%)
  blocking collectives  189 us (10%)
  matrix products  121 us (6%)
  local copies, waits for them, and re-layouts  47.6 us (2%)
  other arithmetic  32.5 us (2%)
    reduce_scatter x1, waiting for transfers between devices, local(): lax.psum_scatter(grad_w_up, 'blk', scatter_dimension=0, tiled=True)  283 us
    reduce_scatter x1, waiting for transfers between devices, local(): lax.psum_scatter(grad_w_down, 'blk', scatter_dimension=0, tiled=True)  282 us
    reduce_scatter x1, waiting for transfers between devices, local(): lax.psum_scatter(grad_w_qkv, 'blk', scatter_dimension=0, tiled=True)  209 us
    all_gather x1, waiting for transfers between devices, local(): lax.all_gather(up_weight, 'blk', axis=0, tiled=True)  124 us
    all_gather x1, waiting for transfers between devices, local(): lax.all_gather(down_weight, 'blk', axis=0, tiled=True)  121 us
    all_gather x1, waiting for transfers between devices, local(): lax.all_gather(qkv_weight, 'blk', axis=0, tiled=True)  98 us
    reduce_scatter x1, waiting for transfers between devices, local(): lax.psum_scatter(inner(express, grad_h0), 'blk', scatter_dimension=0, til...  90.1 us
    reduce_scatter x1, waiting for transfers between devices, local(): lax.psum_scatter(grad_dec, 'blk', scatter_dimension=0, tiled=True)  89.8 us
  transfers between devices with their start and end apart: 17, of which 15 were waited for; matrix products, arithmetic and copies ran while one was open for 9% of the time, Pallas kernels for 0%

commit v1 on v0

--- a/solution.py
+++ b/solution.py
@@ -1,8 +1,12 @@
+import functools
 import math
 
 import jax
 import jax.numpy as jnp
 from jax import lax
+from jax.experimental import pallas as pl
+from jax.experimental.pallas import tpu as pltpu
+from jax.sharding import Mesh
 from jax.sharding import PartitionSpec as P
 
 HEADS = 16
@@ -41,7 +45,7 @@
     )
 
 
-def local(
+def spread_plan(
     counts,
     coords,
     segment_ids,
@@ -134,20 +138,6 @@
     logits = (
         jnp.dot(hidden2_low, w_dec, preferred_element_type=jnp.float32) + b_dec.astype(jnp.float32)
     ).astype(jnp.bfloat16)
-    regathered = (
-        lax.all_gather(enc_weight, "blk", axis=0, tiled=True),
-        lax.all_gather(qkv_weight, "blk", axis=0, tiled=True),
-        lax.all_gather(out_weight, "blk", axis=0, tiled=True),
-        lax.all_gather(up_weight, "blk", axis=0, tiled=True),
-        lax.all_gather(down_weight, "blk", axis=0, tiled=True),
-        lax.all_gather(dec_weight, "blk", axis=0, tiled=True),
-        lax.all_gather(dec_bias, "blk", axis=0, tiled=True),
-        lax.all_gather(norm1_gain, "blk", axis=0, tiled=True),
-        lax.all_gather(norm1_shift, "blk", axis=0, tiled=True),
-        lax.all_gather(norm2_gain, "blk", axis=0, tiled=True),
-        lax.all_gather(norm2_shift, "blk", axis=0, tiled=True),
-    )
-    w_enc, w_qkv, w_out, w_up, w_down, w_dec = regathered[:6]
     cotangent = logit_grad.reshape(row_count, gene_count)
     grad_dec = inner(hidden2_low, cotangent)
     grad_bias = jnp.sum(cotangent.astype(jnp.float32), axis=0)
@@ -174,13 +164,8 @@
         lax.all_gather(logsum, "blk", axis=1, tiled=True),
         lax.all_gather(delta, "blk", axis=1, tiled=True),
     )
-    piece = (
-        lax.all_gather(key_rows, "blk", axis=1, tiled=True),
-        lax.all_gather(values, "blk", axis=1, tiled=True),
-    )
     seg_part = seg_all
-    incoming = (piece[0], piece[1], seg_part)
-    key_part, value_part, query_seg_part = incoming
+    query_seg_part = seg_part
     query_part = queries
     gradout_part = grad_context
     logsum_part = logsum
@@ -283,37 +268,518 @@
     )
 
 
+AXES = ("y", "core", "z", "x")
+SPLIT = 64
+
+
+class Place:
+    def __init__(self, sizes):
+        self.sizes = sizes
+        self.y, self.core, self.z, self.x = (lax.axis_index(name) for name in AXES)
+
+    def send(self, value, move):
+        ny, nc, nz, nx = self.sizes
+
+        def flat(place):
+            y, c, z, x = place
+            return ((y * nc + c) * nz + z) * nx + x
+
+        everywhere = [
+            (y, c, z, x) for y in range(ny) for c in range(nc) for z in range(nz) for x in range(nx)
+        ]
+        return lax.ppermute(value, AXES, [(flat(p), flat(move(*p))) for p in everywhere])
+
+    def swap_core(self, value):
+        return self.send(value, lambda y, c, z, x: (y, 1 - c, z, x))
+
+    def swap_x(self, value):
+        return self.send(value, lambda y, c, z, x: (y, c, z, 1 - x))
+
+    def swap_y(self, value):
+        return self.send(value, lambda y, c, z, x: (1 - y, c, z, x))
+
+    def shift_z(self, value, step):
+        nz = self.sizes[2]
+        return self.send(value, lambda y, c, z, x: (y, c, (z + step) % nz, x))
+
+    def to_group(self, value):
+        low = self.z % 2 == 0
+        first = self.send(
+            jnp.where(low, value[0], value[1]), lambda y, c, z, x: (y, z // 2, 2 * c + z % 2, x)
+        )
+        second = self.send(
+            jnp.where(low, value[1], value[0]),
+            lambda y, c, z, x: (y, z // 2, 2 * c + 1 - z % 2, x),
+        )
+        return first, second
+
+    def from_group(self, value):
+        first, second = self.to_group_raw(value)
+        low = self.z % 2 == 0
+        return jnp.stack([jnp.where(low, first, second), jnp.where(low, second, first)])
+
+    def to_group_raw(self, value):
+        first = self.send(value[0], lambda y, c, z, x: (y, z // 2, 2 * c + z % 2, x))
+        second = self.send(value[1], lambda y, c, z, x: (y, z // 2, 2 * c + 1 - z % 2, x))
+        return first, second
+
+    def whole_group(self, value):
+        half = jnp.concatenate([value, self.swap_x(value)], axis=0)
+        return jnp.concatenate([half, self.swap_core(half)], axis=0)
+
+    def sum_group(self, part):
+        half = part.shape[0] // 2
+        low = part.astype(jnp.bfloat16)
+        mine = (part[:half] + self.swap_core(low[half:]).astype(jnp.float32)).astype(jnp.bfloat16)
+        other = self.swap_x(mine)
+        quarter = half // 2
+        other = jnp.concatenate([other[quarter:], other[:quarter]], axis=0)
+        return mine.astype(jnp.float32) + other.astype(jnp.float32)
+
+
+def in_order(index, mine, other):
+    return jnp.where(index == 0, jnp.stack([mine, other]), jnp.stack([other, mine]))
+
+
+def lay_out(pieces, out_shape, copies):
+    count = len(copies(0, 0, 0, 0))
+
+    def kernel(*refs):
+        sources, target, sems = refs[:-2], refs[-2], refs[-1]
+        place = tuple(lax.axis_index(name) for name in AXES)
+        started = []
+        for number, (piece, rows, columns, row, column) in enumerate(copies(*place)):
+            size = rows[1] - rows[0]
+            width = columns[1] - columns[0]
+            copy = pltpu.make_async_copy(
+                sources[piece].at[rows[0] : rows[1], columns[0] : columns[1]],
+                target.at[pl.ds(pl.multiple_of(row, 16), size), column : column + width],
+                sems.at[number],
+            )
+            copy.start()
+            started.append(copy)
+        for copy in started:
+            copy.wait()
+
+    size = math.prod(out_shape) * 2
+    return pl.pallas_call(
+        kernel,
+        out_shape=jax.ShapeDtypeStruct(out_shape, jnp.bfloat16),
+        in_specs=[pl.BlockSpec(memory_space=pl.ANY)] * len(pieces),
+        out_specs=pl.BlockSpec(memory_space=pl.ANY),
+        scratch_shapes=[pltpu.SemaphoreType.DMA((count,))],
+        cost_estimate=pl.CostEstimate(flops=0, bytes_accessed=2 * size, transcendentals=0),
+    )(*pieces)
+
+
+def dot(left, right):
+    return jnp.dot(left, right, preferred_element_type=jnp.float32)
+
+
+def soft(queries, keys, allowed, scaling):
+    scores = times_t(queries, keys) * scaling
+    scores = jnp.where(allowed, scores, NEGATIVE)
+    expo = jnp.exp(scores - jnp.max(scores, axis=-1, keepdims=True))
+    return expo / jnp.sum(expo, axis=-1, keepdims=True)
+
+
+def attend_kernel(heads, size, qkv_ref, column_ref, row_ref, out_ref):
+    width = heads * size
+    allowed = column_ref[...] == row_ref[...]
+    for head in range(heads):
+        at = head * size
+        queries = qkv_ref[:, at : at + size]
+        keys = qkv_ref[:, width + at : width + at + size]
+        values = qkv_ref[:, 2 * width + at : 2 * width + at + size]
+        probs = soft(queries, keys, allowed, size**-0.5)
+        out_ref[:, at : at + size] = dot(probs.astype(jnp.bfloat16), values).astype(jnp.bfloat16)
+
+
+def attend_back_kernel(heads, size, qkv_ref, grad_ref, column_ref, row_ref, out_ref):
+    width = heads * size
+    allowed = column_ref[...] == row_ref[...]
+    for head in range(heads):
+        at = head * size
+        queries = qkv_ref[:, at : at + size]
+        keys = qkv_ref[:, width + at : width + at + size]
+        values = qkv_ref[:, 2 * width + at : 2 * width + at + size]
+        grad = grad_ref[:, at : at + size]
+        probs = soft(queries, keys, allowed, size**-0.5)
+        dprob = times_t(grad, values)
+        weighted = probs * dprob
+        delta = jnp.sum(weighted, axis=-1, keepdims=True)
+        dscore = (weighted - probs * delta).astype(jnp.bfloat16)
+        grad_queries = dot(dscore, keys) * size**-0.5
+        grad_keys = inner(dscore, queries) * size**-0.5
+        grad_values = inner(probs.astype(jnp.bfloat16), grad)
+        out_ref[:, at : at + size] = grad_queries.astype(jnp.bfloat16)
+        out_ref[:, width + at : width + at + size] = grad_keys.astype(jnp.bfloat16)
+        out_ref[:, 2 * width + at : 2 * width + at + size] = grad_values.astype(jnp.bfloat16)
+
+
+def in_vmem(kernel, out_shape, flops, transcendentals, *operands):
+    whole = pl.BlockSpec(memory_space=pltpu.VMEM)
+    return pl.pallas_call(
+        kernel,
+        out_shape=jax.ShapeDtypeStruct(out_shape, jnp.bfloat16),
+        in_specs=[whole] * len(operands),
+        out_specs=whole,
+        compiler_params=pltpu.CompilerParams(vmem_limit_bytes=40 * 1024 * 1024),
+        cost_estimate=pl.CostEstimate(
+            flops=flops, bytes_accessed=4 * math.prod(out_shape), transcendentals=transcendentals
+        ),
+    )(*operands)
+
+
+def sinusoids_of_whole(coords, width):
+    quarter = width // 4
+    frequency = jnp.exp(jnp.arange(quarter, dtype=jnp.float32) * (-math.log(10000.0) / quarter))
+    number = jnp.arange(32, dtype=jnp.float32)[:, None]
+    far, near = 32.0 * number * frequency, number * frequency
+    far = jnp.concatenate([jnp.sin(far), jnp.cos(far)], axis=1)
+    near = jnp.concatenate([jnp.sin(near), jnp.cos(near)], axis=1)
+    parts = []
+    for coord in coords:
+        whole = coord.astype(jnp.int32)
+        pick_far = (whole // 32 == jnp.arange(32)[None, :]).astype(jnp.float32)
+        pick_near = (whole % 32 == jnp.arange(32)[None, :]).astype(jnp.float32)
+        at_far = jnp.dot(pick_far, far, precision=lax.Precision.HIGHEST)
+        at_near = jnp.dot(pick_near, near, precision=lax.Precision.HIGHEST)
+        sin_far, cos_far = at_far[:, :quarter], at_far[:, quarter:]
+        sin_near, cos_near = at_near[:, :quarter], at_near[:, quarter:]
+        parts.append(sin_far * cos_near + cos_far * sin_near)
+        parts.append(cos_far * cos_near - sin_far * sin_near)
+    return jnp.concatenate(parts, axis=1)
+
+
+def normalise(inputs):
+    centre = inputs - jnp.mean(inputs, axis=-1, keepdims=True)
+    factor = lax.rsqrt(jnp.mean(centre * centre, axis=-1, keepdims=True) + EPSILON)
+    return centre * factor, factor
+
+
+def normalise_back(grad, normal, factor, gain):
+    scaled = grad * gain
+    inside = (
+        scaled
+        - jnp.mean(scaled, axis=-1, keepdims=True)
+        - normal * jnp.mean(scaled * normal, axis=-1, keepdims=True)
+    )
+    return factor * inside, jnp.stack([jnp.sum(grad * normal, axis=0), jnp.sum(grad, axis=0)])
+
+
+def wide(rows):
+    count, width = rows.shape
+    return rows.reshape(count, 4, width // 4).transpose(1, 0, 2).reshape(4 * count, width // 4)
+
+
+def grouped_plan(
+    sizes,
+    counts,
+    coords,
+    segment_ids,
+    logit_grad,
+    enc_weight,
+    qkv_weight,
+    out_weight,
+    up_weight,
+    down_weight,
+    dec_weight,
+    dec_bias,
+    norm1_gain,
+    norm1_shift,
+    norm2_gain,
+    norm2_shift,
+):
+    place = Place(sizes)
+    nz = sizes[2]
+    seqs, cells, genes = counts.shape
+    width = enc_weight.shape[1]
+    block = enc_weight.shape[0]
+    head = width // HEADS
+    heads = HEADS // 4
+    slice_width = width // 4
+    own_rows = seqs * cells
+    rows = 4 * own_rows
+    ff = up_weight.shape[1]
+    ff_slice = ff // 4
+    bf16, f32 = jnp.bfloat16, jnp.float32
+
+    def pick(value, axis, index):
+        return lax.dynamic_index_in_dim(value, index, axis, keepdims=False)
+
+    express = jnp.log1p(counts.astype(f32)).astype(bf16)
+    whole = jnp.stack([coords[0], coords[1], segment_ids], axis=-1)
+    beside = jnp.concatenate([whole // SPLIT, whole % SPLIT], axis=-1).astype(bf16)
+    beside = jnp.pad(beside, ((0, 0), (0, 0), (0, 122)))
+    cell_rows = jnp.concatenate([express, beside], axis=-1)
+    first, second = place.to_group(cell_rows)
+    cell_rows = place.whole_group(jnp.concatenate([first, second], axis=0))
+    express = cell_rows[:, :genes]
+    beside = cell_rows[:, genes:].astype(f32)
+    beside = beside[:, :3] * SPLIT + beside[:, 3:6]
+    segment = beside[:, 2:3]
+    segment_row = segment.reshape(1, rows)
+    embed = sinusoids_of_whole((beside[:, 0:1], beside[:, 1:2]), width)
+
+    vectors = jnp.stack([dec_bias, norm1_gain, norm1_shift, norm2_gain, norm2_shift]).reshape(1, 5 * block)
+    vectors = jnp.pad(vectors, ((0, 15), (0, width - 5 * block)))
+    half = block // 2
+    tall = half + 16
+    enc_own = jnp.concatenate([pick(enc_weight.reshape(2, half, width), 0, place.core), vectors], axis=0)
+    enc_z = jnp.concatenate([enc_own] + [place.shift_z(enc_own, k) for k in range(1, nz)], axis=0)
+    enc_zx = jnp.concatenate([enc_z, place.swap_x(enc_z)], axis=0)
+    enc_far = place.swap_core(enc_zx)
+
+    def enc_copies(y, core, z, x):
+        return [
+            (dc, ((dx * nz + k) * tall, (dx * nz + k) * tall + half), (0, width),
+             (2 * ((z - k) % nz) + (x ^ dx)) * block + (core ^ dc) * half, 0)
+            for dc in range(2) for dx in range(2) for k in range(nz)
+        ]
+
+    def vector_copies(y, core, z, x):
+        return [
+            (0, ((dx * nz + k) * tall + half, (dx * nz + k + 1) * tall), (0, width),
+             (2 * ((z - k) % nz) + (x ^ dx)) * 16, 0)
+            for dx in range(2) for k in range(nz)
+        ]
+
+    w_enc = lay_out((enc_zx, enc_far), (genes, width), enc_copies)
+    vectors = lay_out((enc_zx,), (2 * nz * 16, width), vector_copies)
+    vectors = vectors.reshape(2 * nz, 16, width)[:, 0, : 5 * block].reshape(2 * nz, 5, block)
+    vectors = vectors.transpose(1, 0, 2).reshape(5, width).astype(f32)
+    b_dec, gain_one, shift_one, gain_two, shift_two = (vectors[i : i + 1] for i in range(5))
+
+    qkv_parts = qkv_weight.reshape(block, 3, nz, 2, 2, head)
+    qkv_parts = pick(qkv_parts, 4, place.core)
+    qkv_mine = pick(qkv_parts, 3, place.x).reshape(block, 3 * slice_width)
+    qkv_theirs = pick(qkv_parts, 3, 1 - place.x).reshape(block, 3 * slice_width)
+    qkv_pair = jnp.stack([qkv_mine, place.swap_x(qkv_theirs)]).reshape(2, 2, half, 3 * slice_width)
+    out_parts = pick(out_weight.reshape(2, 2, half // 2, width), 0, place.core)
+    dec_parts = pick(dec_weight.reshape(2, 2, half // 2, genes), 0, place.core)
+    quarter = half // 2
+
+    def piece(of):
+        top = jnp.concatenate(
+            [pick(qkv_pair, 1, of).reshape(block, 3 * slice_width), wide(pick(out_parts, 0, of))],
+            axis=1,
+        )
+        return jnp.concatenate([top, pick(dec_parts, 0, of)], axis=0)
+
+    near = piece(place.y)
+    near = [near] + [place.shift_z(near, k) for k in range(1, nz)]
+    far = [piece(1 - place.y)] + [place.swap_y(part) for part in near[1:]]
+
+    def qkv_copies(y, core, z, x):
+        return [
+            (dy * nz + k, (dx * half, (dx + 1) * half), (0, 3 * slice_width),
+             (2 * ((z - k) % nz) + (x ^ dx)) * block + (y ^ dy) * half, 0)
+            for k in range(nz) for dy in range(2) for dx in range(2)
+        ]
+
+    def out_copies(y, core, z, x):
+        return [
+            (dy * nz + k, (j * quarter, (j + 1) * quarter), (3 * slice_width, width),
+             ((z - k) % nz) * half + (y ^ dy) * quarter, j * slice_width)
+            for k in range(nz) for dy in range(2) for j in range(4)
+        ]
+
+    def dec_copies(y, core, z, x):
+        return [
+            (dy * nz + k, (block, block + quarter), (0, width),
+             ((z - k) % nz) * half + (y ^ dy) * quarter, 0)
+            for k in range(nz) for dy in range(2)
+        ]
+
+    w_qkv = lay_out(near + far, (width, 3 * slice_width), qkv_copies)
+    w_out = lay_out(near + far, (slice_width, width), out_copies)
+    dec_z = lay_out(near + far, (slice_width, genes), dec_copies)
+    dec_zx = jnp.concatenate([dec_z, place.swap_x(dec_z)], axis=0)
+    dec_far = place.swap_core(dec_zx)
+
+    def dec_all_copies(y, core, z, x):
+        return [
+            (dc, ((dx * nz + k) * half, (dx * nz + k + 1) * half), (0, genes),
+             (2 * k + (x ^ dx)) * block + (core ^ dc) * half, 0)
+            for dc in range(2) for dx in range(2) for k in range(nz)
+        ]
+
+    w_dec = lay_out((dec_zx, dec_far), (width, genes), dec_all_copies)
+
+    up_parts = up_weight.reshape(block, nz, 2, 2, 2, ff // (8 * nz))
+    up_parts = pick(pick(up_parts, 4, place.y), 3, place.core)
+    up_mine = pick(up_parts, 2, place.x).reshape(block, ff_slice // 2)
+    up_theirs = pick(up_parts, 2, 1 - place.x).reshape(block, ff_slice // 2)
+    up_own = in_order(place.x, up_mine, place.swap_x(up_theirs)).reshape(2 * block, ff_slice // 2)
+    down_parts = down_weight.reshape(2, 2, down_weight.shape[0] // 4, width)
+    down_own = pick(pick(down_parts, 0, place.core), 0, place.y)
+    w_up = lax.all_gather(up_own, ("y", "z"), axis=0).reshape(2, width, ff_slice // 2)
+    w_down = lax.all_gather(down_own, ("y", "z"), axis=0).reshape(2, ff_slice // 2, width)
+
+    first, second = place.to_group(logit_grad)
+    cotangent = place.whole_group(jnp.concatenate([first, second], axis=0))
+    grad_bias = jnp.sum(cotangent.astype(f32), axis=0, keepdims=True)
+    grad_h2 = times_t(cotangent, w_dec)
+    grad_down = grad_h2.astype(bf16)
+
+    hidden0 = dot(express, w_enc) + embed
+    normal1, factor1 = normalise(hidden0)
+    normed1 = (normal1 * gain_one + shift_one).astype(bf16)
+    qkv = dot(normed1, w_qkv).astype(bf16)
+    pairs = heads * rows * rows
+    context = in_vmem(
+        functools.partial(attend_kernel, heads, head),
+        (rows, slice_width), 4 * pairs * head, pairs, qkv, segment, segment_row,
+    )
+    half_rows = rows // 2
+    hidden1 = hidden0[:half_rows] + place.sum_group(dot(context, w_out))
+    normal2, factor2 = normalise(hidden1)
+    normed2 = (normal2 * gain_two + shift_two).astype(bf16)
+    normed2 = jnp.concatenate([normed2, place.swap_core(normed2)], axis=0)
+    up_value = [dot(normed2, w_up[i]) for i in range(2)]
+    active = [jax.nn.gelu(value).astype(bf16) for value in up_value]
+    hidden2 = hidden1 + place.sum_group(dot(active[0], w_down[0]) + dot(active[1], w_down[1]))
+    hidden2 = hidden2.astype(bf16)
+    logits = (dot(hidden2[:own_rows], w_dec) + b_dec).astype(bf16)
+    logits = place.from_group(logits.reshape(seqs, cells, genes))
+
+    hidden2_parts = pick(hidden2.reshape(half_rows, nz, 2, 2, half), 2, place.x)
+    hidden2_slice = jnp.concatenate(
+        [
+            pick(hidden2_parts, 2, place.core).reshape(half_rows, slice_width),
+            place.swap_core(pick(hidden2_parts, 2, 1 - place.core).reshape(half_rows, slice_width)),
+        ],
+        axis=0,
+    )
+    grad_w_dec = inner(hidden2_slice, cotangent).astype(bf16)
+    grad_w_down = [inner(part, grad_down).astype(bf16) for part in active]
+    grad_active = [times_t(grad_down, w_down[i]) for i in range(2)]
+    grad_up = [
+        jax.vjp(jax.nn.gelu, up_value[i])[1](grad_active[i])[0].astype(bf16) for i in range(2)
+    ]
+    grad_w_up = jnp.concatenate([inner(normed2, part) for part in grad_up], axis=1).astype(bf16)
+    grad_normed2 = place.sum_group(times_t(grad_up[0], w_up[0]) + times_t(grad_up[1], w_up[1]))
+    part_two, sums_two = normalise_back(grad_normed2, normal2, factor2, gain_two)
+    grad_h1 = grad_h2[:half_rows] + part_two
+    grad_attn = grad_h1.astype(bf16)
+
+    def beside_core(value, sums):
+        both = jnp.concatenate([value, jnp.pad(sums.astype(bf16), ((0, 14), (0, 0)))], axis=0)
+        other = place.swap_core(both)
+        return (
+            jnp.concatenate([value, other[:half_rows]], axis=0),
+            sums + other[half_rows : half_rows + 2].astype(f32),
+        )
+
+    grad_attn, sums_two = beside_core(grad_attn, sums_two)
+    grad_w_out = inner(context, grad_attn).astype(bf16)
+    grad_context = times_t(grad_attn, w_out).astype(bf16)
+    grad_qkv = in_vmem(
+        functools.partial(attend_back_kernel, heads, head),
+        (rows, 3 * slice_width), 10 * pairs * head, pairs, qkv, grad_context, segment, segment_row,
+    )
+    grad_w_qkv = inner(normed1, grad_qkv).astype(bf16)
+    grad_normed1 = place.sum_group(times_t(grad_qkv, w_qkv))
+    part_one, sums_one = normalise_back(
+        grad_normed1, normal1[:half_rows], factor1[:half_rows], gain_one
+    )
+    grad_h0 = (grad_h1 + part_one).astype(bf16)
+    input_grad = times_t(grad_h0[:own_rows], w_enc).astype(bf16)
+    input_grad = place.from_group(input_grad.reshape(seqs, cells, genes))
+    grad_h0, sums_one = beside_core(grad_h0, sums_one)
+    express_slice = pick(pick(express.reshape(rows, nz, 2, 2, half), 2, place.x), 2, place.core)
+    grad_w_enc = inner(express_slice.reshape(rows, slice_width), grad_h0)
+
+    def over_z(value):
+        return lax.psum_scatter(value, "z", scatter_dimension=0, tiled=False)
+
+    def over_y(value):
+        return value.astype(f32) + place.swap_y(value).astype(f32)
+
+    ff_piece = ff_slice // (2 * nz)
+    early = jnp.concatenate(
+        [part.reshape(nz, ff_piece, width) for part in grad_w_down]
+        + [grad_w_dec.reshape(nz, half, genes)],
+        axis=1,
+    )
+    early = over_y(over_z(early))
+    early = in_order(place.core, early, place.swap_core(early.astype(bf16)).astype(f32))
+    out_down = early[:, : 2 * ff_piece].reshape(4 * ff_piece, width)
+    out_dec = early[:, 2 * ff_piece :].reshape(block, genes)
+
+    def whole_columns(value):
+        low = value.astype(bf16)
+        mine = pick(value, 0, place.x)
+        theirs = place.swap_x(pick(low, 0, 1 - place.x)).astype(f32)
+        both = in_order(place.x, mine, theirs)
+        other = place.swap_core(both.astype(bf16)).astype(f32)
+        return in_order(place.core, both, other)
+
+    middle = over_y(over_z(grad_w_up.reshape(nz, 2 * block, ff_slice)))
+    out_up = whole_columns(middle.reshape(2, block, ff_slice))
+    out_up = out_up.reshape(2, 2, block, 2, nz, ff_piece).transpose(2, 4, 1, 0, 3, 5)
+    out_up = out_up.reshape(block, ff)
+
+    late = jnp.concatenate(
+        [
+            grad_w_qkv.reshape(nz, 2 * block, 3 * slice_width),
+            grad_w_out.reshape(nz, half, 4, slice_width)
+            .transpose(0, 2, 1, 3)
+            .reshape(nz, 2 * block, slice_width),
+        ],
+        axis=2,
+    )
+    late = over_y(over_z(late))
+    out_qkv = whole_columns(late[:, : 3 * slice_width].reshape(2, block, 3 * slice_width))
+    out_qkv = out_qkv.reshape(2, 2, block, 3, nz, head).transpose(2, 3, 4, 1, 0, 5)
+    out_qkv = out_qkv.reshape(block, 3 * width)
+    out_out = late[:, 3 * slice_width :].reshape(4, half, slice_width).transpose(1, 0, 2)
+    out_out = out_out.reshape(half, width)
+    out_out = in_order(place.core, out_out, place.swap_core(out_out.astype(bf16)).astype(f32))
+    out_out = out_out.reshape(block, width)
+
+    sums = jnp.concatenate([grad_bias, sums_one, sums_two], axis=0).reshape(5, nz, 2, block)
+    sums = pick(sums, 2, place.x).transpose(1, 0, 2).reshape(nz, 1, 5 * block)
+    sums = jnp.pad(sums, ((0, 0), (0, 15), (0, width - 5 * block)))
+    last = jnp.concatenate([grad_w_enc.reshape(nz, half, width), sums], axis=1)
+    last_low = last.astype(bf16)
+    total = pick(last, 0, place.z)
+    for k in range(1, nz):
+        total += place.shift_z(pick(last_low, 0, (place.z + k) % nz), k).astype(f32)
+    total = total + place.swap_y(total.astype(bf16)).astype(f32)
+    out_enc = total[:half]
+    out_enc = in_order(place.core, out_enc, place.swap_core(out_enc.astype(bf16)).astype(f32))
+    out_enc = out_enc.reshape(block, width)
+    sums = total[half, : 5 * block].reshape(5, block)
+    return (
+        logits, input_grad, out_enc, out_qkv, out_out, out_up, out_down, out_dec,
+        sums[0], sums[1], sums[2], sums[3], sums[4],
+    )
+
+
+IN_SPECS = (
+    ("dp", "blk", None), (None, "dp", "blk"), ("dp", "blk"), ("dp", "blk", None),
+    *[("blk", None)] * 6, *[("blk",)] * 5,
+)
+OUT_SPECS = (("dp", "blk", None), ("dp", "blk", None), *[("blk", None)] * 6, *[("blk",)] * 5)
+
+
 def solution(mesh):
-    in_specs = (
-        P("dp", "blk", None),
-        P(None, "dp", "blk"),
-        P("dp", "blk"),
-        P("dp", "blk", None),
-        P("blk", None),
-        P("blk", None),
-        P("blk", None),
-        P("blk", None),
-        P("blk", None),
-        P("blk", None),
-        P("blk"),
-        P("blk"),
-        P("blk"),
-        P("blk"),
-        P("blk"),
-    )
-    out_specs = (
-        P("dp", "blk", None),
-        P("dp", "blk", None),
-        P("blk", None),
-        P("blk", None),
-        P("blk", None),
-        P("blk", None),
-        P("blk", None),
-        P("blk", None),
-        P("blk"),
-        P("blk"),
-        P("blk"),
-        P("blk"),
-        P("blk"),
-    )
-    return jax.shard_map(local, mesh=mesh, in_specs=in_specs, out_specs=out_specs, check_vma=False)
+    groups, blocks = mesh.shape["dp"], mesh.shape["blk"]
+
+    def run(*args):
+        seqs = args[0].shape[0] // groups
+        if groups == 4 and blocks == 4 * seqs and seqs == 2 and HEADS == 4 * (blocks // 2):
+            sizes = (groups // 2, 2, blocks // 2, 2)
+            fine = Mesh(mesh.devices.reshape(sizes), AXES)
+            names = {"dp": ("y", "core"), "blk": ("z", "x"), None: None}
+            plan = functools.partial(grouped_plan, sizes)
+        else:
+            fine, names, plan = mesh, {"dp": "dp", "blk": "blk", None: None}, spread_plan
+        specs = lambda entries: tuple(P(*[names[axis] for axis in entry]) for entry in entries)
+        return jax.shard_map(
+            plan, mesh=fine, in_specs=specs(IN_SPECS), out_specs=specs(OUT_SPECS), check_vma=False
+        )(*args)
+
+    return run

time: 1980 us -> 598 us (0.30)
  waiting for transfers between devices: 1560 us -> 115 us
  Pallas kernels: 0 us -> 231 us
  blocking collectives: 189 us -> 0 us
  starting transfers between devices: 1.47 us -> 79 us
  matrix products: 121 us -> 45.9 us
    reduce_scatter x6 -> x3, waiting for transfers between devices: 980 us -> 6.31 us  [over_z(): return lax.psum_scatter(value, 'z', scatter_dimension=0, tiled=False)]
    all_gather x10 -> x2, waiting for transfers between devices: 566 us -> 0.01 us  [the longest x1 0.01 us: grouped_plan(): lax.all_gather(down_own, ('y', 'z'), axis=0)]
    pallas_call x0 -> x8, Pallas kernels: none -> 231 us  [the longest x6 222 us: lay_out(): pl.pallas_call(kernel, out_shape=jax.ShapeDtypeStruct(out_shape, jnp.bflo...]
    all_gather x8 -> x0, blocking collectives: 147 us -> none  [the longest x1 29.4 us: local(): lax.all_gather(logsum, 'blk', axis=1, tiled=True)]
    ppermute x0 -> x53, waiting for transfers between devices: none -> 109 us  [send(): lax.ppermute(value, AXES, [(flat(p), flat(move(*p))) for p in everywhere])]
    ppermute x0 -> x53, starting transfers between devices: none -> 77.9 us  [send(): lax.ppermute(value, AXES, [(flat(p), flat(move(*p))) for p in everywhere])]
    dot_general x12, matrix products: 63.9 us -> 19.2 us  [the longest x8 16.7 us: dot(): return jnp.dot(left, right, preferred_element_type=jnp.float32)]
    unnamed x1 -> x0, blocking collectives: 26.3 us -> none
  transfers between devices with their start and end apart: 17 -> 58, of which waited for: 15 -> 18; matrix products, arithmetic and copies ran while one was open for 9% -> 21% of each run, Pallas kernels for 0% -> 39%
where the time goes in v1:
time: 598 us; the launch traced here: 593 us
  Pallas kernels  231 us (39%)
  waiting for transfers between devices  115 us (19%)
  starting transfers between devices  79 us (13%)
  local copies, waits for them, and re-layouts  61.9 us (10%)
  matrix products  45.9 us (8%)
  other arithmetic  44.5 us (7%)
  between operations  15.7 us (3%)
    pallas_call x6, Pallas kernels, lay_out(): pl.pallas_call(kernel, out_shape=jax.ShapeDtypeStruct(out_shape, jnp.bflo...  222 us
    ppermute x53, waiting for transfers between devices, send(): lax.ppermute(value, AXES, [(flat(p), flat(move(*p))) for p in everywhere])  109 us
    ppermute x53, starting transfers between devices, send(): lax.ppermute(value, AXES, [(flat(p), flat(move(*p))) for p in everywhere])  77.9 us
    unnamed x134, local copies, waits for them, and re-layouts  24.3 us
    dot_general x8, matrix products, dot(): return jnp.dot(left, right, preferred_element_type=jnp.float32)  16.7 us
    dot_general x8, matrix products, times_t(): lax.dot_general(left, right, (((1,), (1,)), ((), ())), preferred_element_...  13.6 us
    dot_general x8, matrix products, inner(): lax.dot_general(left, right, (((0,), (0,)), ((), ())), preferred_element_...  13 us
  transfers between devices with their start and end apart: 58, of which 18 were waited for; matrix products, arithmetic and copies ran while one was open for 21% of the time, Pallas kernels for 39%

profile of v1, /device:TPU:1, one launch (start us, length us, event | category | flops | bytes accessed | tf_op | source)
XLA Modules:
  0.0 592.9 jit_solution(12526724781897425074)
XLA Ops:
  14.8 5.0 collective-permute-start.26
  23.4 2.6 collective-permute-start
  45.7 5.0 collective-permute-done.5
  53.5 3.1 collective-permute-start.10
  56.7 2.5 collective-permute-start.11
  65.3 5.4 collective-permute-done.10.refs_1_
  70.7 25.8 %collective-permute-done.11.refs_2_ = bf16[160,1024]{1,0:T(8,128)(2,1)S(1)} collective-permute-done((bf16[160,1024]{1,0:T(8,128)(2,1)S(1)}, bf16[160,1024]{1,0:T(8,128)(2,1)S(1)}, u32[]{:S(2)}, u32[]{:S(2)}) %collective-permute-start.11) | collective-permute-done | bytes 327712 | tf_op jit(solution)/shard_map/ppermute | solution.py:290
  101.5 9.1 %shard_map.247 = bf16[128,1024]{1,0:T(8,128)(2,1)} custom-call(bf16[640,1024]{1,0:T(8,128)(2,1)} %copy-done.11), custom_call_target="tpu_custom_call" | custom-call | bytes 524288 | tf_op jit(solution)/shard_map/pallas_call | solution.py:365
  114.8 4.6 collective-permute-done.15.refs_7_
  119.4 17.1 %shard_map.251 = bf16[256,1024]{1,0:T(8,128)(2,1)} custom-call(bf16[160,1024]{1,0:T(8,128)(2,1)} %copy-done.12, bf16[160,1024]{1,0:T(8,128)(2,1)} %copy-done.20, bf16[160,1024]{1,0:T(8,128)(2,1)} %copy-done.21, bf16[160,1024]{1,0:T(8,128)(2,1)} %copy-done.22, bf16[160,1024]{1,0:T(8,128)(2,1)} %pad_maximum_fusion.13.refs_4_, bf16[160,1024]{1,0:T(8,128)(2,1)} %copy-done.23, ...), custom_call_target="tpu_custom_call" | custom-call | bytes 1048576 | tf_op jit(solution)/shard_map/pallas_call | solution.py:365
  136.7 48.9 %shard_map.248 = bf16[1024,768]{1,0:T(8,128)(2,1)} custom-call(bf16[160,1024]{1,0:T(8,128)(2,1)} %copy-done.12, bf16[160,1024]{1,0:T(8,128)(2,1)} %copy-done.20, bf16[160,1024]{1,0:T(8,128)(2,1)} %copy-done.21, bf16[160,1024]{1,0:T(8,128)(2,1)} %copy-done.22, bf16[160,1024]{1,0:T(8,128)(2,1)} %pad_maximum_fusion.13.refs_4_, bf16[160,1024]{1,0:T(8,128)(2,1)} %copy-done.23, ...), custom_call_target="tpu_custom_call" | custom-call | bytes 3145728 | tf_op jit(solution)/shard_map/pallas_call | solution.py:365
  185.6 17.3 %shard_map.250 = bf16[256,1024]{1,0:T(8,128)(2,1)} custom-call(bf16[160,1024]{1,0:T(8,128)(2,1)} %copy-done.12, bf16[160,1024]{1,0:T(8,128)(2,1)} %copy-done.20, bf16[160,1024]{1,0:T(8,128)(2,1)} %copy-done.21, bf16[160,1024]{1,0:T(8,128)(2,1)} %copy-done.22, bf16[160,1024]{1,0:T(8,128)(2,1)} %pad_maximum_fusion.13.refs_4_, bf16[160,1024]{1,0:T(8,128)(2,1)} %copy-done.23, ...), custom_call_target="tpu_custom_call" | custom-call | bytes 1048576 | tf_op jit(solution)/shard_map/pallas_call | solution.py:365
  212.8 64.8 %shard_map.246 = bf16[1024,1024]{1,0:T(8,128)(2,1)} custom-call(bf16[640,1024]{1,0:T(8,128)(2,1)} %copy-done.11, bf16[640,1024]{1,0:T(8,128)(2,1)} %collective-permute-done.8.refs_1_), custom_call_target="tpu_custom_call" | custom-call | bytes 4194304 | tf_op jit(solution)/shard_map/pallas_call | solution.py:365
  277.6 3.0 fusion.105
  283.9 4.1 shard_map.249
  298.5 64.8 %shard_map.252 = bf16[1024,1024]{1,0:T(8,128)(2,1)} custom-call(bf16[512,1024]{1,0:T(8,128)(2,1)} %pad_maximum_fusion.4.refs_0_, bf16[512,1024]{1,0:T(8,128)(2,1)} %collective-permute-done.23.refs_1_), custom_call_target="tpu_custom_call" | custom-call | bytes 4194304 | tf_op jit(solution)/shard_map/pallas_call | solution.py:365
  363.3 4.7 fusion.106
  382.3 3.2 fusion.20
  395.3 3.2 convolution_add_fusion.1
  402.0 11.7 %collective-permute-done.31 = bf16[256,1024]{1,0:T(8,128)(2,1)S(1)} collective-permute-done((bf16[256,1024]{1,0:T(8,128)(2,1)S(1)}, bf16[256,1024]{1,0:T(8,128)(2,1)S(1)}, u32[]{:S(2)}, u32[]{:S(2)}) %collective-permute-start.31) | collective-permute-done | bytes 524320 | tf_op jit(solution)/shard_map/ppermute | solution.py:290
  414.4 10.6 %collective-permute-done.21 = bf16[256,1024]{1,0:T(8,128)(2,1)S(1)} collective-permute-done((bf16[256,1024]{1,0:T(8,128)(2,1)S(1)}, bf16[256,1024]{1,0:T(8,128)(2,1)S(1)}, u32[]{:S(2)}, u32[]{:S(2)}) %collective-permute-start.21) | collective-permute-done | bytes 524320 | tf_op jit(solution)/shard_map/ppermute | solution.py:290
  433.4 4.9 shard_map.253
  447.0 3.5 convolution_convert_fusion.1
  462.5 8.1 %collective-permute-start.25 = (bf16[64,1024]{1,0:T(8,128)(2,1)}, bf16[64,1024]{1,0:T(8,128)(2,1)}, u32[]{:S(2)}, u32[]{:S(2)}) collective-permute-start(bf16[64,1024]{1,0:T(8,128)(2,1)} %get-tuple-element.118), channel_id=1, source_target_pairs={{0,2},{1,3},{2,0},{3,1},{4,10},{5,11},{6,8},{7,9},{8,6},{9,7},{10,... | collective-permute-start | bytes 393224 | tf_op jit(solution)/shard_map/ppermute | solution.py:290
  482.1 2.6 convolution_convert_fusion.8
  484.7 3.7 collective-permute-start.35
  488.4 4.8 collective-permute-start.36
  501.3 22.0 %collective-permute-done.39 = bf16[80,1024]{1,0:T(8,128)(2,1)S(1)} collective-permute-done((bf16[80,1024]{1,0:T(8,128)(2,1)}, bf16[80,1024]{1,0:T(8,128)(2,1)S(1)}, u32[]{:S(2)}, u32[]{:S(2)}) %collective-permute-start.39) | collective-permute-done | bytes 163872 | tf_op jit(solution)/shard_map/ppermute | solution.py:290
  528.1 7.3 %collective-permute-start.42 = (bf16[64,1024]{1,0:T(8,128)(2,1)S(1)}, bf16[64,1024]{1,0:T(8,128)(2,1)S(1)}, u32[]{:S(2)}, u32[]{:S(2)}) collective-permute-start(bf16[64,1024]{1,0:T(8,128)(2,1)S(1)} %slice.500), channel_id=1, source_target_pairs={{0,8},{1,9},{2,10},{3,11},{4,12},{5,13},{6,14},{7,15},{8,0},{9,1},... | collective-permute-start | bytes 393224 | tf_op jit(solution)/shard_map/ppermute | solution.py:290
  537.1 6.7 %collective-permute-done.48 = bf16[128,1024]{1,0:T(8,128)(2,1)S(1)} collective-permute-done((bf16[128,1024]{1,0:T(8,128)(2,1)S(1)}, bf16[128,1024]{1,0:T(8,128)(2,1)S(1)}, u32[]{:S(2)}, u32[]{:S(2)}) %collective-permute-start.48) | collective-permute-done | bytes 262176 | tf_op jit(solution)/shard_map/ppermute | solution.py:290
  549.9 6.3 %reduce-scatter.8.cloned.1.call-done = bf16[1,320,1024]{2,1,0:T(8,128)(2,1)} async-done(((bf16[4,320,1024]{2,1,0:T(8,128)(2,1)}), bf16[1,320,1024]{2,1,0:T(8,128)(2,1)}) %reduce-scatter.8.cloned.1.call-update) | async-done | bytes 655376 | tf_op jit(solution)/shard_map/reduce_scatter | solution.py:695
  563.7 9.1 %collective-permute-done.51 = bf16[320,1024]{1,0:T(8,128)(2,1)} collective-permute-done((bf16[320,1024]{1,0:T(8,128)(2,1)}, bf16[320,1024]{1,0:T(8,128)(2,1)}, u32[]{:S(2)}, u32[]{:S(2)}) %collective-permute-start.51) | collective-permute-done | bytes 655392 | tf_op jit(solution)/shard_map/ppermute | solution.py:290
  (414 shorter events, 181.8 us)
Async XLA Ops:
  7.2 363.0 %all-gather.6.cloned.1.call-start = ((), (), s32[]{:S(2)}) async-start(), calls=%async_computation.7 | async-start | bytes 2359296 | tf_op jit(solution)/shard_map/all_gather | solution.py:618
  11.0 33.1 %collective-permute-start.4 = (bf16[80,1024]{1,0:T(8,128)(2,1)}, bf16[80,1024]{1,0:T(8,128)(2,1)}, u32[]{:S(2)}, u32[]{:S(2)}) collective-permute-start(bf16[80,1024]{1,0:T(8,128)(2,1)} %pad_maximum_fusion.18), channel_id=1, source_target_pairs={{0,2},{1,3},{2,4},{3,5},{4,6},{5,7},{6,0},{7,1},{8,10},{9,11},{10,... | collective-permute-start | bytes 491528 | tf_op jit(solution)/shard_map/ppermute | solution.py:290
  14.8 21.5 %collective-permute-start.26 = (bf16[64,1024]{1,0:T(8,128)(2,1)}, bf16[64,1024]{1,0:T(8,128)(2,1)}, u32[]{:S(2)}, u32[]{:S(2)}) collective-permute-start(bf16[64,1024]{1,0:T(8,128)(2,1)} %get-tuple-element.114), channel_id=1, source_target_pairs={{0,0},{1,1},{2,2},{3,3},{4,8},{5,9},{6,10},{7,11},{8,4},{9,5},{10,... | collective-permute-start | bytes 393224 | tf_op jit(solution)/shard_map/ppermute | solution.py:290
  19.9 16.6 %collective-permute-start.27 = (bf16[64,1024]{1,0:T(8,128)(2,1)}, bf16[64,1024]{1,0:T(8,128)(2,1)}, u32[]{:S(2)}, u32[]{:S(2)}) collective-permute-start(bf16[64,1024]{1,0:T(8,128)(2,1)} %get-tuple-element.113), channel_id=1, source_target_pairs={{0,2},{1,3},{2,0},{3,1},{4,10},{5,11},{6,8},{7,9},{8,6},{9,7},{10,... | collective-permute-start | bytes 393224 | tf_op jit(solution)/shard_map/ppermute | solution.py:290
  21.2 355.3 %all-gather.4.cloned.1.call-start = ((), (), s32[]{:S(2)}) async-start(), calls=%async_computation.3 | async-start | bytes 2359296 | tf_op jit(solution)/shard_map/all_gather | solution.py:617
  23.4 17.0 %collective-permute-start = (bf16[64,1152]{1,0:T(8,128)(2,1)}, bf16[64,1152]{1,0:T(8,128)(2,1)S(1)}, u32[]{:S(2)}, u32[]{:S(2)}) collective-permute-start(bf16[64,1152]{1,0:T(8,128)(2,1)} %get-tuple-element.108), channel_id=1, source_target_pairs={{0,0},{1,1},{2,2},{3,3},{4,8},{5,9},{6,10},{7,11},{8,4},{9,5},{10,... | collective-permute-start | bytes 442376 | tf_op jit(solution)/shard_map/ppermute | solution.py:290
  26.0 15.7 %collective-permute-start.1 = (bf16[64,1152]{1,0:T(8,128)(2,1)}, bf16[64,1152]{1,0:T(8,128)(2,1)S(1)}, u32[]{:S(2)}, u32[]{:S(2)}) collective-permute-start(bf16[64,1152]{1,0:T(8,128)(2,1)} %get-tuple-element.107), channel_id=1, source_target_pairs={{0,2},{1,3},{2,0},{3,1},{4,10},{5,11},{6,8},{7,9},{8,6},{9,7},{10,... | collective-permute-start | bytes 442376 | tf_op jit(solution)/shard_map/ppermute | solution.py:290
  42.4 18.6 %collective-permute-start.2 = (bf16[128,1152]{1,0:T(8,128)(2,1)}, bf16[128,1152]{1,0:T(8,128)(2,1)S(1)}, u32[]{:S(2)}, u32[]{:S(2)}) collective-permute-start(bf16[128,1152]{1,0:T(8,128)(2,1)} %pad_maximum_fusion.14), channel_id=1, source_target_pairs={{0,1},{1,0},{2,3},{3,2},{4,5},{5,4},{6,7},{7,6},{8,9},{9,8},{10,11... | collective-permute-start | bytes 884744 | tf_op jit(solution)/shard_map/ppermute | solution.py:290
  52.0 46.0 %collective-permute-start.7 = (bf16[320,1024]{1,0:T(8,128)(2,1)}, bf16[320,1024]{1,0:T(8,128)(2,1)}, u32[]{:S(2)}, u32[]{:S(2)}) collective-permute-start(bf16[320,1024]{1,0:T(8,128)(2,1)} %get-tuple-element.127), channel_id=1, source_target_pairs={{0,1},{1,0},{2,3},{3,2},{4,5},{5,4},{6,7},{7,6},{8,9},{9,8},{10,11... | collective-permute-start | bytes 1966088 | tf_op jit(solution)/shard_map/ppermute | solution.py:290
  53.5 17.2 %collective-permute-start.10 = (bf16[160,1024]{1,0:T(8,128)(2,1)S(1)}, bf16[160,1024]{1,0:T(8,128)(2,1)S(1)}, u32[]{:S(2)}, u32[]{:S(2)}) collective-permute-start(bf16[160,1024]{1,0:T(8,128)(2,1)S(1)} %pad_maximum_fusion.12.refs_0_), channel_id=1, source_target_pairs={{0,2},{1,3},{2,4},{3,5},{4,6},{5,7},{6,0},{7,1},{8,10},{9,11},{10,... | collective-permute-start | bytes 983048 | tf_op jit(solution)/shard_map/ppermute | solution.py:290
  56.7 39.9 %collective-permute-start.11 = (bf16[160,1024]{1,0:T(8,128)(2,1)S(1)}, bf16[160,1024]{1,0:T(8,128)(2,1)S(1)}, u32[]{:S(2)}, u32[]{:S(2)}) collective-permute-start(bf16[160,1024]{1,0:T(8,128)(2,1)S(1)} %pad_maximum_fusion.12.refs_0_), channel_id=1, source_target_pairs={{0,4},{1,5},{2,6},{3,7},{4,0},{5,1},{6,2},{7,3},{8,12},{9,13},{10,... | collective-permute-start | bytes 983048 | tf_op jit(solution)/shard_map/ppermute | solution.py:290
  59.2 38.6 %collective-permute-start.12 = (bf16[160,1024]{1,0:T(8,128)(2,1)S(1)}, bf16[160,1024]{1,0:T(8,128)(2,1)S(1)}, u32[]{:S(2)}, u32[]{:S(2)}) collective-permute-start(bf16[160,1024]{1,0:T(8,128)(2,1)S(1)} %pad_maximum_fusion.12.refs_0_), channel_id=1, source_target_pairs={{0,6},{1,7},{2,0},{3,1},{4,2},{5,3},{6,4},{7,5},{8,14},{9,15},{10,... | collective-permute-start | bytes 983048 | tf_op jit(solution)/shard_map/ppermute | solution.py:290
  62.8 140.1 %collective-permute-start.3 = (bf16[256,1152]{1,0:T(8,128)(2,1)}, bf16[256,1152]{1,0:T(8,128)(2,1)}, u32[]{:S(2)}, u32[]{:S(2)}) collective-permute-start(bf16[256,1152]{1,0:T(8,128)(2,1)} %pad_maximum_fusion.8), channel_id=1, source_target_pairs={{0,8},{1,9},{2,10},{3,11},{4,12},{5,13},{6,14},{7,15},{8,0},{9,1},... | collective-permute-start | bytes 1769480 | tf_op jit(solution)/shard_map/ppermute | solution.py:290
  70.7 219.2 %collective-permute-start.19 = (bf16[128,512]{0,1:T(8,128)(2,1)}, bf16[128,512]{0,1:T(8,128)(2,1)S(1)}, u32[]{:S(2)}, u32[]{:S(2)}) collective-permute-start(bf16[128,512]{0,1:T(8,128)(2,1)} %bitcast.291), channel_id=1, source_target_pairs={{0,1},{1,0},{2,3},{3,2},{4,5},{5,4},{6,7},{7,6},{8,9},{9,8},{10,11... | collective-permute-start | bytes 393224 | tf_op jit(solution)/shard_map/ppermute | solution.py:290
  98.0 21.3 %collective-permute-start.15 = (bf16[160,1024]{1,0:T(8,128)(2,1)S(1)}, bf16[160,1024]{1,0:T(8,128)(2,1)}, u32[]{:S(2)}, u32[]{:S(2)}) collective-permute-start(bf16[160,1024]{1,0:T(8,128)(2,1)S(1)} %collective-permute-done.12.refs_3_), channel_id=1, source_target_pairs={{0,16},{1,17},{2,18},{3,19},{4,20},{5,21},{6,22},{7,23},{8,24},{9,... | collective-permute-start | bytes 983048 | tf_op jit(solution)/shard_map/ppermute | solution.py:290
  112.1 179.0 %collective-permute-start.28 = (bf16[128,1024]{1,0:T(8,128)(2,1)}, bf16[128,1024]{1,0:T(8,128)(2,1)}, u32[]{:S(2)}, u32[]{:S(2)}) collective-permute-start(bf16[128,1024]{1,0:T(8,128)(2,1)} %pad_maximum_fusion.16), channel_id=1, source_target_pairs={{0,1},{1,0},{2,3},{3,2},{4,5},{5,4},{6,7},{7,6},{8,9},{9,8},{10,11... | collective-permute-start | bytes 786440 | tf_op jit(solution)/shard_map/ppermute | solution.py:290
  112.3 100.5 %collective-permute-start.8 = (bf16[640,1024]{1,0:T(8,128)(2,1)}, bf16[640,1024]{1,0:T(8,128)(2,1)}, u32[]{:S(2)}, u32[]{:S(2)}) collective-permute-start(bf16[640,1024]{1,0:T(8,128)(2,1)} %copy-done.11), channel_id=1, source_target_pairs={{0,8},{1,9},{2,10},{3,11},{4,12},{5,13},{6,14},{7,15},{8,0},{9,1},... | collective-permute-start | bytes 3932168 | tf_op jit(solution)/shard_map/ppermute | solution.py:290
  136.5 73.4 %collective-permute-start.22 = (bf16[256,1024]{1,0:T(8,128)(2,1)}, bf16[256,1024]{1,0:T(8,128)(2,1)S(1)}, u32[]{:S(2)}, u32[]{:S(2)}) collective-permute-start(bf16[256,1024]{1,0:T(8,128)(2,1)} %shard_map.251), channel_id=1, source_target_pairs={{0,1},{1,0},{2,3},{3,2},{4,5},{5,4},{6,7},{7,6},{8,9},{9,8},{10,11... | collective-permute-start | bytes 1572872 | tf_op jit(solution)/shard_map/ppermute | solution.py:290
  211.0 87.5 %collective-permute-start.23 = (bf16[512,1024]{1,0:T(8,128)(2,1)}, bf16[512,1024]{1,0:T(8,128)(2,1)}, u32[]{:S(2)}, u32[]{:S(2)}) collective-permute-start(bf16[512,1024]{1,0:T(8,128)(2,1)} %pad_maximum_fusion.4.refs_0_), channel_id=1, source_target_pairs={{0,8},{1,9},{2,10},{3,11},{4,12},{5,13},{6,14},{7,15},{8,0},{9,1},... | collective-permute-start | bytes 3145736 | tf_op jit(solution)/shard_map/ppermute | solution.py:290
  290.8 209.3 %reduce-scatter.6.cloned.1.call-start = ((), (), s32[]{:S(2)}) async-start(), calls=%async_computation.5 | async-start | bytes 2621440 | tf_op jit(solution)/shard_map/reduce_scatter | solution.py:695
  296.1 71.9 %collective-permute-start.17 = (bf16[256,1024]{1,0:T(8,128)(2,1)S(1)}, bf16[256,1024]{1,0:T(8,128)(2,1)}, u32[]{:S(2)}, u32[]{:S(2)}) collective-permute-start(bf16[256,1024]{1,0:T(8,128)(2,1)S(1)} %fusion.24), channel_id=1, source_target_pairs={{0,1},{1,0},{2,3},{3,2},{4,5},{5,4},{6,7},{7,6},{8,9},{9,8},{10,11... | collective-permute-start | bytes 1572872 | tf_op jit(solution)/shard_map/ppermute | solution.py:290
  394.8 150.3 %reduce-scatter.4.cloned.1.call-start = ((), (), s32[]{:S(2)}) async-start(), calls=%async_computation.4 | async-start | bytes 2621440 | tf_op jit(solution)/shard_map/reduce_scatter | solution.py:695
  400.8 24.2 %collective-permute-start.21 = (bf16[256,1024]{1,0:T(8,128)(2,1)S(1)}, bf16[256,1024]{1,0:T(8,128)(2,1)S(1)}, u32[]{:S(2)}, u32[]{:S(2)}) collective-permute-start(bf16[256,1024]{1,0:T(8,128)(2,1)S(1)} %fusion.23), channel_id=1, source_target_pairs={{0,1},{1,0},{2,3},{3,2},{4,5},{5,4},{6,7},{7,6},{8,9},{9,8},{10,11... | collective-permute-start | bytes 1572872 | tf_op jit(solution)/shard_map/ppermute | solution.py:290
  441.1 115.1 %reduce-scatter.8.cloned.1.call-start = ((), (), s32[]{:S(2)}) async-start(), calls=%async_computation.6 | async-start | bytes 3276800 | tf_op jit(solution)/shard_map/reduce_scatter | solution.py:695
  462.5 33.1 %collective-permute-start.25 = (bf16[64,1024]{1,0:T(8,128)(2,1)}, bf16[64,1024]{1,0:T(8,128)(2,1)}, u32[]{:S(2)}, u32[]{:S(2)}) collective-permute-start(bf16[64,1024]{1,0:T(8,128)(2,1)} %get-tuple-element.118), channel_id=1, source_target_pairs={{0,2},{1,3},{2,0},{3,1},{4,10},{5,11},{6,8},{7,9},{8,6},{9,7},{10,... | collective-permute-start | bytes 393224 | tf_op jit(solution)/shard_map/ppermute | solution.py:290
  470.6 26.5 %collective-permute-start.24 = (bf16[64,1024]{1,0:T(8,128)(2,1)S(1)}, bf16[64,1024]{1,0:T(8,128)(2,1)}, u32[]{:S(2)}, u32[]{:S(2)}) collective-permute-start(bf16[64,1024]{1,0:T(8,128)(2,1)S(1)} %get-tuple-element.117), channel_id=1, source_target_pairs={{0,0},{1,1},{2,2},{3,3},{4,8},{5,9},{6,10},{7,11},{8,4},{9,5},{10,... | collective-permute-start | bytes 393224 | tf_op jit(solution)/shard_map/ppermute | solution.py:290
  495.6 27.6 %collective-permute-start.39 = (bf16[80,1024]{1,0:T(8,128)(2,1)}, bf16[80,1024]{1,0:T(8,128)(2,1)S(1)}, u32[]{:S(2)}, u32[]{:S(2)}) collective-permute-start(bf16[80,1024]{1,0:T(8,128)(2,1)} %get-tuple-element.89), channel_id=1, source_target_pairs={{0,4},{1,5},{2,6},{3,7},{4,0},{5,1},{6,2},{7,3},{8,12},{9,13},{10,... | collective-permute-start | bytes 491528 | tf_op jit(solution)/shard_map/ppermute | solution.py:290
  497.1 26.1 %collective-permute-start.38 = (bf16[80,1024]{1,0:T(8,128)(2,1)S(1)}, bf16[80,1024]{1,0:T(8,128)(2,1)S(1)}, u32[]{:S(2)}, u32[]{:S(2)}) collective-permute-start(bf16[80,1024]{1,0:T(8,128)(2,1)S(1)} %get-tuple-element.87), channel_id=1, source_target_pairs={{0,2},{1,3},{2,4},{3,5},{4,6},{5,7},{6,0},{7,1},{8,10},{9,11},{10,... | collective-permute-start | bytes 491528 | tf_op jit(solution)/shard_map/ppermute | solution.py:290
  500.1 35.3 %collective-permute-start.47 = (bf16[256,1024]{1,0:T(8,128)(2,1)}, bf16[256,1024]{1,0:T(8,128)(2,1)S(1)}, u32[]{:S(2)}, u32[]{:S(2)}) collective-permute-start(bf16[256,1024]{1,0:T(8,128)(2,1)} %bitcast.280), channel_id=1, source_target_pairs={{0,16},{1,17},{2,18},{3,19},{4,20},{5,21},{6,22},{7,23},{8,24},{9,... | collective-permute-start | bytes 1572872 | tf_op jit(solution)/shard_map/ppermute | solution.py:290
  528.1 18.1 %collective-permute-start.42 = (bf16[64,1024]{1,0:T(8,128)(2,1)S(1)}, bf16[64,1024]{1,0:T(8,128)(2,1)S(1)}, u32[]{:S(2)}, u32[]{:S(2)}) collective-permute-start(bf16[64,1024]{1,0:T(8,128)(2,1)S(1)} %slice.500), channel_id=1, source_target_pairs={{0,8},{1,9},{2,10},{3,11},{4,12},{5,13},{6,14},{7,15},{8,0},{9,1},... | collective-permute-start | bytes 393224 | tf_op jit(solution)/shard_map/ppermute | solution.py:290
  556.1 16.7 %collective-permute-start.51 = (bf16[320,1024]{1,0:T(8,128)(2,1)}, bf16[320,1024]{1,0:T(8,128)(2,1)}, u32[]{:S(2)}, u32[]{:S(2)}) collective-permute-start(bf16[320,1024]{1,0:T(8,128)(2,1)} %bitcast.274), channel_id=1, source_target_pairs={{0,16},{1,17},{2,18},{3,19},{4,20},{5,21},{6,22},{7,23},{8,24},{9,... | collective-permute-start | bytes 1966088 | tf_op jit(solution)/shard_map/ppermute | solution.py:290
  560.5 15.8 %collective-permute-start.44 = (bf16[128,768]{1,0:T(8,128)(2,1)S(1)}, bf16[128,768]{1,0:T(8,128)(2,1)S(1)}, u32[]{:S(2)}, u32[]{:S(2)}) collective-permute-start(bf16[128,768]{1,0:T(8,128)(2,1)S(1)} %fusion.62), channel_id=1, source_target_pairs={{0,1},{1,0},{2,3},{3,2},{4,5},{5,4},{6,7},{7,6},{8,9},{9,8},{10,11... | collective-permute-start | bytes 589832 | tf_op jit(solution)/shard_map/ppermute | solution.py:290
  (86 other events, 988.7 us)
Sparse Core Ops, SparseCore 0:
  21.3 78.6 all-gather.5
  290.9 52.7 all-gather.3
  394.9 48.0 reduce-scatter.5
  445.3 48.0 reduce-scatter.3
  495.5 60.5 reduce-scatter.7

commit v2 on v1

--- a/solution.py
+++ b/solution.py
@@ -341,35 +341,45 @@
     return jnp.where(index == 0, jnp.stack([mine, other]), jnp.stack([other, mine]))
 
 
-def lay_out(pieces, out_shape, copies):
-    count = len(copies(0, 0, 0, 0))
-
+def after(value, *earlier):
+    return lax.optimization_barrier((value, *earlier))[0]
+
+
+def coordinates():
+    return tuple(lax.axis_index(name) for name in AXES)
+
+
+def lay_out(pieces, out_shape, copies, dtype=jnp.bfloat16):
     def kernel(*refs):
-        sources, target, sems = refs[:-2], refs[-2], refs[-1]
-        place = tuple(lax.axis_index(name) for name in AXES)
-        started = []
-        for number, (piece, rows, columns, row, column) in enumerate(copies(*place)):
+        sources, target = refs[:-1], refs[-1]
+        for piece, rows, columns, row, column in copies(*coordinates()):
             size = rows[1] - rows[0]
             width = columns[1] - columns[0]
-            copy = pltpu.make_async_copy(
-                sources[piece].at[rows[0] : rows[1], columns[0] : columns[1]],
-                target.at[pl.ds(pl.multiple_of(row, 16), size), column : column + width],
-                sems.at[number],
-            )
-            copy.start()
-            started.append(copy)
-        for copy in started:
-            copy.wait()
-
-    size = math.prod(out_shape) * 2
-    return pl.pallas_call(
-        kernel,
-        out_shape=jax.ShapeDtypeStruct(out_shape, jnp.bfloat16),
-        in_specs=[pl.BlockSpec(memory_space=pl.ANY)] * len(pieces),
-        out_specs=pl.BlockSpec(memory_space=pl.ANY),
-        scratch_shapes=[pltpu.SemaphoreType.DMA((count,))],
-        cost_estimate=pl.CostEstimate(flops=0, bytes_accessed=2 * size, transcendentals=0),
-    )(*pieces)
+            part = sources[piece][rows[0] : rows[1], columns[0] : columns[1]].astype(dtype)
+            if not isinstance(row, int):
+                row = pl.multiple_of(row, 16)
+            if not isinstance(column, int):
+                column = pl.multiple_of(column, 128)
+            target[pl.ds(row, size), pl.ds(column, width)] = part
+
+    return in_vmem(kernel, out_shape, 0, 0, *pieces, dtype=dtype)
+
+
+def own_part(group, core, x, head):
+    pair = jnp.where(x == 0, group[:, : 2 * head], group[:, 2 * head :])
+    return jnp.where(core == 0, pair[:, :head], pair[:, head:])
+
+
+def own_columns(value, first, count, head, flip_x=False, flip_core=False):
+    def kernel(value_ref, out_ref):
+        _, core, _, x = coordinates()
+        core, x = (1 - core if flip_core else core), (1 - x if flip_x else x)
+        for number in range(count):
+            at = first + number * 4 * head
+            part = own_part(value_ref[:, at : at + 4 * head], core, x, head)
+            out_ref[:, number * head : (number + 1) * head] = part
+
+    return in_vmem(kernel, (value.shape[0], count * head), 0, 0, value)
 
 
 def dot(left, right):
@@ -417,11 +427,11 @@
         out_ref[:, 2 * width + at : 2 * width + at + size] = grad_values.astype(jnp.bfloat16)
 
 
-def in_vmem(kernel, out_shape, flops, transcendentals, *operands):
+def in_vmem(kernel, out_shape, flops, transcendentals, *operands, dtype=jnp.bfloat16):
     whole = pl.BlockSpec(memory_space=pltpu.VMEM)
     return pl.pallas_call(
         kernel,
-        out_shape=jax.ShapeDtypeStruct(out_shape, jnp.bfloat16),
+        out_shape=jax.ShapeDtypeStruct(out_shape, dtype),
         in_specs=[whole] * len(operands),
         out_specs=whole,
         compiler_params=pltpu.CompilerParams(vmem_limit_bytes=40 * 1024 * 1024),
@@ -466,11 +476,6 @@
         - normal * jnp.mean(scaled * normal, axis=-1, keepdims=True)
     )
     return factor * inside, jnp.stack([jnp.sum(grad * normal, axis=0), jnp.sum(grad, axis=0)])
-
-
-def wide(rows):
-    count, width = rows.shape
-    return rows.reshape(count, 4, width // 4).transpose(1, 0, 2).reshape(4 * count, width // 4)
 
 
 def grouped_plan(
@@ -508,12 +513,27 @@
     def pick(value, axis, index):
         return lax.dynamic_index_in_dim(value, index, axis, keepdims=False)
 
+    half, quarter = block // 2, block // 4
+    three = 3 * slice_width
+
+    vectors = jnp.stack([dec_bias, norm1_gain, norm1_shift, norm2_gain, norm2_shift])
+    tall = half + 16
+
+    def enc_kernel(enc_ref, vectors_ref, out_ref):
+        _, core, _, _ = coordinates()
+        out_ref[:half, :] = enc_ref[pl.ds(pl.multiple_of(core * half, 16), half), :]
+        out_ref[half:, :] = jnp.zeros((16, width), bf16)
+        out_ref[half : half + 5, :block] = vectors_ref[...]
+
+    enc_own = in_vmem(enc_kernel, (tall, width), 0, 0, enc_weight, vectors)
+    enc_near = [enc_own] + [place.shift_z(enc_own, k) for k in range(1, nz)]
+    enc_pieces = enc_near + [place.swap_x(part) for part in enc_near]
+
     express = jnp.log1p(counts.astype(f32)).astype(bf16)
     whole = jnp.stack([coords[0], coords[1], segment_ids], axis=-1)
     beside = jnp.concatenate([whole // SPLIT, whole % SPLIT], axis=-1).astype(bf16)
     beside = jnp.pad(beside, ((0, 0), (0, 0), (0, 122)))
-    cell_rows = jnp.concatenate([express, beside], axis=-1)
-    first, second = place.to_group(cell_rows)
+    first, second = place.to_group(jnp.concatenate([express, beside], axis=-1))
     cell_rows = place.whole_group(jnp.concatenate([first, second], axis=0))
     express = cell_rows[:, :genes]
     beside = cell_rows[:, genes:].astype(f32)
@@ -522,100 +542,145 @@
     segment_row = segment.reshape(1, rows)
     embed = sinusoids_of_whole((beside[:, 0:1], beside[:, 1:2]), width)
 
-    vectors = jnp.stack([dec_bias, norm1_gain, norm1_shift, norm2_gain, norm2_shift]).reshape(1, 5 * block)
-    vectors = jnp.pad(vectors, ((0, 15), (0, width - 5 * block)))
-    half = block // 2
-    tall = half + 16
-    enc_own = jnp.concatenate([pick(enc_weight.reshape(2, half, width), 0, place.core), vectors], axis=0)
-    enc_z = jnp.concatenate([enc_own] + [place.shift_z(enc_own, k) for k in range(1, nz)], axis=0)
-    enc_zx = jnp.concatenate([enc_z, place.swap_x(enc_z)], axis=0)
-    enc_far = place.swap_core(enc_zx)
+    qkv_mine = own_columns(qkv_weight, 0, 3 * nz, head)
+    qkv_theirs = own_columns(qkv_weight, 0, 3 * nz, head, flip_x=True)
+
+    def rows_kernel(value_ref, out_ref):
+        y, _, _, _ = coordinates()
+        out_ref[...] = value_ref[pl.ds(pl.multiple_of(y * half, 16), half), :]
+
+    qkv_theirs = place.swap_x(in_vmem(rows_kernel, (half, three), 0, 0, qkv_theirs))
+
+    def qkv_kernel(mine_ref, theirs_ref, out_weight_ref, out_ref):
+        y, core, _, _ = coordinates()
+        out_ref[:half, :three] = mine_ref[pl.ds(pl.multiple_of(y * half, 16), half), :]
+        out_ref[half:, :three] = theirs_ref[...]
+        at = pl.multiple_of(core * half + y * quarter, 16)
+        for j in range(4):
+            out_ref[j * quarter : (j + 1) * quarter, three:] = out_weight_ref[
+                pl.ds(at, quarter), j * slice_width : (j + 1) * slice_width
+            ]
+
+    qkv_own = in_vmem(qkv_kernel, (block, width), 0, 0, qkv_mine, qkv_theirs, out_weight)
+    qkv_own = after(qkv_own, *enc_near[1:])
+    near = [qkv_own] + [place.shift_z(qkv_own, k) for k in range(1, nz)]
+    far = [place.swap_y(part) for part in near]
+
+    lanes = ff // (8 * nz)
+    up_half = nz * lanes
+
+    def up_columns(up_ref, out_ref, x):
+        y, core, _, _ = coordinates()
+        for number in range(nz):
+            at = ((2 * number + x) * 2 + core) * 2 + y
+            out_ref[:block, number * lanes : (number + 1) * lanes] = up_ref[
+                :, pl.ds(pl.multiple_of(at * lanes, lanes), lanes)
+            ]
+
+    def dec_rows(dec_ref):
+        y, core, _, _ = coordinates()
+        return dec_ref[pl.ds(pl.multiple_of(core * half + y * quarter, 16), quarter), :]
+
+    def up_theirs_kernel(up_ref, dec_ref, out_ref):
+        _, _, _, x = coordinates()
+        up_columns(up_ref, out_ref, 1 - x)
+        part = dec_rows(dec_ref)
+        out_ref[block : block + quarter, :] = part[:, :up_half]
+        out_ref[block + quarter :, :] = part[:, up_half:]
+
+    up_theirs = in_vmem(up_theirs_kernel, (block + half, up_half), 0, 0, up_weight, dec_weight)
+    up_theirs = place.swap_x(up_theirs)
+    many = down_weight.shape[0] // 4
+    dec_at = block + many
+
+    def up_kernel(up_ref, theirs_ref, down_ref, dec_ref, out_ref):
+        y, core, _, x = coordinates()
+        up_columns(up_ref, out_ref, x)
+        out_ref[:block, up_half:] = theirs_ref[:block, :]
+        out_ref[block:dec_at, :] = down_ref[
+            pl.ds(pl.multiple_of((2 * core + y) * many, 16), many), :
+        ]
+        out_ref[dec_at : dec_at + quarter, :] = dec_rows(dec_ref)
+        out_ref[dec_at + quarter :, :up_half] = theirs_ref[block : block + quarter, :]
+        out_ref[dec_at + quarter :, up_half:] = theirs_ref[block + quarter :, :]
+
+    up_own = in_vmem(
+        up_kernel, (dec_at + half, width), 0, 0, up_weight, up_theirs, down_weight, dec_weight
+    )
+    up_near, up_far = [after(up_own, *near[1:])], []
+    for k in range(1, nz):
+        up_far.append(place.swap_y(up_near[-1]))
+        up_near.append(place.shift_z(after(up_near[-1], *up_far[k - 2 : k - 1]), 1))
+    up_far.append(place.swap_y(up_near[-1]))
+    up_pieces = up_near + up_far
 
     def enc_copies(y, core, z, x):
         return [
-            (dc, ((dx * nz + k) * tall, (dx * nz + k) * tall + half), (0, width),
-             (2 * ((z - k) % nz) + (x ^ dx)) * block + (core ^ dc) * half, 0)
-            for dc in range(2) for dx in range(2) for k in range(nz)
+            (dx * nz + k, (0, half), (0, width), (2 * ((z - k) % nz) + (x ^ dx)) * half, 0)
+            for dx in range(2) for k in range(nz)
         ]
 
     def vector_copies(y, core, z, x):
         return [
-            (0, ((dx * nz + k) * tall + half, (dx * nz + k + 1) * tall), (0, width),
-             (2 * ((z - k) % nz) + (x ^ dx)) * 16, 0)
+            (dx * nz + k, (half, tall), (0, block), 0, (2 * ((z - k) % nz) + (x ^ dx)) * block)
             for dx in range(2) for k in range(nz)
         ]
 
-    w_enc = lay_out((enc_zx, enc_far), (genes, width), enc_copies)
-    vectors = lay_out((enc_zx,), (2 * nz * 16, width), vector_copies)
-    vectors = vectors.reshape(2 * nz, 16, width)[:, 0, : 5 * block].reshape(2 * nz, 5, block)
-    vectors = vectors.transpose(1, 0, 2).reshape(5, width).astype(f32)
+    def both_cores(count):
+        def copies(y, core, z, x):
+            return [
+                (dc, (k * half, (k + 1) * half), (0, width), k * block + (core ^ dc) * half, 0)
+                for dc in range(2) for k in range(count)
+            ]
+
+        return copies
+
+    enc_half = lay_out(enc_pieces, (genes // 2, width), enc_copies)
+    w_enc = lay_out((enc_half, place.swap_core(enc_half)), (genes, width), both_cores(2 * nz))
+    vectors = lay_out(enc_pieces, (16, width), vector_copies, dtype=f32)
     b_dec, gain_one, shift_one, gain_two, shift_two = (vectors[i : i + 1] for i in range(5))
-
-    qkv_parts = qkv_weight.reshape(block, 3, nz, 2, 2, head)
-    qkv_parts = pick(qkv_parts, 4, place.core)
-    qkv_mine = pick(qkv_parts, 3, place.x).reshape(block, 3 * slice_width)
-    qkv_theirs = pick(qkv_parts, 3, 1 - place.x).reshape(block, 3 * slice_width)
-    qkv_pair = jnp.stack([qkv_mine, place.swap_x(qkv_theirs)]).reshape(2, 2, half, 3 * slice_width)
-    out_parts = pick(out_weight.reshape(2, 2, half // 2, width), 0, place.core)
-    dec_parts = pick(dec_weight.reshape(2, 2, half // 2, genes), 0, place.core)
-    quarter = half // 2
-
-    def piece(of):
-        top = jnp.concatenate(
-            [pick(qkv_pair, 1, of).reshape(block, 3 * slice_width), wide(pick(out_parts, 0, of))],
-            axis=1,
-        )
-        return jnp.concatenate([top, pick(dec_parts, 0, of)], axis=0)
-
-    near = piece(place.y)
-    near = [near] + [place.shift_z(near, k) for k in range(1, nz)]
-    far = [piece(1 - place.y)] + [place.swap_y(part) for part in near[1:]]
 
     def qkv_copies(y, core, z, x):
         return [
-            (dy * nz + k, (dx * half, (dx + 1) * half), (0, 3 * slice_width),
+            (dy * nz + k, (dx * half, (dx + 1) * half), (0, three),
              (2 * ((z - k) % nz) + (x ^ dx)) * block + (y ^ dy) * half, 0)
             for k in range(nz) for dy in range(2) for dx in range(2)
         ]
 
     def out_copies(y, core, z, x):
         return [
-            (dy * nz + k, (j * quarter, (j + 1) * quarter), (3 * slice_width, width),
+            (dy * nz + k, (j * quarter, (j + 1) * quarter), (three, width),
              ((z - k) % nz) * half + (y ^ dy) * quarter, j * slice_width)
             for k in range(nz) for dy in range(2) for j in range(4)
         ]
 
+    w_qkv = lay_out(near + far, (width, three), qkv_copies)
+    w_out = lay_out(near + far, (slice_width, width), out_copies)
+
+    def up_copies(y, core, z, x):
+        return [
+            (dy * nz + k, (0, block), (dx * up_half, (dx + 1) * up_half),
+             (2 * ((z - k) % nz) + (x ^ dx)) * block, (y ^ dy) * up_half)
+            for k in range(nz) for dy in range(2) for dx in range(2)
+        ]
+
+    def down_copies(y, core, z, x):
+        return [
+            (dy * nz + k, (block, dec_at), (0, width), ((y ^ dy) * nz + ((z - k) % nz)) * many, 0)
+            for k in range(nz) for dy in range(2)
+        ]
+
     def dec_copies(y, core, z, x):
         return [
-            (dy * nz + k, (block, block + quarter), (0, width),
-             ((z - k) % nz) * half + (y ^ dy) * quarter, 0)
-            for k in range(nz) for dy in range(2)
-        ]
-
-    w_qkv = lay_out(near + far, (width, 3 * slice_width), qkv_copies)
-    w_out = lay_out(near + far, (slice_width, width), out_copies)
-    dec_z = lay_out(near + far, (slice_width, genes), dec_copies)
-    dec_zx = jnp.concatenate([dec_z, place.swap_x(dec_z)], axis=0)
-    dec_far = place.swap_core(dec_zx)
-
-    def dec_all_copies(y, core, z, x):
-        return [
-            (dc, ((dx * nz + k) * half, (dx * nz + k + 1) * half), (0, genes),
-             (2 * k + (x ^ dx)) * block + (core ^ dc) * half, 0)
-            for dc in range(2) for dx in range(2) for k in range(nz)
-        ]
-
-    w_dec = lay_out((dec_zx, dec_far), (width, genes), dec_all_copies)
-
-    up_parts = up_weight.reshape(block, nz, 2, 2, 2, ff // (8 * nz))
-    up_parts = pick(pick(up_parts, 4, place.y), 3, place.core)
-    up_mine = pick(up_parts, 2, place.x).reshape(block, ff_slice // 2)
-    up_theirs = pick(up_parts, 2, 1 - place.x).reshape(block, ff_slice // 2)
-    up_own = in_order(place.x, up_mine, place.swap_x(up_theirs)).reshape(2 * block, ff_slice // 2)
-    down_parts = down_weight.reshape(2, 2, down_weight.shape[0] // 4, width)
-    down_own = pick(pick(down_parts, 0, place.core), 0, place.y)
-    w_up = lax.all_gather(up_own, ("y", "z"), axis=0).reshape(2, width, ff_slice // 2)
-    w_down = lax.all_gather(down_own, ("y", "z"), axis=0).reshape(2, ff_slice // 2, width)
+            (dy * nz + k, (dec_at + dx * quarter, dec_at + (dx + 1) * quarter), (0, genes),
+             (2 * ((z - k) % nz) + (x ^ dx)) * half + (y ^ dy) * quarter, 0)
+            for k in range(nz) for dy in range(2) for dx in range(2)
+        ]
+
+    dec_half = lay_out(up_pieces, (width // 2, genes), dec_copies)
+    w_dec = lay_out((dec_half, place.swap_core(dec_half)), (width, genes), both_cores(2 * nz))
+    w_up = lay_out(up_pieces, (width, ff_slice), up_copies)
+    w_down = lay_out(up_pieces, (ff_slice, width), down_copies)
 
     first, second = place.to_group(logit_grad)
     cotangent = place.whole_group(jnp.concatenate([first, second], axis=0))
@@ -637,29 +702,26 @@
     normal2, factor2 = normalise(hidden1)
     normed2 = (normal2 * gain_two + shift_two).astype(bf16)
     normed2 = jnp.concatenate([normed2, place.swap_core(normed2)], axis=0)
-    up_value = [dot(normed2, w_up[i]) for i in range(2)]
-    active = [jax.nn.gelu(value).astype(bf16) for value in up_value]
-    hidden2 = hidden1 + place.sum_group(dot(active[0], w_down[0]) + dot(active[1], w_down[1]))
+    up_value = dot(normed2, w_up)
+    active = jax.nn.gelu(up_value).astype(bf16)
+    hidden2 = hidden1 + place.sum_group(dot(active, w_down))
     hidden2 = hidden2.astype(bf16)
     logits = (dot(hidden2[:own_rows], w_dec) + b_dec).astype(bf16)
     logits = place.from_group(logits.reshape(seqs, cells, genes))
 
-    hidden2_parts = pick(hidden2.reshape(half_rows, nz, 2, 2, half), 2, place.x)
     hidden2_slice = jnp.concatenate(
         [
-            pick(hidden2_parts, 2, place.core).reshape(half_rows, slice_width),
-            place.swap_core(pick(hidden2_parts, 2, 1 - place.core).reshape(half_rows, slice_width)),
+            own_columns(hidden2, 0, nz, half),
+            place.swap_core(own_columns(hidden2, 0, nz, half, flip_core=True)),
         ],
         axis=0,
     )
     grad_w_dec = inner(hidden2_slice, cotangent).astype(bf16)
-    grad_w_down = [inner(part, grad_down).astype(bf16) for part in active]
-    grad_active = [times_t(grad_down, w_down[i]) for i in range(2)]
-    grad_up = [
-        jax.vjp(jax.nn.gelu, up_value[i])[1](grad_active[i])[0].astype(bf16) for i in range(2)
-    ]
-    grad_w_up = jnp.concatenate([inner(normed2, part) for part in grad_up], axis=1).astype(bf16)
-    grad_normed2 = place.sum_group(times_t(grad_up[0], w_up[0]) + times_t(grad_up[1], w_up[1]))
+    grad_w_down = inner(active, grad_down).astype(bf16)
+    grad_active = times_t(grad_down, w_down)
+    grad_up = jax.vjp(jax.nn.gelu, up_value)[1](grad_active)[0].astype(bf16)
+    grad_w_up = inner(normed2, grad_up).astype(bf16)
+    grad_normed2 = place.sum_group(times_t(grad_up, w_up))
     part_two, sums_two = normalise_back(grad_normed2, normal2, factor2, gain_two)
     grad_h1 = grad_h2[:half_rows] + part_two
     grad_attn = grad_h1.astype(bf16)
@@ -688,70 +750,101 @@
     input_grad = times_t(grad_h0[:own_rows], w_enc).astype(bf16)
     input_grad = place.from_group(input_grad.reshape(seqs, cells, genes))
     grad_h0, sums_one = beside_core(grad_h0, sums_one)
-    express_slice = pick(pick(express.reshape(rows, nz, 2, 2, half), 2, place.x), 2, place.core)
-    grad_w_enc = inner(express_slice.reshape(rows, slice_width), grad_h0)
-
-    def over_z(value):
-        return lax.psum_scatter(value, "z", scatter_dimension=0, tiled=False)
-
-    def over_y(value):
-        return value.astype(f32) + place.swap_y(value).astype(f32)
-
-    ff_piece = ff_slice // (2 * nz)
-    early = jnp.concatenate(
-        [part.reshape(nz, ff_piece, width) for part in grad_w_down]
-        + [grad_w_dec.reshape(nz, half, genes)],
-        axis=1,
-    )
-    early = over_y(over_z(early))
-    early = in_order(place.core, early, place.swap_core(early.astype(bf16)).astype(f32))
-    out_down = early[:, : 2 * ff_piece].reshape(4 * ff_piece, width)
-    out_dec = early[:, 2 * ff_piece :].reshape(block, genes)
+    express_slice = own_columns(cell_rows, 0, nz, half)
+    grad_w_enc = inner(express_slice, grad_h0)
+
+    def half_over_y(value):
+        parts = value.reshape(nz, 2, value.shape[1] // 2, value.shape[2])
+        other = place.swap_y(pick(parts, 1, 1 - place.y))
+        return (pick(parts, 1, place.y).astype(f32) + other.astype(f32)).astype(bf16)
+
+    def direct_over_z(value):
+        total = pick(value, 0, place.z).astype(f32)
+        for k in range(1, nz):
+            total += place.shift_z(pick(value, 0, (place.z + k) % nz), k).astype(f32)
+        return total
+
+    down_sum = jnp.swapaxes(grad_w_down.reshape(2, nz, many, width), 0, 1)
+    down_sum = half_over_y(down_sum.reshape(nz, 2 * many, width))
+    down_sum = direct_over_z(down_sum).astype(bf16)
+    down_sum = in_order(place.y, down_sum, place.swap_y(down_sum)).reshape(2 * many, width)
+
+    def down_copies_out(y, core, z, x):
+        return [
+            (dc, (0, 2 * many), (0, width), (core ^ dc) * 2 * many, 0) for dc in range(2)
+        ]
+
+    out_down = lay_out(
+        (down_sum, place.swap_core(down_sum)), (4 * many, width), down_copies_out, dtype=f32
+    )
 
     def whole_columns(value):
-        low = value.astype(bf16)
+        value = value.reshape(2, block, value.shape[-1])
         mine = pick(value, 0, place.x)
-        theirs = place.swap_x(pick(low, 0, 1 - place.x)).astype(f32)
-        both = in_order(place.x, mine, theirs)
-        other = place.swap_core(both.astype(bf16)).astype(f32)
-        return in_order(place.core, both, other)
-
-    middle = over_y(over_z(grad_w_up.reshape(nz, 2 * block, ff_slice)))
-    out_up = whole_columns(middle.reshape(2, block, ff_slice))
-    out_up = out_up.reshape(2, 2, block, 2, nz, ff_piece).transpose(2, 4, 1, 0, 3, 5)
-    out_up = out_up.reshape(block, ff)
-
-    late = jnp.concatenate(
-        [
-            grad_w_qkv.reshape(nz, 2 * block, 3 * slice_width),
-            grad_w_out.reshape(nz, half, 4, slice_width)
-            .transpose(0, 2, 1, 3)
-            .reshape(nz, 2 * block, slice_width),
-        ],
-        axis=2,
-    )
-    late = over_y(over_z(late))
-    out_qkv = whole_columns(late[:, : 3 * slice_width].reshape(2, block, 3 * slice_width))
-    out_qkv = out_qkv.reshape(2, 2, block, 3, nz, head).transpose(2, 3, 4, 1, 0, 5)
-    out_qkv = out_qkv.reshape(block, 3 * width)
-    out_out = late[:, 3 * slice_width :].reshape(4, half, slice_width).transpose(1, 0, 2)
-    out_out = out_out.reshape(half, width)
-    out_out = in_order(place.core, out_out, place.swap_core(out_out.astype(bf16)).astype(f32))
-    out_out = out_out.reshape(block, width)
+        both = jnp.concatenate([mine, place.swap_x(pick(value, 0, 1 - place.x))], axis=0)
+        return both, place.swap_core(both)
+
+    up_sum = half_over_y(grad_w_up.reshape(nz, 2 * block, ff_slice))
+    up_sum = direct_over_z(up_sum).astype(bf16)
+    up_sum = in_order(place.y, up_sum, place.swap_y(up_sum))
+
+    def up_copies_out(y, core, z, x):
+        return [
+            (dc, (dx * block, (dx + 1) * block), ((j * nz + k) * lanes, (j * nz + k + 1) * lanes),
+             0, (((2 * k + (x ^ dx)) * 2 + (core ^ dc)) * 2 + j) * lanes)
+            for dc in range(2) for dx in range(2) for j in range(2) for k in range(nz)
+        ]
+
+    out_up = lay_out(whole_columns(up_sum), (block, ff), up_copies_out, dtype=f32)
+
+    few = jnp.concatenate(
+        [grad_w_out.reshape(nz, half, width), grad_w_dec.reshape(nz, half, genes)], axis=1
+    )
+    few = direct_over_z(half_over_y(few)).astype(bf16)
+    few = in_order(place.y, few, place.swap_y(few)).reshape(block, width)
+
+    def half_copies_out(first):
+        def copies(y, core, z, x):
+            return [
+                (dc, (first, first + half), (0, width), (core ^ dc) * half, 0) for dc in range(2)
+            ]
+
+        return copies
+
+    few = (few, place.swap_core(few))
+    out_out = lay_out(few, (block, width), half_copies_out(0), dtype=f32)
+    out_dec = lay_out(few, (block, genes), half_copies_out(half), dtype=f32)
+
+    qkv_sum = half_over_y(grad_w_qkv.reshape(nz, 2 * block, three))
+    qkv_sum = direct_over_z(qkv_sum).astype(bf16)
+    qkv_sum = in_order(place.y, qkv_sum, place.swap_y(qkv_sum))
+
+    def qkv_out_kernel(near_ref, far_ref, out_ref):
+        _, core, _, x = coordinates()
+        for dx in range(2):
+            for number in range(3 * nz):
+                at = slice(dx * block, (dx + 1) * block), slice(number * head, (number + 1) * head)
+                near_part, far_part = near_ref[at].astype(f32), far_ref[at].astype(f32)
+                low = jnp.where(core == 0, near_part, far_part)
+                high = jnp.where(core == 0, far_part, near_part)
+                column = pl.multiple_of(number * 4 * head + (x ^ dx) * 2 * head, 2 * head)
+                out_ref[:, pl.ds(column, 2 * head)] = jnp.concatenate([low, high], axis=1)
+
+    out_qkv = in_vmem(
+        qkv_out_kernel, (block, 3 * width), 0, 0, *whole_columns(qkv_sum), dtype=f32
+    )
 
     sums = jnp.concatenate([grad_bias, sums_one, sums_two], axis=0).reshape(5, nz, 2, block)
-    sums = pick(sums, 2, place.x).transpose(1, 0, 2).reshape(nz, 1, 5 * block)
-    sums = jnp.pad(sums, ((0, 0), (0, 15), (0, width - 5 * block)))
-    last = jnp.concatenate([grad_w_enc.reshape(nz, half, width), sums], axis=1)
-    last_low = last.astype(bf16)
-    total = pick(last, 0, place.z)
-    for k in range(1, nz):
-        total += place.shift_z(pick(last_low, 0, (place.z + k) % nz), k).astype(f32)
-    total = total + place.swap_y(total.astype(bf16)).astype(f32)
-    out_enc = total[:half]
-    out_enc = in_order(place.core, out_enc, place.swap_core(out_enc.astype(bf16)).astype(f32))
-    out_enc = out_enc.reshape(block, width)
-    sums = total[half, : 5 * block].reshape(5, block)
+    sums = pick(sums, 2, place.x).transpose(1, 0, 2)
+    sums = jnp.pad(sums, ((0, 0), (0, 11), (0, width - block)))
+    last = jnp.concatenate([grad_w_enc.reshape(nz, half, width), sums], axis=1).astype(bf16)
+    last = direct_over_z(last)
+    last = last + place.swap_y(last.astype(bf16)).astype(f32)
+    sums = last[half : half + 5, :block]
+    last = last[:half].astype(bf16)
+    out_enc = lay_out(
+        (last, place.swap_core(last)), (block, width), half_copies_out(0), dtype=f32
+    )
     return (
         logits, input_grad, out_enc, out_qkv, out_out, out_up, out_down, out_dec,
         sums[0], sums[1], sums[2], sums[3], sums[4],

time: 598 us -> 361 us (0.60)
  Pallas kernels: 231 us -> 24.7 us
  local copies, waits for them, and re-layouts: 61.9 us -> 17.4 us
  starting transfers between devices: 79 us -> 115 us
  waiting for transfers between devices: 115 us -> 138 us
  other arithmetic: 44.5 us -> 22.5 us
  between operations: 15.7 us -> 2.36 us
  matrix products: 45.9 us -> 34.2 us
    pallas_call x8 -> x27, Pallas kernels: 231 us -> 24.7 us  [in_vmem(): pl.pallas_call(kernel, out_shape=jax.ShapeDtypeStruct(out_shape, dtype),...]
    ppermute x53 -> x80, starting transfers between devices: 77.9 us -> 115 us  [send(): lax.ppermute(value, AXES, [(flat(p), flat(move(*p))) for p in everywhere])]
    ppermute x53 -> x80, waiting for transfers between devices: 109 us -> 138 us  [send(): lax.ppermute(value, AXES, [(flat(p), flat(move(*p))) for p in everywhere])]
    unnamed x134 -> x92, local copies, waits for them, and re-layouts: 24.3 us -> 9.95 us
    slice x10 -> x2, local copies, waits for them, and re-layouts: 11.6 us -> 0.61 us  [the longest x1 0.6 us: grouped_plan(): vectors[i:i + 1]]
    dot_general x8 -> x6, matrix products: 16.7 us -> 7.09 us  [dot(): return jnp.dot(left, right, preferred_element_type=jnp.float32)]
    concatenate x9 -> x5, other arithmetic: 8.54 us -> 1.15 us  [the longest x2 0.99 us: whole_columns(): jnp.concatenate([mine, place.swap_x(pick(value, 0, 1 - place.x))], axis=0)]
    dot_general x8 -> x6, matrix products: 13.6 us -> 7.24 us  [times_t(): lax.dot_general(left, right, (((1,), (1,)), ((), ())), preferred_element_...]
  transfers between devices with their start and end apart: 58 -> 80, of which waited for: 18 -> 33; matrix products, arithmetic and copies ran while one was open for 21% -> 18% of each run, Pallas kernels for 39% -> 7%
where the time goes in v2:
time: 361 us; the launch traced here: 354 us
  waiting for transfers between devices  138 us (38%)
  starting transfers between devices  115 us (32%)
  matrix products  34.2 us (9%)
  Pallas kernels  24.7 us (7%)
  other arithmetic  22.5 us (6%)
  local copies, waits for them, and re-layouts  17.4 us (5%)
    ppermute x80, waiting for transfers between devices, send(): lax.ppermute(value, AXES, [(flat(p), flat(move(*p))) for p in everywhere])  138 us
    ppermute x80, starting transfers between devices, send(): lax.ppermute(value, AXES, [(flat(p), flat(move(*p))) for p in everywhere])  115 us
    pallas_call x27, Pallas kernels, in_vmem(): pl.pallas_call(kernel, out_shape=jax.ShapeDtypeStruct(out_shape, dtype),...  24.7 us
    dot_general x6, matrix products, inner(): lax.dot_general(left, right, (((0,), (0,)), ((), ())), preferred_element_...  17.3 us
    unnamed x92, local copies, waits for them, and re-layouts  9.95 us
    dot_general x6, matrix products, times_t(): lax.dot_general(left, right, (((1,), (1,)), ((), ())), preferred_element_...  7.24 us
  transfers between devices with their start and end apart: 80, of which 33 were waited for; matrix products, arithmetic and copies ran while one was open for 18% of the time, Pallas kernels for 7%

profile of v2, /device:TPU:1, one launch (start us, length us, event | category | flops | bytes accessed | tf_op | source)
XLA Modules:
  0.0 354.2 jit_solution(1961272017769416150)
XLA Ops:
  4.6 3.3 collective-permute-start.6
  12.4 4.2 %collective-permute-start = (bf16[64,1152]{1,0:T(8,128)(2,1)S(1)}, bf16[64,1152]{1,0:T(8,128)(2,1)S(1)}, u32[]{:S(2)}, u32[]{:S(2)}) collective-permute-start(bf16[64,1152]{1,0:T(8,128)(2,1)S(1)} %get-tuple-element.77), channel_id=1, source_target_pairs={{0,0},{1,1},{2,2},{3,3},{4,8},{5,9},{6,10},{7,11},{8,4},{9,5},{10,... | collective-permute-start | bytes 442376 | tf_op jit(solution)/shard_map/ppermute | solution.py:290
  19.5 5.3 %collective-permute-done = bf16[64,1152]{1,0:T(8,128)(2,1)S(1)} collective-permute-done((bf16[64,1152]{1,0:T(8,128)(2,1)S(1)}, bf16[64,1152]{1,0:T(8,128)(2,1)S(1)}, u32[]{:S(2)}, u32[]{:S(2)}) %collective-permute-start) | collective-permute-done | bytes 147488 | tf_op jit(solution)/shard_map/ppermute | solution.py:290
  29.1 3.8 %collective-permute-done.4.refs_1_ = bf16[80,1024]{1,0:T(8,128)(2,1)S(1)} collective-permute-done((bf16[80,1024]{1,0:T(8,128)(2,1)S(1)}, bf16[80,1024]{1,0:T(8,128)(2,1)S(1)}, u32[]{:S(2)}, u32[]{:S(2)}) %collective-permute-start.4) | collective-permute-done | bytes 163872 | tf_op jit(solution)/shard_map/ppermute | solution.py:290
  37.1 2.9 collective-permute-done.10.refs_7_
  41.5 6.0 %collective-permute-start.3 = (bf16[256,1152]{1,0:T(8,128)(2,1)S(1)}, bf16[256,1152]{1,0:T(8,128)(2,1)S(1)}, u32[]{:S(2)}, u32[]{:S(2)}) collective-permute-start(bf16[256,1152]{1,0:T(8,128)(2,1)S(1)} %pad_maximum_fusion.7), channel_id=1, source_target_pairs={{0,8},{1,9},{2,10},{3,11},{4,12},{5,13},{6,14},{7,15},{8,0},{9,1},... | collective-permute-start | bytes 1769480 | tf_op jit(solution)/shard_map/ppermute | solution.py:290
  49.3 7.5 %collective-permute-done.14.refs_2_ = bf16[128,1024]{1,0:T(8,128)(2,1)S(1)} collective-permute-done((bf16[128,1024]{1,0:T(8,128)(2,1)S(1)}, bf16[128,1024]{1,0:T(8,128)(2,1)S(1)}, u32[]{:S(2)}, u32[]{:S(2)}) %collective-permute-start.14) | collective-permute-done | bytes 262176 | tf_op jit(solution)/shard_map/ppermute | solution.py:290
  66.7 4.1 %collective-permute-done.17.refs_5_ = bf16[128,1024]{1,0:T(8,128)(2,1)S(1)} collective-permute-done((bf16[128,1024]{1,0:T(8,128)(2,1)S(1)}, bf16[128,1024]{1,0:T(8,128)(2,1)S(1)}, u32[]{:S(2)}, u32[]{:S(2)}) %collective-permute-start.17) | collective-permute-done | bytes 262176 | tf_op jit(solution)/shard_map/ppermute | solution.py:290
  75.3 3.4 collective-permute-done.24.refs_1_
  78.6 6.2 %collective-permute-done.25.refs_4_ = bf16[320,1024]{1,0:T(8,128)(2,1)S(1)} collective-permute-done((bf16[320,1024]{1,0:T(8,128)(2,1)S(1)}, bf16[320,1024]{1,0:T(8,128)(2,1)S(1)}, u32[]{:S(2)}, u32[]{:S(2)}) %collective-permute-start.25) | collective-permute-done | bytes 655392 | tf_op jit(solution)/shard_map/ppermute | solution.py:290
  91.2 4.1 %shard_map.255 = bf16[512,256]{1,0:T(8,128)(2,1)S(1)} custom-call(bf16[512,768]{1,0:T(8,128)(2,1)S(1)} %convolution_convert_fusion.3.qkv_ref, f32[512,1]{1,0:T(8,128)S(1)} %get-tuple-element.89.column_ref, f32[1,512]{1,0:T(1,128)S(1)} %bitcast.175), custom_call_target="tpu_custom_call" | custom-call | flops 268435456 | bytes 524288 | tf_op jit(solution)/shard_map/pallas_call | solution.py:432
  95.9 3.7 %collective-permute-start.20 = (bf16[256,1024]{1,0:T(8,128)(2,1)S(1)}, bf16[256,1024]{1,0:T(8,128)(2,1)S(1)}, u32[]{:S(2)}, u32[]{:S(2)}) collective-permute-start(bf16[256,1024]{1,0:T(8,128)(2,1)S(1)} %slice.429), channel_id=1, source_target_pairs={{0,8},{1,9},{2,10},{3,11},{4,12},{5,13},{6,14},{7,15},{8,0},{9,1},... | collective-permute-start | bytes 1572872 | tf_op jit(solution)/shard_map/ppermute | solution.py:290
  101.6 6.7 %collective-permute-start.37 = (bf16[64,1024]{1,0:T(8,128)(2,1)S(1)}, bf16[64,1024]{1,0:T(8,128)(2,1)S(1)}, u32[]{:S(2)}, u32[]{:S(2)}) collective-permute-start(bf16[64,1024]{1,0:T(8,128)(2,1)S(1)} %get-tuple-element.82), channel_id=1, source_target_pairs={{0,2},{1,3},{2,0},{3,1},{4,10},{5,11},{6,8},{7,9},{8,6},{9,7},{10,... | collective-permute-start | bytes 393224 | tf_op jit(solution)/shard_map/ppermute | solution.py:290
  111.8 3.8 %collective-permute-done.28.refs_3_ = bf16[320,1024]{1,0:T(8,128)(2,1)} collective-permute-done((bf16[320,1024]{1,0:T(8,128)(2,1)}, bf16[320,1024]{1,0:T(8,128)(2,1)}, u32[]{:S(2)}, u32[]{:S(2)}) %collective-permute-start.28) | collective-permute-done | bytes 655392 | tf_op jit(solution)/shard_map/ppermute | solution.py:290
  119.2 6.0 %collective-permute-start.22 = (bf16[256,1024]{1,0:T(8,128)(2,1)}, bf16[256,1024]{1,0:T(8,128)(2,1)}, u32[]{:S(2)}, u32[]{:S(2)}) collective-permute-start(bf16[256,1024]{1,0:T(8,128)(2,1)} %add_convert_fusion.3), channel_id=1, source_target_pairs={{0,8},{1,9},{2,10},{3,11},{4,12},{5,13},{6,14},{7,15},{8,0},{9,1},... | collective-permute-start | bytes 1572872 | tf_op jit(solution)/shard_map/ppermute | solution.py:290
  126.6 8.2 %collective-permute-done.38 = bf16[128,1024]{1,0:T(8,128)(2,1)} collective-permute-done((bf16[128,1024]{1,0:T(8,128)(2,1)}, bf16[128,1024]{1,0:T(8,128)(2,1)}, u32[]{:S(2)}, u32[]{:S(2)}) %collective-permute-start.38) | collective-permute-done | bytes 262176 | tf_op jit(solution)/shard_map/ppermute | solution.py:290
  159.9 6.5 %collective-permute-done.32 = bf16[256,1024]{1,0:T(8,128)(2,1)S(1)} collective-permute-done((bf16[256,1024]{1,0:T(8,128)(2,1)S(1)}, bf16[256,1024]{1,0:T(8,128)(2,1)S(1)}, u32[]{:S(2)}, u32[]{:S(2)}) %collective-permute-start.32) | collective-permute-done | bytes 524320 | tf_op jit(solution)/shard_map/ppermute | solution.py:290
  171.7 12.5 %convolution_convert_fusion = bf16[1024,1024]{1,0:T(8,128)(2,1)S(1)} fusion(f32[512,1024]{1,0:T(8,128)S(1)} %fusion.110, f32[512,1024]{1,0:T(8,128)S(1)} %fusion.28), kind=kOutput, calls=%fused_computation.19 | convolution fusion | flops 1080033280 | bytes 6291456 | tf_op jit(solution)/shard_map/dot_general | solution.py:37
  188.8 3.7 %collective-permute-done.67 = bf16[4,128,1024]{2,1,0:T(8,128)(2,1)S(1)} collective-permute-done((bf16[4,128,1024]{2,1,0:T(8,128)(2,1)S(1)}, bf16[4,128,1024]{2,1,0:T(8,128)(2,1)S(1)}, u32[]{:S(2)}, u32[]{:S(2)}) %collective-permute-start.67) | collective-permute-done | bytes 1048608 | tf_op jit(solution)/shard_map/ppermute | solution.py:290
  196.3 18.7 %collective-permute-done.74 = bf16[4,128,1024]{2,1,0:T(8,128)(2,1)S(1)} collective-permute-done((bf16[4,128,1024]{2,1,0:T(8,128)(2,1)S(1)}, bf16[4,128,1024]{2,1,0:T(8,128)(2,1)S(1)}, u32[]{:S(2)}, u32[]{:S(2)}) %collective-permute-start.74) | collective-permute-done | bytes 1048608 | tf_op jit(solution)/shard_map/ppermute | solution.py:290
  224.3 4.7 %collective-permute-done.77 = bf16[128,1024]{1,0:T(8,128)(2,1)S(1)} collective-permute-done((bf16[128,1024]{1,0:T(8,128)(2,1)S(1)}, bf16[128,1024]{1,0:T(8,128)(2,1)S(1)}, u32[]{:S(2)}, u32[]{:S(2)}) %collective-permute-start.77) | collective-permute-done | bytes 262176 | tf_op jit(solution)/shard_map/ppermute | solution.py:290
  229.1 10.9 %collective-permute-done.76 = bf16[128,1024]{1,0:T(8,128)(2,1)S(1)} collective-permute-done((bf16[128,1024]{1,0:T(8,128)(2,1)S(1)}, bf16[128,1024]{1,0:T(8,128)(2,1)S(1)}, u32[]{:S(2)}, u32[]{:S(2)}) %collective-permute-start.76) | collective-permute-done | bytes 262176 | tf_op jit(solution)/shard_map/ppermute | solution.py:290
  250.4 4.9 %shard_map.263 = bf16[512,768]{1,0:T(8,128)(2,1)S(1)} custom-call(bf16[512,768]{1,0:T(8,128)(2,1)S(1)} %copy-done.25, bf16[512,256]{1,0:T(8,128)(2,1)S(1)} %convolution_convert_fusion.8.grad_ref, f32[512,1]{1,0:T(8,128)S(1)} %copy-done.21, f32[1,512]{1,0:T(1,128)S(1)} %bitcast.176), custom_call_target="tpu_custom_call" | custom-call | flops 671088640 | bytes 1572864 | tf_op jit(solution)/shard_map/pallas_call | solution.py:432
  260.5 8.5 %collective-permute-done.61 = bf16[4,64,1024]{2,1,0:T(8,128)(2,1)S(1)} collective-permute-done((bf16[4,64,1024]{2,1,0:T(8,128)(2,1)S(1)}, bf16[4,64,1024]{2,1,0:T(8,128)(2,1)S(1)}, u32[]{:S(2)}, u32[]{:S(2)}) %collective-permute-start.61) | collective-permute-done | bytes 524320 | tf_op jit(solution)/shard_map/ppermute | solution.py:290
  269.3 3.3 collective-permute-start.64
  275.1 3.8 %collective-permute-start.73 = (bf16[256,1024]{1,0:T(8,128)(2,1)S(1)}, bf16[256,1024]{1,0:T(8,128)(2,1)S(1)}, u32[]{:S(2)}, u32[]{:S(2)}) collective-permute-start(bf16[256,1024]{1,0:T(8,128)(2,1)S(1)} %pad_maximum_fusion.11.refs_0_), channel_id=1, source_target_pairs={{0,8},{1,9},{2,10},{3,11},{4,12},{5,13},{6,14},{7,15},{8,0},{9,1},... | collective-permute-start | bytes 1572872 | tf_op jit(solution)/shard_map/ppermute | solution.py:290
  280.3 3.7 %collective-permute-done.63 = bf16[64,1024]{1,0:T(8,128)(2,1)S(1)} collective-permute-done((bf16[64,1024]{1,0:T(8,128)(2,1)S(1)}, bf16[64,1024]{1,0:T(8,128)(2,1)S(1)}, u32[]{:S(2)}, u32[]{:S(2)}) %collective-permute-start.63) | collective-permute-done | bytes 131104 | tf_op jit(solution)/shard_map/ppermute | solution.py:290
  287.9 3.3 collective-permute-start.56
  296.1 6.0 %collective-permute-start.34 = (bf16[64,1024]{1,0:T(8,128)(2,1)}, bf16[64,1024]{1,0:T(8,128)(2,1)}, u32[]{:S(2)}, u32[]{:S(2)}) collective-permute-start(bf16[64,1024]{1,0:T(8,128)(2,1)} %get-tuple-element.86), channel_id=1, source_target_pairs={{0,0},{1,1},{2,2},{3,3},{4,8},{5,9},{6,10},{7,11},{8,4},{9,5},{10,... | collective-permute-start | bytes 393224 | tf_op jit(solution)/shard_map/ppermute | solution.py:290
  303.6 7.9 %collective-permute-done.55 = bf16[128,768]{1,0:T(8,128)(2,1)} collective-permute-done((bf16[128,768]{1,0:T(8,128)(2,1)}, bf16[128,768]{1,0:T(8,128)(2,1)}, u32[]{:S(2)}, u32[]{:S(2)}) %collective-permute-start.55) | collective-permute-done | bytes 196640 | tf_op jit(solution)/shard_map/ppermute | solution.py:290
  334.6 3.2 collective-permute-done.50
  337.7 7.4 %collective-permute-done.49 = bf16[80,1024]{1,0:T(8,128)(2,1)S(1)} collective-permute-done((bf16[80,1024]{1,0:T(8,128)(2,1)S(1)}, bf16[80,1024]{1,0:T(8,128)(2,1)S(1)}, u32[]{:S(2)}, u32[]{:S(2)}) %collective-permute-start.49) | collective-permute-done | bytes 163872 | tf_op jit(solution)/shard_map/ppermute | solution.py:290
  (377 shorter events, 163.7 us)
Async XLA Ops:
  2.4 32.4 %collective-permute-start.7 = (bf16[80,1024]{1,0:T(8,128)(2,1)S(1)}, bf16[80,1024]{1,0:T(8,128)(2,1)S(1)}, u32[]{:S(2)}, u32[]{:S(2)}) collective-permute-start(bf16[80,1024]{1,0:T(8,128)(2,1)S(1)} %shard_map.246.refs_0_), channel_id=1, source_target_pairs={{0,1},{1,0},{2,3},{3,2},{4,5},{5,4},{6,7},{7,6},{8,9},{9,8},{10,11... | collective-permute-start | bytes 491528 | tf_op jit(solution)/shard_map/ppermute | solution.py:290
  4.6 24.4 %collective-permute-start.6 = (bf16[80,1024]{1,0:T(8,128)(2,1)S(1)}, bf16[80,1024]{1,0:T(8,128)(2,1)S(1)}, u32[]{:S(2)}, u32[]{:S(2)}) collective-permute-start(bf16[80,1024]{1,0:T(8,128)(2,1)S(1)} %shard_map.246.refs_0_), channel_id=1, source_target_pairs={{0,6},{1,7},{2,0},{3,1},{4,2},{5,3},{6,4},{7,5},{8,14},{9,15},{10,... | collective-permute-start | bytes 491528 | tf_op jit(solution)/shard_map/ppermute | solution.py:290
  7.9 21.2 %collective-permute-start.5 = (bf16[80,1024]{1,0:T(8,128)(2,1)S(1)}, bf16[80,1024]{1,0:T(8,128)(2,1)S(1)}, u32[]{:S(2)}, u32[]{:S(2)}) collective-permute-start(bf16[80,1024]{1,0:T(8,128)(2,1)S(1)} %shard_map.246.refs_0_), channel_id=1, source_target_pairs={{0,4},{1,5},{2,6},{3,7},{4,0},{5,1},{6,2},{7,3},{8,12},{9,13},{10,... | collective-permute-start | bytes 491528 | tf_op jit(solution)/shard_map/ppermute | solution.py:290
  32.9 16.1 %collective-permute-start.15 = (bf16[128,1024]{1,0:T(8,128)(2,1)S(1)}, bf16[128,1024]{1,0:T(8,128)(2,1)S(1)}, u32[]{:S(2)}, u32[]{:S(2)}) collective-permute-start(bf16[128,1024]{1,0:T(8,128)(2,1)S(1)} %shard_map.253.refs_0_), channel_id=1, source_target_pairs={{0,6},{1,7},{2,0},{3,1},{4,2},{5,3},{6,4},{7,5},{8,14},{9,15},{10,... | collective-permute-start | bytes 786440 | tf_op jit(solution)/shard_map/ppermute | solution.py:290
  32.9 23.9 %collective-permute-start.14 = (bf16[128,1024]{1,0:T(8,128)(2,1)S(1)}, bf16[128,1024]{1,0:T(8,128)(2,1)S(1)}, u32[]{:S(2)}, u32[]{:S(2)}) collective-permute-start(bf16[128,1024]{1,0:T(8,128)(2,1)S(1)} %shard_map.253.refs_0_), channel_id=1, source_target_pairs={{0,4},{1,5},{2,6},{3,7},{4,0},{5,1},{6,2},{7,3},{8,12},{9,13},{10,... | collective-permute-start | bytes 786440 | tf_op jit(solution)/shard_map/ppermute | solution.py:290
  34.8 23.2 %collective-permute-start.13 = (bf16[128,1024]{1,0:T(8,128)(2,1)S(1)}, bf16[128,1024]{1,0:T(8,128)(2,1)S(1)}, u32[]{:S(2)}, u32[]{:S(2)}) collective-permute-start(bf16[128,1024]{1,0:T(8,128)(2,1)S(1)} %shard_map.253.refs_0_), channel_id=1, source_target_pairs={{0,2},{1,3},{2,4},{3,5},{4,6},{5,7},{6,0},{7,1},{8,10},{9,11},{10,... | collective-permute-start | bytes 786440 | tf_op jit(solution)/shard_map/ppermute | solution.py:290
  41.5 29.5 %collective-permute-start.3 = (bf16[256,1152]{1,0:T(8,128)(2,1)S(1)}, bf16[256,1152]{1,0:T(8,128)(2,1)S(1)}, u32[]{:S(2)}, u32[]{:S(2)}) collective-permute-start(bf16[256,1152]{1,0:T(8,128)(2,1)S(1)} %pad_maximum_fusion.7), channel_id=1, source_target_pairs={{0,8},{1,9},{2,10},{3,11},{4,12},{5,13},{6,14},{7,15},{8,0},{9,1},... | collective-permute-start | bytes 1769480 | tf_op jit(solution)/shard_map/ppermute | solution.py:290
  59.0 28.7 %collective-permute-start.11 = (bf16[512,1024]{1,0:T(8,128)(2,1)S(1)}, bf16[512,1024]{1,0:T(8,128)(2,1)S(1)}, u32[]{:S(2)}, u32[]{:S(2)}) collective-permute-start(bf16[512,1024]{1,0:T(8,128)(2,1)S(1)} %shard_map.247.refs_0_), channel_id=1, source_target_pairs={{0,8},{1,9},{2,10},{3,11},{4,12},{5,13},{6,14},{7,15},{8,0},{9,1},... | collective-permute-start | bytes 3145736 | tf_op jit(solution)/shard_map/ppermute | solution.py:290
  61.8 23.0 %collective-permute-start.25 = (bf16[320,1024]{1,0:T(8,128)(2,1)S(1)}, bf16[320,1024]{1,0:T(8,128)(2,1)S(1)}, u32[]{:S(2)}, u32[]{:S(2)}) collective-permute-start(bf16[320,1024]{1,0:T(8,128)(2,1)S(1)} %shard_map.258.refs_0_), channel_id=1, source_target_pairs={{0,16},{1,17},{2,18},{3,19},{4,20},{5,21},{6,22},{7,23},{8,24},{9,... | collective-permute-start | bytes 1966088 | tf_op jit(solution)/shard_map/ppermute | solution.py:290
  101.6 23.6 %collective-permute-start.37 = (bf16[64,1024]{1,0:T(8,128)(2,1)S(1)}, bf16[64,1024]{1,0:T(8,128)(2,1)S(1)}, u32[]{:S(2)}, u32[]{:S(2)}) collective-permute-start(bf16[64,1024]{1,0:T(8,128)(2,1)S(1)} %get-tuple-element.82), channel_id=1, source_target_pairs={{0,2},{1,3},{2,0},{3,1},{4,10},{5,11},{6,8},{7,9},{8,6},{9,7},{10,... | collective-permute-start | bytes 393224 | tf_op jit(solution)/shard_map/ppermute | solution.py:290
  108.3 16.9 %collective-permute-start.36 = (bf16[64,1024]{1,0:T(8,128)(2,1)S(1)}, bf16[64,1024]{1,0:T(8,128)(2,1)S(1)}, u32[]{:S(2)}, u32[]{:S(2)}) collective-permute-start(bf16[64,1024]{1,0:T(8,128)(2,1)S(1)} %get-tuple-element.83), channel_id=1, source_target_pairs={{0,0},{1,1},{2,2},{3,3},{4,8},{5,9},{6,10},{7,11},{8,4},{9,5},{10,... | collective-permute-start | bytes 393224 | tf_op jit(solution)/shard_map/ppermute | solution.py:290
  110.5 26.2 %collective-permute-start.29 = (bf16[320,1024]{1,0:T(8,128)(2,1)}, bf16[320,1024]{1,0:T(8,128)(2,1)}, u32[]{:S(2)}, u32[]{:S(2)}) collective-permute-start(bf16[320,1024]{1,0:T(8,128)(2,1)} %collective-permute-done.26.refs_2_), channel_id=1, source_target_pairs={{0,16},{1,17},{2,18},{3,19},{4,20},{5,21},{6,22},{7,23},{8,24},{9,... | collective-permute-start | bytes 1966088 | tf_op jit(solution)/shard_map/ppermute | solution.py:290
  115.7 22.2 %collective-permute-start.30 = (bf16[320,1024]{1,0:T(8,128)(2,1)}, bf16[320,1024]{1,0:T(8,128)(2,1)}, u32[]{:S(2)}, u32[]{:S(2)}) collective-permute-start(bf16[320,1024]{1,0:T(8,128)(2,1)} %collective-permute-done.28.refs_3_), channel_id=1, source_target_pairs={{0,16},{1,17},{2,18},{3,19},{4,20},{5,21},{6,22},{7,23},{8,24},{9,... | collective-permute-start | bytes 1966088 | tf_op jit(solution)/shard_map/ppermute | solution.py:290
  119.2 27.3 %collective-permute-start.22 = (bf16[256,1024]{1,0:T(8,128)(2,1)}, bf16[256,1024]{1,0:T(8,128)(2,1)}, u32[]{:S(2)}, u32[]{:S(2)}) collective-permute-start(bf16[256,1024]{1,0:T(8,128)(2,1)} %add_convert_fusion.3), channel_id=1, source_target_pairs={{0,8},{1,9},{2,10},{3,11},{4,12},{5,13},{6,14},{7,15},{8,0},{9,1},... | collective-permute-start | bytes 1572872 | tf_op jit(solution)/shard_map/ppermute | solution.py:290
  169.0 23.5 %collective-permute-start.67 = (bf16[4,128,1024]{2,1,0:T(8,128)(2,1)S(1)}, bf16[4,128,1024]{2,1,0:T(8,128)(2,1)S(1)}, u32[]{:S(2)}, u32[]{:S(2)}) collective-permute-start(bf16[4,128,1024]{2,1,0:T(8,128)(2,1)S(1)} %dynamic-slice_bitcast_fusion.1), channel_id=1, source_target_pairs={{0,16},{1,17},{2,18},{3,19},{4,20},{5,21},{6,22},{7,23},{8,24},{9,... | collective-permute-start | bytes 3145736 | tf_op jit(solution)/shard_map/ppermute | solution.py:290
  184.3 30.7 %collective-permute-start.74 = (bf16[4,128,1024]{2,1,0:T(8,128)(2,1)S(1)}, bf16[4,128,1024]{2,1,0:T(8,128)(2,1)S(1)}, u32[]{:S(2)}, u32[]{:S(2)}) collective-permute-start(bf16[4,128,1024]{2,1,0:T(8,128)(2,1)S(1)} %dynamic-slice_bitcast_fusion), channel_id=1, source_target_pairs={{0,16},{1,17},{2,18},{3,19},{4,20},{5,21},{6,22},{7,23},{8,24},{9,... | collective-permute-start | bytes 3145736 | tf_op jit(solution)/shard_map/ppermute | solution.py:290
  193.0 25.8 %collective-permute-start.68 = (bf16[128,1024]{1,0:T(8,128)(2,1)S(1)}, bf16[128,1024]{1,0:T(8,128)(2,1)S(1)}, u32[]{:S(2)}, u32[]{:S(2)}) collective-permute-start(bf16[128,1024]{1,0:T(8,128)(2,1)S(1)} %get-tuple-element.46), channel_id=1, source_target_pairs={{0,2},{1,3},{2,4},{3,5},{4,6},{5,7},{6,0},{7,1},{8,10},{9,11},{10,... | collective-permute-start | bytes 786440 | tf_op jit(solution)/shard_map/ppermute | solution.py:290
  193.8 25.7 %collective-permute-start.70 = (bf16[128,1024]{1,0:T(8,128)(2,1)S(1)}, bf16[128,1024]{1,0:T(8,128)(2,1)S(1)}, u32[]{:S(2)}, u32[]{:S(2)}) collective-permute-start(bf16[128,1024]{1,0:T(8,128)(2,1)S(1)} %get-tuple-element.47), channel_id=1, source_target_pairs={{0,6},{1,7},{2,0},{3,1},{4,2},{5,3},{6,4},{7,5},{8,14},{9,15},{10,... | collective-permute-start | bytes 786440 | tf_op jit(solution)/shard_map/ppermute | solution.py:290
  196.3 26.0 %collective-permute-start.69 = (bf16[128,1024]{1,0:T(8,128)(2,1)S(1)}, bf16[128,1024]{1,0:T(8,128)(2,1)S(1)}, u32[]{:S(2)}, u32[]{:S(2)}) collective-permute-start(bf16[128,1024]{1,0:T(8,128)(2,1)S(1)} %get-tuple-element.48), channel_id=1, source_target_pairs={{0,4},{1,5},{2,6},{3,7},{4,0},{5,1},{6,2},{7,3},{8,12},{9,13},{10,... | collective-permute-start | bytes 786440 | tf_op jit(solution)/shard_map/ppermute | solution.py:290
  218.8 21.2 %collective-permute-start.76 = (bf16[128,1024]{1,0:T(8,128)(2,1)S(1)}, bf16[128,1024]{1,0:T(8,128)(2,1)S(1)}, u32[]{:S(2)}, u32[]{:S(2)}) collective-permute-start(bf16[128,1024]{1,0:T(8,128)(2,1)S(1)} %get-tuple-element.45), channel_id=1, source_target_pairs={{0,4},{1,5},{2,6},{3,7},{4,0},{5,1},{6,2},{7,3},{8,12},{9,13},{10,... | collective-permute-start | bytes 786440 | tf_op jit(solution)/shard_map/ppermute | solution.py:290
  219.6 21.8 %collective-permute-start.60 = (bf16[256,256]{1,0:T(8,128)(2,1)S(1)}, bf16[256,256]{1,0:T(8,128)(2,1)S(1)}, u32[]{:S(2)}, u32[]{:S(2)}) collective-permute-start(bf16[256,256]{1,0:T(8,128)(2,1)S(1)} %shard_map.268), channel_id=1, source_target_pairs={{0,8},{1,9},{2,10},{3,11},{4,12},{5,13},{6,14},{7,15},{8,0},{9,1},... | collective-permute-start | bytes 393224 | tf_op jit(solution)/shard_map/ppermute | solution.py:290
  222.3 26.8 %collective-permute-start.42 = (bf16[272,1024]{1,0:T(8,128)(2,1)S(1)}, bf16[272,1024]{1,0:T(8,128)(2,1)S(1)}, u32[]{:S(2)}, u32[]{:S(2)}) collective-permute-start(bf16[272,1024]{1,0:T(8,128)(2,1)S(1)} %fusion.31), channel_id=1, source_target_pairs={{0,8},{1,9},{2,10},{3,11},{4,12},{5,13},{6,14},{7,15},{8,0},{9,1},... | collective-permute-start | bytes 1671176 | tf_op jit(solution)/shard_map/ppermute | solution.py:290
  223.1 18.7 %collective-permute-start.71 = (bf16[128,1024]{1,0:T(8,128)(2,1)S(1)}, bf16[128,1024]{1,0:T(8,128)(2,1)S(1)}, u32[]{:S(2)}, u32[]{:S(2)}) collective-permute-start(bf16[128,1024]{1,0:T(8,128)(2,1)S(1)} %fusion.38), channel_id=1, source_target_pairs={{0,16},{1,17},{2,18},{3,19},{4,20},{5,21},{6,22},{7,23},{8,24},{9,... | collective-permute-start | bytes 786440 | tf_op jit(solution)/shard_map/ppermute | solution.py:290
  242.0 18.4 %collective-permute-start.72 = (bf16[128,1024]{1,0:T(8,128)(2,1)S(1)}, bf16[128,1024]{1,0:T(8,128)(2,1)S(1)}, u32[]{:S(2)}, u32[]{:S(2)}) collective-permute-start(bf16[128,1024]{1,0:T(8,128)(2,1)S(1)} %get-tuple-element.57), channel_id=1, source_target_pairs={{0,1},{1,0},{2,3},{3,2},{4,5},{5,4},{6,7},{7,6},{8,9},{9,8},{10,11... | collective-permute-start | bytes 786440 | tf_op jit(solution)/shard_map/ppermute | solution.py:290
  246.4 40.7 %collective-permute-start.79 = (bf16[256,1024]{1,0:T(8,128)(2,1)S(1)}, bf16[256,1024]{1,0:T(8,128)(2,1)S(1)}, u32[]{:S(2)}, u32[]{:S(2)}) collective-permute-start(bf16[256,1024]{1,0:T(8,128)(2,1)S(1)} %bitcast.173), channel_id=1, source_target_pairs={{0,8},{1,9},{2,10},{3,11},{4,12},{5,13},{6,14},{7,15},{8,0},{9,1},... | collective-permute-start | bytes 1572872 | tf_op jit(solution)/shard_map/ppermute | solution.py:290
  259.3 26.7 %collective-permute-start.53 = (bf16[4,128,768]{2,1,0:T(8,128)(2,1)S(1)}, bf16[4,128,768]{2,1,0:T(8,128)(2,1)S(1)}, u32[]{:S(2)}, u32[]{:S(2)}) collective-permute-start(bf16[4,128,768]{2,1,0:T(8,128)(2,1)S(1)} %dynamic-slice_bitcast_fusion.2), channel_id=1, source_target_pairs={{0,16},{1,17},{2,18},{3,19},{4,20},{5,21},{6,22},{7,23},{8,24},{9,... | collective-permute-start | bytes 2359304 | tf_op jit(solution)/shard_map/ppermute | solution.py:290
  278.9 35.1 %collective-permute-start.44 = (bf16[256,1024]{1,0:T(8,128)(2,1)}, bf16[256,1024]{1,0:T(8,128)(2,1)}, u32[]{:S(2)}, u32[]{:S(2)}) collective-permute-start(bf16[256,1024]{1,0:T(8,128)(2,1)} %fusion.13), channel_id=1, source_target_pairs={{0,1},{1,0},{2,3},{3,2},{4,5},{5,4},{6,7},{7,6},{8,9},{9,8},{10,11... | collective-permute-start | bytes 1572872 | tf_op jit(solution)/shard_map/ppermute | solution.py:290
  287.1 16.1 %collective-permute-start.54 = (bf16[128,768]{1,0:T(8,128)(2,1)}, bf16[128,768]{1,0:T(8,128)(2,1)}, u32[]{:S(2)}, u32[]{:S(2)}) collective-permute-start(bf16[128,768]{1,0:T(8,128)(2,1)} %get-tuple-element.50), channel_id=1, source_target_pairs={{0,2},{1,3},{2,4},{3,5},{4,6},{5,7},{6,0},{7,1},{8,10},{9,11},{10,... | collective-permute-start | bytes 589832 | tf_op jit(solution)/shard_map/ppermute | solution.py:290
  292.0 19.6 %collective-permute-start.55 = (bf16[128,768]{1,0:T(8,128)(2,1)}, bf16[128,768]{1,0:T(8,128)(2,1)}, u32[]{:S(2)}, u32[]{:S(2)}) collective-permute-start(bf16[128,768]{1,0:T(8,128)(2,1)} %get-tuple-element.52), channel_id=1, source_target_pairs={{0,4},{1,5},{2,6},{3,7},{4,0},{5,1},{6,2},{7,3},{8,12},{9,13},{10,... | collective-permute-start | bytes 589832 | tf_op jit(solution)/shard_map/ppermute | solution.py:290
  296.1 30.5 %collective-permute-start.34 = (bf16[64,1024]{1,0:T(8,128)(2,1)}, bf16[64,1024]{1,0:T(8,128)(2,1)}, u32[]{:S(2)}, u32[]{:S(2)}) collective-permute-start(bf16[64,1024]{1,0:T(8,128)(2,1)} %get-tuple-element.86), channel_id=1, source_target_pairs={{0,0},{1,1},{2,2},{3,3},{4,8},{5,9},{6,10},{7,11},{8,4},{9,5},{10,... | collective-permute-start | bytes 393224 | tf_op jit(solution)/shard_map/ppermute | solution.py:290
  303.2 25.8 %collective-permute-start.35 = (bf16[64,1024]{1,0:T(8,128)(2,1)}, bf16[64,1024]{1,0:T(8,128)(2,1)}, u32[]{:S(2)}, u32[]{:S(2)}) collective-permute-start(bf16[64,1024]{1,0:T(8,128)(2,1)} %get-tuple-element.87), channel_id=1, source_target_pairs={{0,2},{1,3},{2,0},{3,1},{4,10},{5,11},{6,8},{7,9},{8,6},{9,7},{10,... | collective-permute-start | bytes 393224 | tf_op jit(solution)/shard_map/ppermute | solution.py:290
  303.2 16.7 %collective-permute-start.66 = (bf16[128,1024]{1,0:T(8,128)(2,1)S(1)}, bf16[128,1024]{1,0:T(8,128)(2,1)S(1)}, u32[]{:S(2)}, u32[]{:S(2)}) collective-permute-start(bf16[128,1024]{1,0:T(8,128)(2,1)S(1)} %bitcast.170), channel_id=1, source_target_pairs={{0,8},{1,9},{2,10},{3,11},{4,12},{5,13},{6,14},{7,15},{8,0},{9,1},... | collective-permute-start | bytes 786440 | tf_op jit(solution)/shard_map/ppermute | solution.py:290
  (92 other events, 827.4 us)

commit v3 on v0

--- a/solution.py
+++ b/solution.py
@@ -1,8 +1,12 @@
+import functools
 import math
 
 import jax
 import jax.numpy as jnp
 from jax import lax
+from jax.experimental import pallas as pl
+from jax.experimental.pallas import tpu as pltpu
+from jax.sharding import Mesh
 from jax.sharding import PartitionSpec as P
 
 HEADS = 16
@@ -41,7 +45,7 @@
     )
 
 
-def local(
+def spread_plan(
     counts,
     coords,
     segment_ids,
@@ -134,20 +138,6 @@
     logits = (
         jnp.dot(hidden2_low, w_dec, preferred_element_type=jnp.float32) + b_dec.astype(jnp.float32)
     ).astype(jnp.bfloat16)
-    regathered = (
-        lax.all_gather(enc_weight, "blk", axis=0, tiled=True),
-        lax.all_gather(qkv_weight, "blk", axis=0, tiled=True),
-        lax.all_gather(out_weight, "blk", axis=0, tiled=True),
-        lax.all_gather(up_weight, "blk", axis=0, tiled=True),
-        lax.all_gather(down_weight, "blk", axis=0, tiled=True),
-        lax.all_gather(dec_weight, "blk", axis=0, tiled=True),
-        lax.all_gather(dec_bias, "blk", axis=0, tiled=True),
-        lax.all_gather(norm1_gain, "blk", axis=0, tiled=True),
-        lax.all_gather(norm1_shift, "blk", axis=0, tiled=True),
-        lax.all_gather(norm2_gain, "blk", axis=0, tiled=True),
-        lax.all_gather(norm2_shift, "blk", axis=0, tiled=True),
-    )
-    w_enc, w_qkv, w_out, w_up, w_down, w_dec = regathered[:6]
     cotangent = logit_grad.reshape(row_count, gene_count)
     grad_dec = inner(hidden2_low, cotangent)
     grad_bias = jnp.sum(cotangent.astype(jnp.float32), axis=0)
@@ -174,13 +164,8 @@
         lax.all_gather(logsum, "blk", axis=1, tiled=True),
         lax.all_gather(delta, "blk", axis=1, tiled=True),
     )
-    piece = (
-        lax.all_gather(key_rows, "blk", axis=1, tiled=True),
-        lax.all_gather(values, "blk", axis=1, tiled=True),
-    )
     seg_part = seg_all
-    incoming = (piece[0], piece[1], seg_part)
-    key_part, value_part, query_seg_part = incoming
+    query_seg_part = seg_part
     query_part = queries
     gradout_part = grad_context
     logsum_part = logsum
@@ -283,37 +268,839 @@
     )
 
 
+AXES = ("y", "core", "z", "x")
+SPLIT = 64
+
+
+class Place:
+    def __init__(self, sizes):
+        self.sizes = sizes
+        self.y, self.core, self.z, self.x = (lax.axis_index(name) for name in AXES)
+
+    def send(self, value, move):
+        ny, nc, nz, nx = self.sizes
+
+        def flat(place):
+            y, c, z, x = place
+            return ((y * nc + c) * nz + z) * nx + x
+
+        everywhere = [
+            (y, c, z, x) for y in range(ny) for c in range(nc) for z in range(nz) for x in range(nx)
+        ]
+        return lax.ppermute(value, AXES, [(flat(p), flat(move(*p))) for p in everywhere])
+
+    def swap_core(self, value):
+        return self.send(value, lambda y, c, z, x: (y, 1 - c, z, x))
+
+    def swap_x(self, value):
+        return self.send(value, lambda y, c, z, x: (y, c, z, 1 - x))
+
+    def swap_y(self, value):
+        return self.send(value, lambda y, c, z, x: (1 - y, c, z, x))
+
+    def shift_z(self, value, step):
+        nz = self.sizes[2]
+        return self.send(value, lambda y, c, z, x: (y, c, (z + step) % nz, x))
+
+    def swap_z(self, value, distance):
+        return self.send(value, lambda y, c, z, x: (y, c, z ^ distance, x))
+
+    def exchange_z(self, value):
+        return lax.all_to_all(value, "z", split_axis=0, concat_axis=0, tiled=True)
+
+    def regroup(self, first, second):
+        return (
+            self.send(first, lambda y, c, z, x: (y, z // 2, 2 * c + z % 2, x)),
+            self.send(second, lambda y, c, z, x: (y, z // 2, 2 * c + 1 - z % 2, x)),
+        )
+
+    def by_parity(self, pair):
+        even = self.z % 2 == 0
+        return jnp.where(even, pair[0], pair[1]), jnp.where(even, pair[1], pair[0])
+
+
+def after(value, *earlier):
+    return lax.optimization_barrier((value, *earlier))[0]
+
+
+def coordinates():
+    return tuple(lax.axis_index(name) for name in AXES)
+
+
+def put(target, row, column, part):
+    if not isinstance(row, int):
+        row = pl.multiple_of(row, 16)
+    if not isinstance(column, int):
+        column = pl.multiple_of(column, 128)
+    target[pl.ds(row, part.shape[0]), pl.ds(column, part.shape[1])] = part.astype(target.dtype)
+
+
+def rows_at(source, row, count):
+    return source[pl.ds(pl.multiple_of(row, 16), count), :]
+
+
+def own_part(group, core, x, head):
+    pair = jnp.where(x == 0, group[:, : 2 * head], group[:, 2 * head :])
+    return jnp.where(core == 0, pair[:, :head], pair[:, head:])
+
+
+def dot(left, right):
+    return jnp.dot(left, right, preferred_element_type=jnp.float32)
+
+
+def soft(queries, keys, allowed, scaling):
+    scores = times_t(queries, keys) * scaling
+    scores = jnp.where(allowed, scores, NEGATIVE)
+    expo = jnp.exp(scores - jnp.max(scores, axis=-1, keepdims=True))
+    return expo / jnp.sum(expo, axis=-1, keepdims=True)
+
+
+def one_head(ref, part, heads, number, size):
+    at = (part * heads + number) * size
+    return ref[:, at : at + size]
+
+
+def in_vmem(kernel, outs, *operands, flops=0, exps=0, scratch=()):
+    whole = pl.BlockSpec(memory_space=pltpu.VMEM)
+    shapes = [jax.ShapeDtypeStruct(shape, dtype) for shape, dtype in outs]
+    held = sum(math.prod(v.shape) * v.dtype.itemsize for v in (*operands, *shapes))
+    kept = sum(math.prod(shape) * jnp.dtype(dtype).itemsize for shape, dtype in scratch)
+    results = pl.pallas_call(
+        kernel,
+        out_shape=shapes,
+        in_specs=[whole] * len(operands),
+        out_specs=[whole] * len(shapes),
+        scratch_shapes=[pltpu.VMEM(shape, dtype) for shape, dtype in scratch],
+        compiler_params=pltpu.CompilerParams(
+            vmem_limit_bytes=(held // 2 if flops else held) + kept + (8 if flops else 4) * 1024 * 1024
+        ),
+        cost_estimate=pl.CostEstimate(flops=0, bytes_accessed=1024, transcendentals=0),
+    )(*operands)
+    return results if len(shapes) > 1 else results[0]
+
+
+def sinusoids_of_whole(coords, width):
+    quarter = width // 4
+    frequency = jnp.exp(jnp.arange(quarter, dtype=jnp.float32) * (-math.log(10000.0) / quarter))
+    number = jnp.arange(32, dtype=jnp.float32)[:, None]
+    far, near = 32.0 * number * frequency, number * frequency
+    far = jnp.concatenate([jnp.sin(far), jnp.cos(far)], axis=1)
+    near = jnp.concatenate([jnp.sin(near), jnp.cos(near)], axis=1)
+    parts = []
+    for coord in coords:
+        whole = coord.astype(jnp.int32)
+        pick_far = (whole // 32 == jnp.arange(32)[None, :]).astype(jnp.float32)
+        pick_near = (whole % 32 == jnp.arange(32)[None, :]).astype(jnp.float32)
+        at_far = jnp.dot(pick_far, far, precision=lax.Precision.HIGHEST)
+        at_near = jnp.dot(pick_near, near, precision=lax.Precision.HIGHEST)
+        sin_far, cos_far = at_far[:, :quarter], at_far[:, quarter:]
+        sin_near, cos_near = at_near[:, :quarter], at_near[:, quarter:]
+        parts.append(sin_far * cos_near + cos_far * sin_near)
+        parts.append(cos_far * cos_near - sin_far * sin_near)
+    return jnp.concatenate(parts, axis=1)
+
+
+def normalise(inputs):
+    centre = inputs - jnp.mean(inputs, axis=-1, keepdims=True)
+    factor = lax.rsqrt(jnp.mean(centre * centre, axis=-1, keepdims=True) + EPSILON)
+    return centre * factor, factor
+
+
+def normalise_back(inputs, grad, gain):
+    normal, factor = normalise(inputs)
+    scaled = grad * gain
+    inside = (
+        scaled
+        - jnp.mean(scaled, axis=-1, keepdims=True)
+        - normal * jnp.mean(scaled * normal, axis=-1, keepdims=True)
+    )
+    return (
+        factor * inside,
+        jnp.sum(grad * normal, axis=0, keepdims=True),
+        jnp.sum(grad, axis=0, keepdims=True),
+    )
+
+
+def gelu_parts(value):
+    root = math.sqrt(2.0 / math.pi)
+    square = value * value
+    bent = jnp.tanh(root * value * (1.0 + 0.044715 * square))
+    slope = 0.5 * (1.0 + bent) + 0.5 * value * (1.0 - bent * bent) * root * (1.0 + 0.134145 * square)
+    return 0.5 * value * (1.0 + bent), slope
+
+
+def grouped_plan(
+    sizes,
+    counts,
+    coords,
+    segment_ids,
+    logit_grad,
+    enc_weight,
+    qkv_weight,
+    out_weight,
+    up_weight,
+    down_weight,
+    dec_weight,
+    dec_bias,
+    norm1_gain,
+    norm1_shift,
+    norm2_gain,
+    norm2_shift,
+):
+    place = Place(sizes)
+    nz = sizes[2]
+    seqs, cells, genes = counts.shape
+    width = enc_weight.shape[1]
+    block = enc_weight.shape[0]
+    head = width // HEADS
+    heads = HEADS // 4
+    slice_width = width // 4
+    own_rows = seqs * cells
+    rows = 4 * own_rows
+    ff = up_weight.shape[1]
+    ff_slice = ff // 4
+    bf16, f32 = jnp.bfloat16, jnp.float32
+
+    half, quarter = block // 2, block // 4
+    three = 3 * slice_width
+    lanes = ff // (8 * nz)
+    up_half = nz * lanes
+    many = down_weight.shape[0] // 4
+    half_rows = rows // 2
+    pairs = heads * rows * rows
+    square = 2 * rows * width * width // 4
+
+    vectors = jnp.stack([dec_bias, norm1_gain, norm1_shift, norm2_gain, norm2_shift])
+    tall = half + quarter + 16
+
+    def whole_kernel(enc_ref, dec_ref, vectors_ref, out_ref):
+        y, core, _, _ = coordinates()
+        for k in range(nz):
+            at = k * tall
+            put(out_ref, at, 0, rows_at(enc_ref, core * half, half))
+            put(out_ref, at + half, 0, rows_at(dec_ref, core * half + y * quarter, quarter))
+            out_ref[at + half + quarter : at + tall, :] = jnp.zeros((16, width), bf16)
+            out_ref[at + half + quarter : at + half + quarter + 5, :block] = vectors_ref[...]
+
+    whole_own = in_vmem(
+        whole_kernel, [((nz * tall, width), bf16)], enc_weight, dec_weight, vectors
+    )
+    whole_near = place.exchange_z(whole_own)
+
+    def up_columns(up_ref, out_ref, first, x):
+        y, core, _, _ = coordinates()
+        for number in range(nz):
+            at = ((2 * number + x) * 2 + core) * 2 + y
+            out_ref[first : first + block, number * lanes : (number + 1) * lanes] = up_ref[
+                :, pl.ds(pl.multiple_of(at * lanes, lanes), lanes)
+            ]
+
+    def qkv_columns(qkv_ref, out_ref, core, x, y):
+        at_rows = pl.ds(pl.multiple_of(y * half, 16), half)
+        for at in range(3 * nz):
+            part = own_part(qkv_ref[at_rows, at * 4 * head : (at + 1) * 4 * head], core, x, head)
+            out_ref[:half, at * head : (at + 1) * head] = part
+
+    def theirs_kernel(qkv_ref, up_ref, out_ref):
+        y, core, _, x = coordinates()
+        qkv_columns(qkv_ref, out_ref, core, 1 - x, y)
+        up_columns(up_ref, out_ref, half, 1 - x)
+        out_ref[half:, up_half:] = jnp.zeros((block, three - up_half), bf16)
+
+    theirs = in_vmem(
+        theirs_kernel, [((half + block, three), bf16)], after(qkv_weight, whole_own), up_weight
+    )
+    theirs = place.swap_x(theirs)
+
+    def qkv_kernel(qkv_ref, theirs_ref, out_weight_ref, out_ref):
+        y, core, _, x = coordinates()
+        qkv_columns(qkv_ref, out_ref, core, x, y)
+        out_ref[half:, :three] = theirs_ref[:half, :]
+        part = rows_at(out_weight_ref, core * half + y * quarter, quarter)
+        for j in range(4):
+            out_ref[j * quarter : (j + 1) * quarter, three:] = part[
+                :, j * slice_width : (j + 1) * slice_width
+            ]
+
+    qkv_own = in_vmem(qkv_kernel, [((block, width), bf16)], qkv_weight, theirs, out_weight)
+    qkv_own = after(qkv_own, whole_near)
+    near = [qkv_own] + [place.shift_z(qkv_own, k) for k in range(1, nz)]
+    qkv_pieces = near + [place.swap_y(part) for part in near]
+
+    def up_kernel(up_ref, theirs_ref, down_ref, out_ref):
+        y, core, _, x = coordinates()
+        up_columns(up_ref, out_ref, 0, x)
+        out_ref[:block, up_half:] = theirs_ref[half:, :up_half]
+        out_ref[block:, :] = rows_at(down_ref, (2 * core + y) * many, many)
+
+    up_own = in_vmem(
+        up_kernel, [((block + many, width), bf16)], up_weight, theirs, down_weight
+    )
+    up_near, up_far = [up_own], [place.swap_y(up_own)]
+    for k in range(1, nz):
+        up_near.append(place.shift_z(after(up_near[-1], up_far[0], near[1]), 1))
+        if k < nz - 1:
+            up_far.append(place.swap_y(up_near[-1]))
+    up_far.append(place.shift_z(up_far[-1], 1))
+
+    whole_far = place.swap_x(after(whole_near, qkv_pieces[nz]))
+
+    express = jnp.log1p(counts.astype(f32)).astype(bf16)
+    numbers = jnp.stack([coords[0], coords[1], segment_ids], axis=-1)
+    beside = jnp.concatenate([numbers // SPLIT, numbers % SPLIT], axis=-1).astype(bf16)
+    beside = jnp.pad(beside, ((0, 0), (0, 0), (0, 122)))
+    pair = place.by_parity(jnp.concatenate([express, logit_grad, beside], axis=-1))
+    near_cells = jnp.concatenate(
+        place.regroup(*(after(part, theirs) for part in pair)), axis=0
+    )
+    near_cells = jnp.concatenate(
+        [near_cells, after(
+                place.swap_x(near_cells), up_far[0], *near[1:], up_near[1], whole_far,
+            )], axis=0
+    )
+    far_cells = place.swap_core(near_cells)
+    beside = jnp.concatenate([near_cells[:, 2 * genes :], far_cells[:, 2 * genes :]], axis=0).astype(f32)
+    beside = beside[:, :3] * SPLIT + beside[:, 3:6]
+    segment = beside[:, 2:3]
+    segment_row = segment.reshape(1, rows)
+    embed = sinusoids_of_whole((beside[:, 0:1], beside[:, 1:2]), width)
+
+
+    def enc_half_kernel(near_ref, far_ref, out_ref, vectors_ref):
+        _, _, _, x = coordinates()
+        for dx, ref in enumerate((near_ref, far_ref)):
+            for k in range(nz):
+                at = k * tall
+                put(out_ref, (2 * k + (x ^ dx)) * half, 0, ref[at : at + half, :])
+                part = ref[at + half + quarter : at + tall, :block]
+                put(vectors_ref, 0, (2 * k + (x ^ dx)) * block, part)
+
+    enc_half, vectors = in_vmem(
+        enc_half_kernel, [((genes // 2, width), bf16), ((16, width), f32)], whole_near, whole_far
+    )
+    enc_far = place.swap_core(enc_half)
+
+    def both_cores(near_ref, far_ref, out_ref):
+        _, core, _, _ = coordinates()
+        for dc, ref in enumerate((near_ref, far_ref)):
+            for k in range(2 * nz):
+                put(out_ref, k * block + (core ^ dc) * half, 0, ref[k * half : (k + 1) * half, :])
+
+    def by_y(out_mine, out_send, value, first):
+        y, _, _, _ = coordinates()
+        for k in range(nz):
+            low = value[:, 2 * k * block : (2 * k + 1) * block]
+            high = value[:, (2 * k + 1) * block : (2 * k + 2) * block]
+            at = slice(first, first + value.shape[0]), slice(k * block, (k + 1) * block)
+            out_mine[at] = jnp.where(y == 0, low, high)
+            out_send[at] = jnp.where(y == 0, high, low)
+
+    def first_kernel(
+        near_ref, far_ref, enc_near_ref, enc_far_ref, embed_ref, vectors_ref,
+        enc_ref, hidden_ref, normed_ref, mine_ref, send_ref,
+    ):
+        both_cores(enc_near_ref, enc_far_ref, enc_ref)
+        for number, ref in enumerate((near_ref, far_ref)):
+            first = number * half_rows
+            hidden = dot(ref[:, :genes], enc_ref[...]) + embed_ref[first : first + half_rows, :]
+            if number == 0:
+                hidden_ref[...] = hidden
+            normal, _ = normalise(hidden)
+            normed = (normal * vectors_ref[1:2, :] + vectors_ref[2:3, :]).astype(bf16)
+            normed_ref[first : first + half_rows, :] = normed
+            by_y(mine_ref, send_ref, normed, first)
+
+    square_bf16, half_bf16 = ((width, width), bf16), ((half_rows, width), bf16)
+    half_f32 = ((half_rows, width), f32)
+    columns_bf16 = ((rows, width // 2), bf16)
+    w_enc, hidden0, normed1, normed1_mine, normed1_send = in_vmem(
+        first_kernel, [square_bf16, half_f32, ((rows, width), bf16), columns_bf16, columns_bf16],
+        near_cells, far_cells, enc_half, enc_far, embed, vectors, flops=4 * square,
+    )
+
+    def attend_kernel(normed_ref, *refs):
+        pieces, refs = refs[: 2 * nz], refs[2 * nz :]
+        column_ref, row_ref, w_ref, w_out_ref, qkv_ref, out_ref, own_ref, send_ref = refs
+        y, _, z, x = coordinates()
+        for dy in range(2):
+            for k in range(nz):
+                ref = pieces[dy * nz + k]
+                there = (z - k) % nz
+                for dx in range(2):
+                    row = (2 * there + (x ^ dx)) * block + (y ^ dy) * half
+                    put(w_ref, row, 0, ref[dx * half : (dx + 1) * half, :three])
+                for j in range(4):
+                    row = there * half + (y ^ dy) * quarter
+                    part = ref[j * quarter : (j + 1) * quarter, three:]
+                    put(w_out_ref, row, j * slice_width, part)
+        qkv_ref[...] = dot(normed_ref[...], w_ref[...]).astype(bf16)
+        allowed = column_ref[...] == row_ref[...]
+        for number in range(heads):
+            queries, keys, values = (one_head(qkv_ref, i, heads, number, head) for i in range(3))
+            probs = soft(queries, keys, allowed, head**-0.5)
+            at = slice(number * head, (number + 1) * head)
+            out_ref[:, at] = dot(probs.astype(bf16), values).astype(bf16)
+        own_ref[...] = dot(out_ref[:half_rows, :], w_out_ref[...])
+        send_ref[...] = dot(out_ref[half_rows:, :], w_out_ref[...]).astype(bf16)
+
+    w_qkv, w_out, qkv, context, own, send = in_vmem(
+        attend_kernel,
+        [((width, three), bf16), ((slice_width, width), bf16), ((rows, three), bf16),
+         ((rows, slice_width), bf16), half_f32, half_bf16],
+        after(normed1, up_near[2], up_far[1]), *qkv_pieces, segment, segment_row,
+        flops=4 * square + 4 * pairs * head, exps=pairs,
+    )
+
+    def add_kernel(own_ref, other_ref, out_ref):
+        out_ref[...] = (own_ref[...].astype(f32) + other_ref[...].astype(f32)).astype(out_ref.dtype)
+
+    def add(own, other, dtype=bf16):
+        return in_vmem(add_kernel, [(own.shape, dtype)], own, other)
+
+    def sum_x(mine_ref, other_ref):
+        other = jnp.concatenate([other_ref[own_rows:, :], other_ref[:own_rows, :]], axis=0)
+        return mine_ref[...].astype(f32) + other.astype(f32)
+
+    mine = add(own, after(place.swap_core(send), up_far[1], up_near[3], up_far[2]))
+
+    def second_kernel(hidden_ref, mine_ref, other_ref, vectors_ref, out_ref, normed_ref):
+        hidden = hidden_ref[...] + sum_x(mine_ref, other_ref)
+        out_ref[...] = hidden
+        normal, _ = normalise(hidden)
+        normed_ref[...] = (normal * vectors_ref[3:4, :] + vectors_ref[4:5, :]).astype(bf16)
+
+    hidden1, normed2 = in_vmem(
+        second_kernel, [half_f32, half_bf16],
+        hidden0, mine, after(place.swap_x(mine), up_far[3]), vectors,
+    )
+    normed2_far = place.swap_core(normed2)
+
+    def dec_rows_kernel(near_ref, far_ref, out_ref):
+        for dx, ref in enumerate((near_ref, far_ref)):
+            for k in range(nz):
+                at, out = k * tall + half, (dx * nz + k) * quarter
+                out_ref[out : out + quarter, :] = ref[at : at + quarter, :]
+
+    dec_near = in_vmem(
+        dec_rows_kernel, [((2 * nz * quarter, genes), bf16)], whole_near, after(whole_far, qkv)
+    )
+
+    def dec_half_kernel(near_ref, far_ref, out_ref):
+        y, _, _, x = coordinates()
+        for dy, ref in enumerate((near_ref, far_ref)):
+            for dx in range(2):
+                for k in range(nz):
+                    at = (dx * nz + k) * quarter
+                    row = (2 * k + (x ^ dx)) * half + (y ^ dy) * quarter
+                    put(out_ref, row, 0, ref[at : at + quarter, :])
+
+    dec_half = in_vmem(
+        dec_half_kernel, [((width // 2, genes), bf16)],
+        dec_near, after(place.swap_y(dec_near), mine),
+    )
+    dec_far = place.swap_core(dec_half)
+
+    def decoder_kernel(near_ref, far_ref, dec_near_ref, dec_far_ref, dec_ref, grad_ref, low_ref, sums_ref):
+        both_cores(dec_near_ref, dec_far_ref, dec_ref)
+        grad = times_t(near_ref[:, genes : 2 * genes], dec_ref[...])
+        grad_ref[...] = grad
+        low_ref[:half_rows, :] = grad.astype(bf16)
+        low_ref[half_rows:, :] = times_t(far_ref[:, genes : 2 * genes], dec_ref[...]).astype(bf16)
+        sums_ref[...] = sum(
+            jnp.sum(ref[:, genes : 2 * genes].astype(f32), axis=0, keepdims=True)
+            for ref in (near_ref, far_ref)
+        )
+
+    w_dec, grad_h2, grad_down, bias_sums = in_vmem(
+        decoder_kernel,
+        [square_bf16, half_f32, ((rows, width), bf16), ((1, width), f32)],
+        near_cells, far_cells, dec_half, dec_far, flops=4 * square,
+    )
+
+    def feed_kernel(normed_ref, normed_far_ref, grad_ref, *refs):
+        pieces, refs = refs[: 2 * nz], refs[2 * nz :]
+        active_ref, grad_up_ref, own_ref, send_ref, own2_ref, send2_ref, mine_ref, theirs_ref = refs[:8]
+        w_up_ref, w_down_ref, normed_all, back, ahead = refs[8:]
+        y, _, z, x = coordinates()
+        for dy in range(2):
+            for k in range(nz):
+                ref = pieces[dy * nz + k]
+                there = (z - k) % nz
+                for dx in range(2):
+                    for number in range(nz):
+                        at = dx * up_half + number * lanes
+                        column = (2 * number + (y ^ dy)) * lanes
+                        put(w_up_ref, (2 * there + (x ^ dx)) * block, column, ref[:block, at : at + lanes])
+                put(w_down_ref, (2 * there + (y ^ dy)) * many, 0, ref[block:, :])
+        normed_all[:half_rows, :] = normed_ref[...]
+        normed_all[half_rows:, :] = normed_far_ref[...]
+        by_y(mine_ref, theirs_ref, normed_ref[...], 0)
+        by_y(mine_ref, theirs_ref, normed_far_ref[...], half_rows)
+        chunk = 2 * lanes
+        for number in range(nz):
+            at = slice(number * chunk, (number + 1) * chunk)
+            active, slope = gelu_parts(dot(normed_all[...], w_up_ref[:, at]))
+            active = active.astype(bf16)
+            active_ref[:, at] = active
+            grad_up = (times_t(grad_ref[...], w_down_ref[at, :]) * slope).astype(bf16)
+            grad_up_ref[:, at] = grad_up
+            part, part2 = times_t(grad_up, w_up_ref[:, at]), dot(active, w_down_ref[at, :])
+            back[...] = part if number == 0 else back[...] + part
+            ahead[...] = part2 if number == 0 else ahead[...] + part2
+        for sums, one, two in ((back, own_ref, send_ref), (ahead, own2_ref, send2_ref)):
+            one[...] = sums[:half_rows, :]
+            two[...] = sums[half_rows:, :].astype(bf16)
+
+    full_bf16, full_f32 = ((rows, width), bf16), ((rows, width), f32)
+    active, grad_up, own, send, own2, send2, normed2_mine, normed2_send = in_vmem(
+        feed_kernel,
+        [full_bf16, full_bf16, half_f32, half_bf16, half_f32, half_bf16, columns_bf16, columns_bf16],
+        normed2, normed2_far, grad_down, *up_near, *up_far,
+        flops=16 * square, exps=rows * ff_slice,
+        scratch=[square_bf16, square_bf16, full_bf16, full_f32, full_f32],
+    )
+    mine = add(own, place.swap_core(send))
+
+    def down_halve_kernel(value_ref, *refs):
+        _, _, z, _ = coordinates()
+        for number in range(2):
+            for ref, low in ((refs[2 * number], z % 2), (refs[2 * number + 1], 1 - z % 2)):
+                for high in range(2):
+                    part = rows_at(value_ref, ((2 * high + low) * 2 + number) * many, many)
+                    ref[high * many : (high + 1) * many, :] = part
+
+    def sum_halve_kernel(*refs):
+        parts, (out_ref, send_ref, all_ref) = refs[:-3], refs[-3:]
+        at = 0
+        for ref in parts[1:]:
+            rows_here = slice(at, at + ref.shape[0])
+            all_ref[rows_here, :] = parts[0][rows_here, :].astype(f32) + ref[...].astype(f32)
+            at += ref.shape[0]
+        _, _, z, _ = coordinates()
+        count = out_ref.shape[0] // 2
+        for high in range(2):
+            at = slice(high * count, (high + 1) * count)
+            out_ref[at, :] = rows_at(all_ref, (2 * high + z % 2) * count, count).astype(bf16)
+            send_ref[at, :] = rows_at(all_ref, (2 * high + 1 - z % 2) * count, count).astype(bf16)
+
+    def sum_halve(own, *others):
+        shape = ((own.shape[0] // 2, own.shape[1]), bf16)
+        return in_vmem(
+            sum_halve_kernel, [shape, shape], own, *others, scratch=[(own.shape, f32)]
+        )
+
+    def add_split_kernel(own_ref, other_ref, out_ref, send_ref):
+        _, _, z, _ = coordinates()
+        count = out_ref.shape[0]
+        for ref, part in ((out_ref, z // 2), (send_ref, 1 - z // 2)):
+            own, other = (rows_at(r, part * count, count).astype(f32) for r in (own_ref, other_ref))
+            ref[...] = (own + other).astype(bf16)
+
+    def add_halve(own, other):
+        shape = ((own.shape[0] // 2, own.shape[1]), bf16)
+        return in_vmem(add_split_kernel, [shape, shape], own, other)
+
+    down_one = in_vmem(
+        down_halve_kernel, [((2 * many, width), bf16)] * 4, inner(active, grad_down).astype(bf16)
+    )
+    down_one = [down_one[:2], down_one[2:]]
+    down_other = place.swap_z(down_one[0][1], 1)
+    up_mine = inner(after(normed2_mine, mine), grad_up).astype(bf16)
+    up_send = inner(after(normed2_send, mine), grad_up).astype(bf16)
+    low_rows = nz * block // 2
+    up_other_low = place.swap_y(up_send[:low_rows])
+    ahead = add(own2, after(place.swap_core(send2), mine))
+    other = after(place.swap_x(mine), up_mine, up_send, ahead, up_other_low, down_other)
+    up_other_high = place.swap_y(after(up_send[low_rows:], other))
+    down_two = [add_halve(down_one[0][0], after(down_other, other))]
+    down_two_other = place.swap_z(down_two[0][1], 2)
+    down_other = place.swap_z(after(down_one[1][1], other), 1)
+
+    def back_kernel(hidden_ref, mine_ref, other_ref, grad_ref, vectors_ref, out_ref, low_ref, row):
+        inside, gain_sums, shift_sums = normalise_back(
+            hidden_ref[...], sum_x(mine_ref, other_ref), vectors_ref[row : row + 1, :]
+        )
+        grad = grad_ref[...] + inside
+        if out_ref is not None:
+            out_ref[...] = grad
+        low_ref[:half_rows, :] = grad.astype(bf16)
+        low_ref[half_rows:, :] = jnp.zeros((16, width), bf16)
+        low_ref[half_rows : half_rows + 1, :] = gain_sums.astype(bf16)
+        low_ref[half_rows + 1 : half_rows + 2, :] = shift_sums.astype(bf16)
+
+    def second_back_kernel(*refs):
+        back_kernel(*refs, 3)
+
+    def first_back_kernel(*refs):
+        back_kernel(*refs[:5], None, refs[5], 1)
+
+    message = ((half_rows + 16, width), bf16)
+    grad_h1, near_two = in_vmem(
+        second_back_kernel, [half_f32, message], hidden1, mine, other, grad_h2, vectors
+    )
+    far_two = place.swap_core(near_two)
+    ahead_other = place.swap_x(after(ahead, other))
+
+    def attend_back_kernel(
+        near_ref, far_ref, w_out_ref, qkv_ref, column_ref, row_ref, w_ref,
+        out_ref, own_ref, send_ref, all_ref, grad_ref,
+    ):
+        all_ref[:half_rows, :] = near_ref[:half_rows, :]
+        all_ref[half_rows:, :] = far_ref[:half_rows, :]
+        grad_ref[...] = times_t(all_ref[...], w_out_ref[...]).astype(bf16)
+        allowed = column_ref[...] == row_ref[...]
+        scaling = head**-0.5
+        for number in range(heads):
+            queries, keys, values = (one_head(qkv_ref, i, heads, number, head) for i in range(3))
+            grad = one_head(grad_ref, 0, heads, number, head)
+            probs = soft(queries, keys, allowed, scaling)
+            weighted = probs * times_t(grad, values)
+            delta = jnp.sum(weighted, axis=-1, keepdims=True)
+            dscore = (weighted - probs * delta).astype(bf16)
+            parts = (
+                dot(dscore, keys) * scaling,
+                inner(dscore, queries) * scaling,
+                inner(probs.astype(bf16), grad),
+            )
+            for i, part in enumerate(parts):
+                at = (i * heads + number) * head
+                out_ref[:, at : at + head] = part.astype(bf16)
+        own_ref[...] = times_t(out_ref[:half_rows, :], w_ref[...])
+        send_ref[...] = times_t(out_ref[half_rows:, :], w_ref[...]).astype(bf16)
+
+    grad_qkv, own, send, grad_attn = in_vmem(
+        attend_back_kernel, [((rows, three), bf16), half_f32, half_bf16, full_bf16],
+        near_two, far_two, w_out, qkv, segment, segment_row, w_qkv,
+        flops=4 * square + 10 * pairs * head, exps=pairs,
+        scratch=[((rows, slice_width), bf16)],
+    )
+    qkv_send = inner(normed1_send, grad_qkv).astype(bf16)
+    qkv_other = place.swap_y(qkv_send)
+    up_one = sum_halve(up_mine, up_other_low, after(up_other_high, grad_qkv))
+    down_two.append(add_halve(down_one[1][0], after(down_other, grad_qkv)))
+    down_sum = [add(down_two[0][0], after(down_two_other, grad_qkv))]
+    mine = add(
+        own, after(
+            place.swap_core(send), qkv_send, up_one[1], ahead_other, down_two[1][1], down_sum[0]
+        ),
+    )
+    other = place.swap_x(mine)
+    down_two_other = place.swap_z(after(down_two[1][1], mine), 2)
+    up_one_other = place.swap_z(up_one[1], 1)
+
+    qkv_mine = inner(normed1_mine, grad_qkv).astype(bf16)
+    grad_w_out = inner(context, grad_attn).astype(bf16)
+
+    def logits_kernel(hidden_ref, mine_ref, other_ref, dec_ref, vectors_ref, one_ref, two_ref, own_ref, send_ref):
+        _, core, _, x = coordinates()
+        hidden = (hidden_ref[...] + sum_x(mine_ref, other_ref)).astype(bf16)
+        logits = (dot(hidden[:own_rows, :], dec_ref[...]) + vectors_ref[0:1, :]).astype(bf16)
+        one_ref[...] = logits[:cells, :]
+        two_ref[...] = logits[cells:, :]
+        for k in range(nz):
+            group = hidden[:, 2 * k * block : (2 * k + 2) * block]
+            at = slice(k * half, (k + 1) * half)
+            own_ref[:, at] = own_part(group, core, x, half)
+            send_ref[:, at] = own_part(group, 1 - core, x, half)
+
+    cells_bf16, part_bf16 = ((cells, genes), bf16), ((half_rows, slice_width), bf16)
+    one, two, hidden2_own, hidden2_send = in_vmem(
+        logits_kernel, [cells_bf16, cells_bf16, part_bf16, part_bf16],
+        hidden1, ahead, after(ahead_other, mine), w_dec, vectors, flops=square,
+    )
+    hidden2_far = place.swap_core(hidden2_send)
+    grad_w_dec = inner(hidden2_own, near_cells[:, genes : 2 * genes])
+    grad_w_dec += inner(hidden2_far, far_cells[:, genes : 2 * genes])
+    grad_w_dec = grad_w_dec.astype(bf16)
+    few_mine = jnp.where(place.y == 0, grad_w_out, grad_w_dec)
+    few_send = jnp.where(place.y == 0, grad_w_dec, grad_w_out)
+    few_other = place.swap_y(few_send)
+
+    other = after(other, qkv_mine, few_send, qkv_other, up_one_other, down_two_other)
+    qkv_one = sum_halve(qkv_mine, qkv_other)
+    qkv_one_other = place.swap_z(qkv_one[1], 1)
+    up_two = add_halve(up_one[0], after(up_one_other, other))
+    up_two_other = place.swap_z(up_two[1], 2)
+    near_one = in_vmem(first_back_kernel, [message], hidden0, mine, other, grad_h1, vectors)
+    far_one = place.swap_core(near_one)
+    input_grad = times_t(near_one[:own_rows], w_enc).astype(bf16)
+
+    def last_kernel(near_ref, far_ref, one_ref, one_far_ref, two_ref, two_far_ref, bias_ref, *refs):
+        own_ref, send_ref, slice_ref, grad_ref, sums_ref = refs
+        _, core, z, x = coordinates()
+        for number, ref in enumerate((near_ref, far_ref)):
+            for k in range(nz):
+                group = ref[:, 2 * k * block : (2 * k + 2) * block]
+                slice_ref[
+                    number * half_rows : (number + 1) * half_rows, k * half : (k + 1) * half
+                ] = own_part(group, core, x, half)
+        grad_ref[...] = inner(slice_ref[:half_rows, :], one_ref[:half_rows, :]) + inner(
+            slice_ref[half_rows:, :], one_far_ref[:half_rows, :]
+        )
+        sums_ref[...] = jnp.zeros((8, width), f32)
+        sums_ref[0:1, :] = bias_ref[...]
+        at = slice(half_rows, half_rows + 2)
+        sums_ref[1:3, :] = one_ref[at, :].astype(f32) + one_far_ref[at, :].astype(f32)
+        sums_ref[3:5, :] = two_ref[at, :].astype(f32) + two_far_ref[at, :].astype(f32)
+        for ref, low in ((own_ref, z % 2), (send_ref, 1 - z % 2)):
+            ref[...] = jnp.zeros(ref.shape, bf16)
+            for high in range(2):
+                there, first = 2 * high + low, high * (half + 16)
+                ref[first : first + half, :] = rows_at(grad_ref, there * half, half).astype(bf16)
+                column = pl.multiple_of((2 * there + x) * block, block)
+                part = sums_ref[:, pl.ds(column, block)].astype(bf16)
+                ref[first + half : first + half + 8, :block] = part
+
+    last_one = in_vmem(
+        last_kernel, [((2 * (half + 16), width), bf16)] * 2,
+        near_cells, far_cells, near_one, after(far_one, few_other, qkv_one_other, up_two_other),
+        near_two, far_two, bias_sums, flops=square,
+        scratch=[((rows, slice_width), bf16), ((slice_width, width), f32), ((8, width), f32)],
+    )
+    last_one_other = place.swap_z(last_one[1], 1)
+    qkv_two = add_halve(qkv_one[0], after(qkv_one_other, last_one[1]))
+    qkv_two_other = place.swap_z(qkv_two[1], 2)
+    up_sum = add(up_two[0], after(up_two_other, last_one[1]))
+    up_other = place.swap_y(up_sum)
+    down_sum.append(add(down_two[1][0], after(down_two_other, last_one[1])))
+    down_sum = jnp.concatenate(down_sum, axis=0)
+    down_other = place.swap_y(down_sum)
+    few_one = sum_halve(few_mine, after(few_other, last_one[1]))
+    few_one_other = place.swap_z(few_one[1], 1)
+
+    def by_x_kernel(own_ref, other_ref, mine_ref, send_ref):
+        y, _, _, x = coordinates()
+        at = slice(0, mine_ref.shape[0]), slice(0, mine_ref.shape[1])
+        mine_ref[...] = jnp.where(y == x, own_ref[at], other_ref[at])
+        send_ref[...] = jnp.where(y == x, other_ref[at], own_ref[at])
+
+    def by_x(own, other, width):
+        return in_vmem(by_x_kernel, [((block, width), bf16)] * 2, own, other)
+
+    qkv_sum = add(
+        qkv_two[0], after(qkv_two_other, last_one_other, few_one_other, down_other, up_other)
+    )
+    qkv_other = place.swap_y(qkv_sum)
+    up_mine, up_send = by_x(up_sum, up_other, ff_slice)
+    up_both = place.swap_x(up_send)
+    down_sum = add(down_sum, down_other)
+    down_far = place.swap_core(down_sum)
+    last_two = add_halve(last_one[0], after(last_one_other, qkv_sum))
+    last_two_other = place.swap_z(last_two[1], 2)
+    few_two = add_halve(few_one[0], after(few_one_other, qkv_sum))
+    few_two_other = place.swap_z(few_two[1], 2)
+    qkv_other, up_both, down_far, last_two_other, few_two_other, one, two = lax.optimization_barrier(
+        (qkv_other, up_both, down_far, last_two_other, few_two_other, one, two)
+    )
+    logits = place.regroup(one, two)
+    last = add(last_two[0], last_two_other)
+    last_other = place.swap_y(last)
+
+    def last_add_kernel(one_ref, other_ref, out_ref, sums_ref):
+        total = one_ref[...].astype(f32) + other_ref[...].astype(f32)
+        out_ref[...] = total[:half, :].astype(bf16)
+        sums_ref[...] = total[half : half + 8, :block]
+
+    out_enc, sums = in_vmem(
+        last_add_kernel, [((half, width), bf16), ((8, block), f32)], last, last_other
+    )
+
+    def halves_kernel(near_ref, far_ref, out_ref):
+        _, core, _, _ = coordinates()
+        count = near_ref.shape[0]
+        for dc, ref in enumerate((near_ref, far_ref)):
+            put(out_ref, (core ^ dc) * count, 0, ref[...])
+
+    def halves(near, far):
+        return in_vmem(
+            halves_kernel, [((2 * near.shape[0], near.shape[1]), f32)], near, far
+        )
+
+    out_enc = halves(out_enc, place.swap_core(out_enc))
+    out_down = halves(down_sum, down_far)
+
+    up_both = jnp.concatenate([up_mine, up_both], axis=0)
+
+    def up_out_kernel(near_ref, far_ref, out_ref):
+        _, core, _, x = coordinates()
+        for dc, ref in enumerate((near_ref, far_ref)):
+            for dx in range(2):
+                for k in range(nz):
+                    part = ref[dx * block : (dx + 1) * block, 2 * k * lanes : 2 * (k + 1) * lanes]
+                    put(out_ref, 0, ((2 * k + (x ^ dx)) * 2 + (core ^ dc)) * 2 * lanes, part)
+
+    out_up = in_vmem(up_out_kernel, [((block, ff), f32)], up_both, place.swap_core(up_both))
+
+    qkv_mine, qkv_send = by_x(qkv_sum, qkv_other, three)
+    qkv_both = jnp.concatenate([qkv_mine, place.swap_x(qkv_send)], axis=0)
+    few_sum = add(few_two[0], few_two_other)
+    pair = place.regroup(
+        *(after(input_grad[i * cells : (i + 1) * cells], qkv_other) for i in range(2))
+    )
+    input_grad = jnp.stack(place.by_parity(pair))
+    logits = jnp.stack(place.by_parity(logits))
+
+    def few_kernel(own_ref, other_ref, out_ref):
+        y, _, _, _ = coordinates()
+        put(out_ref, y * half, 0, own_ref[...])
+        put(out_ref, (1 - y) * half, 0, other_ref[...])
+
+    few = in_vmem(few_kernel, [((block, genes), bf16)], few_sum, place.swap_y(few_sum))
+
+    def few_out_kernel(near_ref, far_ref, out_ref, dec_ref):
+        _, core, _, _ = coordinates()
+        for dc, ref in enumerate((near_ref, far_ref)):
+            put(out_ref, (core ^ dc) * half, 0, ref[:half, :])
+            put(dec_ref, (core ^ dc) * half, 0, ref[half:, :])
+
+    out_out, out_dec = in_vmem(
+        few_out_kernel, [((block, width), f32), ((block, genes), f32)], few, place.swap_core(few)
+    )
+
+    def qkv_out_kernel(near_ref, far_ref, out_ref):
+        _, core, _, x = coordinates()
+        for dx in range(2):
+            for number in range(3 * nz):
+                at = slice(dx * block, (dx + 1) * block), slice(number * head, (number + 1) * head)
+                near_part, far_part = near_ref[at].astype(f32), far_ref[at].astype(f32)
+                low = jnp.where(core == 0, near_part, far_part)
+                high = jnp.where(core == 0, far_part, near_part)
+                put(
+                    out_ref, 0, number * 4 * head + (x ^ dx) * 2 * head,
+                    jnp.concatenate([low, high], axis=1),
+                )
+
+    out_qkv = in_vmem(
+        qkv_out_kernel, [((block, 3 * width), f32)], qkv_both, place.swap_core(qkv_both)
+    )
+    return (
+        logits, input_grad, out_enc, out_qkv, out_out, out_up, out_down, out_dec,
+        sums[0], sums[1], sums[2], sums[3], sums[4],
+    )
+
+
+IN_SPECS = (
+    ("dp", "blk", None), (None, "dp", "blk"), ("dp", "blk"), ("dp", "blk", None),
+    *[("blk", None)] * 6, *[("blk",)] * 5,
+)
+OUT_SPECS = (("dp", "blk", None), ("dp", "blk", None), *[("blk", None)] * 6, *[("blk",)] * 5)
+
+
 def solution(mesh):
-    in_specs = (
-        P("dp", "blk", None),
-        P(None, "dp", "blk"),
-        P("dp", "blk"),
-        P("dp", "blk", None),
-        P("blk", None),
-        P("blk", None),
-        P("blk", None),
-        P("blk", None),
-        P("blk", None),
-        P("blk", None),
-        P("blk"),
-        P("blk"),
-        P("blk"),
-        P("blk"),
-        P("blk"),
-    )
-    out_specs = (
-        P("dp", "blk", None),
-        P("dp", "blk", None),
-        P("blk", None),
-        P("blk", None),
-        P("blk", None),
-        P("blk", None),
-        P("blk", None),
-        P("blk", None),
-        P("blk"),
-        P("blk"),
-        P("blk"),
-        P("blk"),
-        P("blk"),
-    )
-    return jax.shard_map(local, mesh=mesh, in_specs=in_specs, out_specs=out_specs, check_vma=False)
+    groups, blocks = mesh.shape["dp"], mesh.shape["blk"]
+
+    def run(*args):
+        seqs = args[0].shape[0] // groups
+        if groups == 4 and blocks == 4 * seqs and seqs == 2 and HEADS == 4 * (blocks // 2):
+            sizes = (groups // 2, 2, blocks // 2, 2)
+            fine = Mesh(mesh.devices.reshape(sizes), AXES)
+            names = {"dp": ("y", "core"), "blk": ("z", "x"), None: None}
+            plan = functools.partial(grouped_plan, sizes)
+        else:
+            fine, names, plan = mesh, {"dp": "dp", "blk": "blk", None: None}, spread_plan
+        specs = lambda entries: tuple(P(*[names[axis] for axis in entry]) for entry in entries)
+        return jax.shard_map(
+            plan, mesh=fine, in_specs=specs(IN_SPECS), out_specs=specs(OUT_SPECS), check_vma=False
+        )(*args)
+
+    return run

time: 1980 us -> 316 us (0.16)
  waiting for transfers between devices: 1560 us -> 142 us
  blocking collectives: 189 us -> 0 us
  matrix products: 121 us -> 9.33 us
  starting transfers between devices: 1.47 us -> 86.8 us
  Pallas kernels: 0 us -> 43.8 us
  local copies, waits for them, and re-layouts: 47.6 us -> 18.2 us
  other arithmetic: 32.5 us -> 7.68 us
    reduce_scatter x6 -> x0, waiting for transfers between devices: 980 us -> none  [the longest x1 283 us: local(): lax.psum_scatter(grad_w_up, 'blk', scatter_dimension=0, tiled=True)]
    all_gather x10 -> x0, waiting for transfers between devices: 566 us -> none  [the longest x1 124 us: local(): lax.all_gather(up_weight, 'blk', axis=0, tiled=True)]
    all_gather x8 -> x0, blocking collectives: 147 us -> none  [the longest x1 29.4 us: local(): lax.all_gather(logsum, 'blk', axis=1, tiled=True)]
    ppermute x0 -> x67, waiting for transfers between devices: none -> 133 us  [send(): lax.ppermute(value, AXES, [(flat(p), flat(move(*p))) for p in everywhere])]
    ppermute x0 -> x67, starting transfers between devices: none -> 81.3 us  [send(): lax.ppermute(value, AXES, [(flat(p), flat(move(*p))) for p in everywhere])]
    dot_general x12 -> x4, matrix products: 63.9 us -> 2.47 us  [the longest x2 1.24 us: sinusoids_of_whole(): at_far = jnp.dot(pick_far, far, precision=lax.Precision.HIGHEST)]
    pallas_call x0 -> x47, Pallas kernels: none -> 43.8 us  [in_vmem(): pl.pallas_call(kernel, out_shape=shapes, in_specs=[whole] * len(operands)...]
    dot_general x6 -> x8, matrix products: 34.6 us -> 6.03 us  [inner(): lax.dot_general(left, right, (((0,), (0,)), ((), ())), preferred_element_...]
  transfers between devices with their start and end apart: 17 -> 68, of which waited for: 15 -> 27; matrix products, arithmetic and copies ran while one was open for 9% -> 7% of each run, Pallas kernels for 0% -> 10%
where the time goes in v3:
time: 316 us; the launch traced here: 309 us
  waiting for transfers between devices  142 us (45%)
  starting transfers between devices  86.8 us (27%)
  Pallas kernels  43.8 us (14%)
  local copies, waits for them, and re-layouts  18.2 us (6%)
  matrix products  9.33 us (3%)
  other arithmetic  7.68 us (2%)
    ppermute x67, waiting for transfers between devices, send(): lax.ppermute(value, AXES, [(flat(p), flat(move(*p))) for p in everywhere])  133 us
    ppermute x67, starting transfers between devices, send(): lax.ppermute(value, AXES, [(flat(p), flat(move(*p))) for p in everywhere])  81.3 us
    pallas_call x47, Pallas kernels, in_vmem(): pl.pallas_call(kernel, out_shape=shapes, in_specs=[whole] * len(operands)...  43.8 us
    unnamed x86, local copies, waits for them, and re-layouts  15.6 us
    all_to_all x1, waiting for transfers between devices, exchange_z(): return lax.all_to_all(value, 'z', split_axis=0, concat_axis=0, tiled=True)  8.62 us
  transfers between devices with their start and end apart: 68, of which 27 were waited for; matrix products, arithmetic and copies ran while one was open for 7% of the time, Pallas kernels for 10%

profile of v3, /device:TPU:1, one launch (start us, length us, event | category | flops | bytes accessed | tf_op | source)
XLA Modules:
  0.0 309.4 jit_solution(13496213530519836003)
XLA Ops:
  4.3 5.6 %all-to-all-start = ((bf16[4,112,1024]{2,1,0:T(8,128)(2,1)}), bf16[4,112,1024]{2,1,0:T(8,128)(2,1)S(1)}, u32[]{:S(2)}, u32[]{:S(2)}) async-start(bf16[4,112,1024]{2,1,0:T(8,128)(2,1)} %bitcast.10), calls=%async_computation | async-start | bytes 1835008 | tf_op jit(solution)/shard_map/all_to_all | solution.py:309
  14.7 3.0 collective-permute-done.theirs_ref
  17.8 6.0 %collective-permute-start.1 = (bf16[64,2176]{1,0:T(8,128)(2,1)}, bf16[64,2176]{1,0:T(8,128)(2,1)}, u32[]{:S(2)}, u32[]{:S(2)}) collective-permute-start(bf16[64,2176]{1,0:T(8,128)(2,1)} %get-tuple-element.130), channel_id=1, source_target_pairs={{0,0},{1,1},{2,2},{3,3},{4,8},{5,9},{6,10},{7,11},{8,4},{9,5},{10,... | collective-permute-start | bytes 835592 | tf_op jit(solution)/shard_map/ppermute | solution.py:290
  25.1 8.6 %all-to-all-done = bf16[4,112,1024]{2,1,0:T(8,128)(2,1)S(1)} async-done(((bf16[4,112,1024]{2,1,0:T(8,128)(2,1)}), bf16[4,112,1024]{2,1,0:T(8,128)(2,1)S(1)}, u32[]{:S(2)}, u32[]{:S(2)}) %all-to-all-start) | async-done | bytes 917536 | tf_op jit(solution)/shard_map/all_to_all | solution.py:309
  36.5 2.4 collective-permute-start.5
  46.8 4.9 %collective-permute-start.8 = (bf16[256,1024]{1,0:T(8,128)(2,1)S(1)}, bf16[256,1024]{1,0:T(8,128)(2,1)S(1)}, u32[]{:S(2)}, u32[]{:S(2)}) collective-permute-start(bf16[256,1024]{1,0:T(8,128)(2,1)S(1)} %shard_map.248.refs_0_), channel_id=1, source_target_pairs={{0,2},{1,3},{2,4},{3,5},{4,6},{5,7},{6,0},{7,1},{8,10},{9,11},{10,... | collective-permute-start | bytes 1572872 | tf_op jit(solution)/shard_map/ppermute | solution.py:290
  52.7 3.1 collective-permute-start.7
  57.1 7.1 %collective-permute-done.3 = bf16[128,2176]{1,0:T(8,128)(2,1)S(1)} collective-permute-done((bf16[128,2176]{1,0:T(8,128)(2,1)S(1)}, bf16[128,2176]{1,0:T(8,128)(2,1)S(1)}, u32[]{:S(2)}, u32[]{:S(2)}) %collective-permute-start.3) | collective-permute-done | bytes 557088 | tf_op jit(solution)/shard_map/ppermute | solution.py:290
  64.2 7.2 %collective-permute-done.7.refs_3_ = bf16[128,1024]{1,0:T(8,128)(2,1)S(1)} collective-permute-done((bf16[128,1024]{1,0:T(8,128)(2,1)S(1)}, bf16[128,1024]{1,0:T(8,128)(2,1)S(1)}, u32[]{:S(2)}, u32[]{:S(2)}) %collective-permute-start.7) | collective-permute-done | bytes 262176 | tf_op jit(solution)/shard_map/ppermute | solution.py:290
  71.3 12.6 %collective-permute-done.6.refs_2_ = bf16[128,1024]{1,0:T(8,128)(2,1)S(1)} collective-permute-done((bf16[128,1024]{1,0:T(8,128)(2,1)S(1)}, bf16[128,1024]{1,0:T(8,128)(2,1)S(1)}, u32[]{:S(2)}, u32[]{:S(2)}) %collective-permute-start.6) | collective-permute-done | bytes 262176 | tf_op jit(solution)/shard_map/ppermute | solution.py:290
  87.8 12.1 %collective-permute-done.13.refs_2_ = bf16[256,1024]{1,0:T(8,128)(2,1)S(1)} collective-permute-done((bf16[256,1024]{1,0:T(8,128)(2,1)S(1)}, bf16[256,1024]{1,0:T(8,128)(2,1)S(1)}, u32[]{:S(2)}, u32[]{:S(2)}) %collective-permute-start.13) | collective-permute-done | bytes 524320 | tf_op jit(solution)/shard_map/ppermute | solution.py:290
  111.0 4.3 %collective-permute-done.14.refs_5_ = bf16[256,1024]{1,0:T(8,128)(2,1)S(1)} collective-permute-done((bf16[256,1024]{1,0:T(8,128)(2,1)S(1)}, bf16[256,1024]{1,0:T(8,128)(2,1)S(1)}, u32[]{:S(2)}, u32[]{:S(2)}) %collective-permute-start.14) | collective-permute-done | bytes 524320 | tf_op jit(solution)/shard_map/ppermute | solution.py:290
  116.8 3.9 %shard_map.252 = (bf16[1024,768]{1,0:T(8,128)(2,1)S(1)}, bf16[256,1024]{1,0:T(8,128)(2,1)S(1)}, bf16[512,768]{1,0:T(8,128)(2,1)S(1)}, bf16[512,256]{1,0:T(8,128)...) custom-call(bf16[512,1024]{1,0:T(8,128)(2,1)S(1)} %get-tuple-element.142.normed_ref, ...), custom_call_target="tpu_custom_call" | custom-call | bytes 1024 | tf_op jit(solution)/shard_map/pallas_call | solution.py:368
  122.3 5.6 %collective-permute-done.20.refs_6_ = bf16[256,1024]{1,0:T(8,128)(2,1)S(1)} collective-permute-done((bf16[256,1024]{1,0:T(8,128)(2,1)S(1)}, bf16[256,1024]{1,0:T(8,128)(2,1)S(1)}, u32[]{:S(2)}, u32[]{:S(2)}) %collective-permute-start.20) | collective-permute-done | bytes 524320 | tf_op jit(solution)/shard_map/ppermute | solution.py:290
  129.7 9.4 %collective-permute-done.24.far_ref = bf16[256,1024]{1,0:T(8,128)(2,1)S(1)} collective-permute-done((bf16[256,1024]{1,0:T(8,128)(2,1)S(1)}, bf16[256,1024]{1,0:T(8,128)(2,1)S(1)}, u32[]{:S(2)}, u32[]{:S(2)}) %collective-permute-start.24) | collective-permute-done | bytes 524320 | tf_op jit(solution)/shard_map/ppermute | solution.py:290
  141.6 3.4 %collective-permute-start.23 = (bf16[256,1024]{1,0:T(8,128)(2,1)S(1)}, bf16[256,1024]{1,0:T(8,128)(2,1)S(1)}, u32[]{:S(2)}, u32[]{:S(2)}) collective-permute-start(bf16[256,1024]{1,0:T(8,128)(2,1)S(1)} %get-tuple-element.149.normed_ref), channel_id=1, source_target_pairs={{0,8},{1,9},{2,10},{3,11},{4,12},{5,13},{6,14},{7,15},{8,0},{9,1},... | collective-permute-start | bytes 1572872 | tf_op jit(solution)/shard_map/ppermute | solution.py:290
  147.9 6.3 %shard_map.258 = (bf16[512,1024]{1,0:T(8,128)(2,1)S(1)}, bf16[512,1024]{1,0:T(8,128)(2,1)S(1)}, f32[256,1024]{1,0:T(8,128)S(1)}, bf16[256,1024]{1,0:T(8,128)(2,1...) custom-call(bf16[256,1024]{1,0:T(8,128)(2,1)S(1)} %get-tuple-element, ...), custom_call_target="tpu_custom_call" | custom-call | bytes 1024 | tf_op jit(solution)/shard_map/pallas_call | solution.py:368
  164.6 6.0 %collective-permute-done.30.other_ref = bf16[256,1024]{1,0:T(8,128)(2,1)S(1)} collective-permute-done((bf16[256,1024]{1,0:T(8,128)(2,1)S(1)}, bf16[256,1024]{1,0:T(8,128)(2,1)S(1)}, u32[]{:S(2)}, u32[]{:S(2)}) %collective-permute-start.30) | collective-permute-done | bytes 524320 | tf_op jit(solution)/shard_map/ppermute | solution.py:290
  171.4 2.5 collective-permute-done.29.refs_1_
  181.4 6.9 %shard_map.263 = (bf16[512,768]{1,0:T(8,128)(2,1)S(1)}, f32[256,1024]{1,0:T(8,128)S(1)}, bf16[256,1024]{1,0:T(8,128)(2,1)}, bf16[512,1024]{1,0:T(8,128)(2,1)S(1)}) custom-call(bf16[272,1024]{1,0:T(8,128)(2,1)S(1)} %get-tuple-element.168.near_ref.two_ref, bf16[272,1024]{1,0:T(8,128)(2,1)S(1)} %collective-permute-done.31.far_ref.two_far_ref, ...), custom_call_target="tpu_custom_call" | custom-call | bytes 1024 | tf_op jit(solution)/shard_map/pallas_call | solution.py:368
  192.3 2.9 collective-permute-done.38.other_ref
  213.5 12.6 %collective-permute-done.42.other_ref = bf16[128,1024]{1,0:T(8,128)(2,1)S(1)} collective-permute-done((bf16[128,1024]{1,0:T(8,128)(2,1)S(1)}, bf16[128,1024]{1,0:T(8,128)(2,1)S(1)}, u32[]{:S(2)}, u32[]{:S(2)}) %collective-permute-start.42) | collective-permute-done | bytes 262176 | tf_op jit(solution)/shard_map/ppermute | solution.py:290
  230.6 13.9 %collective-permute-done.33.other_ref = bf16[256,768]{1,0:T(8,128)(2,1)S(1)} collective-permute-done((bf16[256,768]{1,0:T(8,128)(2,1)S(1)}, bf16[256,768]{1,0:T(8,128)(2,1)S(1)}, u32[]{:S(2)}, u32[]{:S(2)}) %collective-permute-start.33) | collective-permute-done | bytes 393248 | tf_op jit(solution)/shard_map/ppermute | solution.py:290
  250.6 7.5 %collective-permute-done.49.other_ref = bf16[256,1024]{1,0:T(8,128)(2,1)S(1)} collective-permute-done((bf16[256,1024]{1,0:T(8,128)(2,1)S(1)}, bf16[256,1024]{1,0:T(8,128)(2,1)S(1)}, u32[]{:S(2)}, u32[]{:S(2)}) %collective-permute-start.49) | collective-permute-done | bytes 524320 | tf_op jit(solution)/shard_map/ppermute | solution.py:290
  258.3 3.9 %collective-permute-start.53 = (bf16[256,1024]{1,0:T(8,128)(2,1)S(1)}, bf16[256,1024]{1,0:T(8,128)(2,1)S(1)}, u32[]{:S(2)}, u32[]{:S(2)}) collective-permute-start(bf16[256,1024]{1,0:T(8,128)(2,1)S(1)} %shard_map.280.near_ref), channel_id=1, source_target_pairs={{0,8},{1,9},{2,10},{3,11},{4,12},{5,13},{6,14},{7,15},{8,0},{9,1},... | collective-permute-start | bytes 1572872 | tf_op jit(solution)/shard_map/ppermute | solution.py:290
  269.6 8.6 %collective-permute-done.55.other_ref = bf16[64,1024]{1,0:T(8,128)(2,1)S(1)} collective-permute-done((bf16[64,1024]{1,0:T(8,128)(2,1)S(1)}, bf16[64,1024]{1,0:T(8,128)(2,1)S(1)}, u32[]{:S(2)}, u32[]{:S(2)}) %collective-permute-start.55) | collective-permute-done | bytes 131104 | tf_op jit(solution)/shard_map/ppermute | solution.py:290
  278.2 3.5 %collective-permute-done.54.other_ref = bf16[80,1024]{1,0:T(8,128)(2,1)S(1)} collective-permute-done((bf16[80,1024]{1,0:T(8,128)(2,1)S(1)}, bf16[80,1024]{1,0:T(8,128)(2,1)S(1)}, u32[]{:S(2)}, u32[]{:S(2)}) %collective-permute-start.54) | collective-permute-done | bytes 163872 | tf_op jit(solution)/shard_map/ppermute | solution.py:290
  281.8 2.5 collective-permute-start.58
  284.3 2.5 collective-permute-start.59
  286.8 3.6 %collective-permute-start.56 = (bf16[64,1024]{1,0:T(8,128)(2,1)S(1)}, bf16[64,1024]{1,0:T(8,128)(2,1)S(1)}, u32[]{:S(2)}, u32[]{:S(2)}) collective-permute-start(bf16[64,1024]{1,0:T(8,128)(2,1)S(1)} %get-tuple-element.226), channel_id=1, source_target_pairs={{0,0},{1,1},{2,2},{3,3},{4,8},{5,9},{6,10},{7,11},{8,4},{9,5},{10,... | collective-permute-start | bytes 393224 | tf_op jit(solution)/shard_map/ppermute | solution.py:290
  293.3 3.0 collective-permute-done.64.other_ref
  298.2 2.9 collective-permute-done.62
  (282 shorter events, 119.2 us)
Async XLA Ops:
  4.3 29.4 %all-to-all-start = ((bf16[4,112,1024]{2,1,0:T(8,128)(2,1)}), bf16[4,112,1024]{2,1,0:T(8,128)(2,1)S(1)}, u32[]{:S(2)}, u32[]{:S(2)}) async-start(bf16[4,112,1024]{2,1,0:T(8,128)(2,1)} %bitcast.10), calls=%async_computation | async-start | bytes 1835008 | tf_op jit(solution)/shard_map/all_to_all | solution.py:309
  17.8 24.3 %collective-permute-start.1 = (bf16[64,2176]{1,0:T(8,128)(2,1)}, bf16[64,2176]{1,0:T(8,128)(2,1)}, u32[]{:S(2)}, u32[]{:S(2)}) collective-permute-start(bf16[64,2176]{1,0:T(8,128)(2,1)} %get-tuple-element.130), channel_id=1, source_target_pairs={{0,0},{1,1},{2,2},{3,3},{4,8},{5,9},{6,10},{7,11},{8,4},{9,5},{10,... | collective-permute-start | bytes 835592 | tf_op jit(solution)/shard_map/ppermute | solution.py:290
  23.8 18.3 %collective-permute-start.2 = (bf16[64,2176]{1,0:T(8,128)(2,1)}, bf16[64,2176]{1,0:T(8,128)(2,1)}, u32[]{:S(2)}, u32[]{:S(2)}) collective-permute-start(bf16[64,2176]{1,0:T(8,128)(2,1)} %get-tuple-element.131), channel_id=1, source_target_pairs={{0,2},{1,3},{2,0},{3,1},{4,10},{5,11},{6,8},{7,9},{8,6},{9,7},{10,... | collective-permute-start | bytes 835592 | tf_op jit(solution)/shard_map/ppermute | solution.py:290
  39.2 44.8 %collective-permute-start.10 = (bf16[448,1024]{1,0:T(8,128)(2,1)S(1)}, bf16[448,1024]{1,0:T(8,128)(2,1)S(1)}, u32[]{:S(2)}, u32[]{:S(2)}) collective-permute-start(bf16[448,1024]{1,0:T(8,128)(2,1)S(1)} %bitcast.50), channel_id=1, source_target_pairs={{0,1},{1,0},{2,3},{3,2},{4,5},{5,4},{6,7},{7,6},{8,9},{9,8},{10,11... | collective-permute-start | bytes 2752520 | tf_op jit(solution)/shard_map/ppermute | solution.py:290
  43.2 21.0 %collective-permute-start.3 = (bf16[128,2176]{1,0:T(8,128)(2,1)S(1)}, bf16[128,2176]{1,0:T(8,128)(2,1)S(1)}, u32[]{:S(2)}, u32[]{:S(2)}) collective-permute-start(bf16[128,2176]{1,0:T(8,128)(2,1)S(1)} %pad_maximum_fusion.1), channel_id=1, source_target_pairs={{0,1},{1,0},{2,3},{3,2},{4,5},{5,4},{6,7},{7,6},{8,9},{9,8},{10,11... | collective-permute-start | bytes 1671176 | tf_op jit(solution)/shard_map/ppermute | solution.py:290
  46.8 37.2 %collective-permute-start.8 = (bf16[256,1024]{1,0:T(8,128)(2,1)S(1)}, bf16[256,1024]{1,0:T(8,128)(2,1)S(1)}, u32[]{:S(2)}, u32[]{:S(2)}) collective-permute-start(bf16[256,1024]{1,0:T(8,128)(2,1)S(1)} %shard_map.248.refs_0_), channel_id=1, source_target_pairs={{0,2},{1,3},{2,4},{3,5},{4,6},{5,7},{6,0},{7,1},{8,10},{9,11},{10,... | collective-permute-start | bytes 1572872 | tf_op jit(solution)/shard_map/ppermute | solution.py:290
  52.7 18.7 %collective-permute-start.7 = (bf16[128,1024]{1,0:T(8,128)(2,1)S(1)}, bf16[128,1024]{1,0:T(8,128)(2,1)S(1)}, u32[]{:S(2)}, u32[]{:S(2)}) collective-permute-start(bf16[128,1024]{1,0:T(8,128)(2,1)S(1)} %shard_map.249.refs_0_), channel_id=1, source_target_pairs={{0,6},{1,7},{2,0},{3,1},{4,2},{5,3},{6,4},{7,5},{8,14},{9,15},{10,... | collective-permute-start | bytes 786440 | tf_op jit(solution)/shard_map/ppermute | solution.py:290
  55.7 28.2 %collective-permute-start.6 = (bf16[128,1024]{1,0:T(8,128)(2,1)S(1)}, bf16[128,1024]{1,0:T(8,128)(2,1)S(1)}, u32[]{:S(2)}, u32[]{:S(2)}) collective-permute-start(bf16[128,1024]{1,0:T(8,128)(2,1)S(1)} %shard_map.249.refs_0_), channel_id=1, source_target_pairs={{0,4},{1,5},{2,6},{3,7},{4,0},{5,1},{6,2},{7,3},{8,12},{9,13},{10,... | collective-permute-start | bytes 786440 | tf_op jit(solution)/shard_map/ppermute | solution.py:290
  84.1 17.1 %collective-permute-start.11 = (bf16[256,2176]{1,0:T(8,128)(2,1)S(1)}, bf16[256,2176]{1,0:T(8,128)(2,1)S(1)}, u32[]{:S(2)}, u32[]{:S(2)}) collective-permute-start(bf16[256,2176]{1,0:T(8,128)(2,1)S(1)} %constant_dynamic-update-slice_fusion.near_ref), channel_id=1, source_target_pairs={{0,8},{1,9},{2,10},{3,11},{4,12},{5,13},{6,14},{7,15},{8,0},{9,1},... | collective-permute-start | bytes 3342344 | tf_op jit(solution)/shard_map/ppermute | solution.py:290
  84.6 15.3 %collective-permute-start.13 = (bf16[256,1024]{1,0:T(8,128)(2,1)S(1)}, bf16[256,1024]{1,0:T(8,128)(2,1)S(1)}, u32[]{:S(2)}, u32[]{:S(2)}) collective-permute-start(bf16[256,1024]{1,0:T(8,128)(2,1)S(1)} %collective-permute-done.8.refs_1_), channel_id=1, source_target_pairs={{0,2},{1,3},{2,4},{3,5},{4,6},{5,7},{6,0},{7,1},{8,10},{9,11},{10,... | collective-permute-start | bytes 1572872 | tf_op jit(solution)/shard_map/ppermute | solution.py:290
  84.9 31.9 %collective-permute-start.17 = (bf16[128,1024]{1,0:T(8,128)(2,1)S(1)}, bf16[128,1024]{1,0:T(8,128)(2,1)S(1)}, u32[]{:S(2)}, u32[]{:S(2)}) collective-permute-start(bf16[128,1024]{1,0:T(8,128)(2,1)S(1)} %collective-permute-done.7.refs_3_), channel_id=1, source_target_pairs={{0,16},{1,17},{2,18},{3,19},{4,20},{5,21},{6,22},{7,23},{8,24},{9,... | collective-permute-start | bytes 786440 | tf_op jit(solution)/shard_map/ppermute | solution.py:290
  86.2 30.6 %collective-permute-start.16 = (bf16[128,1024]{1,0:T(8,128)(2,1)S(1)}, bf16[128,1024]{1,0:T(8,128)(2,1)S(1)}, u32[]{:S(2)}, u32[]{:S(2)}) collective-permute-start(bf16[128,1024]{1,0:T(8,128)(2,1)S(1)} %collective-permute-done.6.refs_2_), channel_id=1, source_target_pairs={{0,16},{1,17},{2,18},{3,19},{4,20},{5,21},{6,22},{7,23},{8,24},{9,... | collective-permute-start | bytes 786440 | tf_op jit(solution)/shard_map/ppermute | solution.py:290
  86.5 30.4 %collective-permute-start.15 = (bf16[128,1024]{1,0:T(8,128)(2,1)S(1)}, bf16[128,1024]{1,0:T(8,128)(2,1)S(1)}, u32[]{:S(2)}, u32[]{:S(2)}) collective-permute-start(bf16[128,1024]{1,0:T(8,128)(2,1)S(1)} %collective-permute-done.5.refs_1_), channel_id=1, source_target_pairs={{0,16},{1,17},{2,18},{3,19},{4,20},{5,21},{6,22},{7,23},{8,24},{9,... | collective-permute-start | bytes 786440 | tf_op jit(solution)/shard_map/ppermute | solution.py:290
  99.9 15.4 %collective-permute-start.14 = (bf16[256,1024]{1,0:T(8,128)(2,1)S(1)}, bf16[256,1024]{1,0:T(8,128)(2,1)S(1)}, u32[]{:S(2)}, u32[]{:S(2)}) collective-permute-start(bf16[256,1024]{1,0:T(8,128)(2,1)S(1)} %collective-permute-done.8.refs_1_), channel_id=1, source_target_pairs={{0,16},{1,17},{2,18},{3,19},{4,20},{5,21},{6,22},{7,23},{8,24},{9,... | collective-permute-start | bytes 1572872 | tf_op jit(solution)/shard_map/ppermute | solution.py:290
  106.5 21.8 %collective-permute-start.19 = (bf16[256,1024]{1,0:T(8,128)(2,1)S(1)}, bf16[256,1024]{1,0:T(8,128)(2,1)S(1)}, u32[]{:S(2)}, u32[]{:S(2)}) collective-permute-start(bf16[256,1024]{1,0:T(8,128)(2,1)S(1)} %collective-permute-done.13.refs_2_), channel_id=1, source_target_pairs={{0,2},{1,3},{2,4},{3,5},{4,6},{5,7},{6,0},{7,1},{8,10},{9,11},{10,... | collective-permute-start | bytes 1572872 | tf_op jit(solution)/shard_map/ppermute | solution.py:290
  122.0 17.1 %collective-permute-start.24 = (bf16[256,1024]{1,0:T(8,128)(2,1)S(1)}, bf16[256,1024]{1,0:T(8,128)(2,1)S(1)}, u32[]{:S(2)}, u32[]{:S(2)}) collective-permute-start(bf16[256,1024]{1,0:T(8,128)(2,1)S(1)} %shard_map.255.near_ref), channel_id=1, source_target_pairs={{0,16},{1,17},{2,18},{3,19},{4,20},{5,21},{6,22},{7,23},{8,24},{9,... | collective-permute-start | bytes 1572872 | tf_op jit(solution)/shard_map/ppermute | solution.py:290
  177.2 19.5 %collective-permute-start.37 = (bf16[256,1024]{1,0:T(8,128)(2,1)}, bf16[256,1024]{1,0:T(8,128)(2,1)}, u32[]{:S(2)}, u32[]{:S(2)}) collective-permute-start(bf16[256,1024]{1,0:T(8,128)(2,1)} %get-tuple-element.183), channel_id=1, source_target_pairs={{0,2},{1,3},{2,0},{3,1},{4,6},{5,7},{6,4},{7,5},{8,10},{9,11},{10,... | collective-permute-start | bytes 1572872 | tf_op jit(solution)/shard_map/ppermute | solution.py:290
  178.0 18.7 %collective-permute-start.35 = (bf16[256,1024]{1,0:T(8,128)(2,1)}, bf16[256,1024]{1,0:T(8,128)(2,1)}, u32[]{:S(2)}, u32[]{:S(2)}) collective-permute-start(bf16[256,1024]{1,0:T(8,128)(2,1)} %get-tuple-element.177), channel_id=1, source_target_pairs={{0,16},{1,17},{2,18},{3,19},{4,20},{5,21},{6,22},{7,23},{8,24},{9,... | collective-permute-start | bytes 1572872 | tf_op jit(solution)/shard_map/ppermute | solution.py:290
  180.0 15.3 %collective-permute-start.38 = (bf16[128,1024]{1,0:T(8,128)(2,1)}, bf16[128,1024]{1,0:T(8,128)(2,1)}, u32[]{:S(2)}, u32[]{:S(2)}) collective-permute-start(bf16[128,1024]{1,0:T(8,128)(2,1)} %get-tuple-element.189), channel_id=1, source_target_pairs={{0,4},{1,5},{2,6},{3,7},{4,0},{5,1},{6,2},{7,3},{8,12},{9,13},{10,... | collective-permute-start | bytes 786440 | tf_op jit(solution)/shard_map/ppermute | solution.py:290
  181.2 25.0 %collective-permute-start.36 = (bf16[256,1024]{1,0:T(8,128)(2,1)}, bf16[256,1024]{1,0:T(8,128)(2,1)}, u32[]{:S(2)}, u32[]{:S(2)}) collective-permute-start(bf16[256,1024]{1,0:T(8,128)(2,1)} %shard_map.260.mine_ref), channel_id=1, source_target_pairs={{0,1},{1,0},{2,3},{3,2},{4,5},{5,4},{6,7},{7,6},{8,9},{9,8},{10,11... | collective-permute-start | bytes 1572872 | tf_op jit(solution)/shard_map/ppermute | solution.py:290
  191.2 15.0 %collective-permute-start.34 = (bf16[256,1024]{1,0:T(8,128)(2,1)}, bf16[256,1024]{1,0:T(8,128)(2,1)}, u32[]{:S(2)}, u32[]{:S(2)}) collective-permute-start(bf16[256,1024]{1,0:T(8,128)(2,1)} %get-tuple-element.176), channel_id=1, source_target_pairs={{0,8},{1,9},{2,10},{3,11},{4,12},{5,13},{6,14},{7,15},{8,0},{9,1},... | collective-permute-start | bytes 1572872 | tf_op jit(solution)/shard_map/ppermute | solution.py:290
  202.5 23.6 %collective-permute-start.32 = (bf16[512,768]{1,0:T(8,128)(2,1)S(1)}, bf16[512,768]{1,0:T(8,128)(2,1)S(1)}, u32[]{:S(2)}, u32[]{:S(2)}) collective-permute-start(bf16[512,768]{1,0:T(8,128)(2,1)S(1)} %convolution_convert_fusion.3), channel_id=1, source_target_pairs={{0,16},{1,17},{2,18},{3,19},{4,20},{5,21},{6,22},{7,23},{8,24},{9,... | collective-permute-start | bytes 2359304 | tf_op jit(solution)/shard_map/ppermute | solution.py:290
  211.3 14.8 %collective-permute-start.39 = (bf16[256,1024]{1,0:T(8,128)(2,1)S(1)}, bf16[256,1024]{1,0:T(8,128)(2,1)S(1)}, u32[]{:S(2)}, u32[]{:S(2)}) collective-permute-start(bf16[256,1024]{1,0:T(8,128)(2,1)S(1)} %shard_map.269.refs_1_), channel_id=1, source_target_pairs={{0,1},{1,0},{2,3},{3,2},{4,5},{5,4},{6,7},{7,6},{8,9},{9,8},{10,11... | collective-permute-start | bytes 1572872 | tf_op jit(solution)/shard_map/ppermute | solution.py:290
  227.0 17.4 %collective-permute-start.43 = (bf16[272,1024]{1,0:T(8,128)(2,1)S(1)}, bf16[272,1024]{1,0:T(8,128)(2,1)S(1)}, u32[]{:S(2)}, u32[]{:S(2)}) collective-permute-start(bf16[272,1024]{1,0:T(8,128)(2,1)S(1)} %shard_map.271.one_ref), channel_id=1, source_target_pairs={{0,8},{1,9},{2,10},{3,11},{4,12},{5,13},{6,14},{7,15},{8,0},{9,1},... | collective-permute-start | bytes 1671176 | tf_op jit(solution)/shard_map/ppermute | solution.py:290
  227.8 16.6 %collective-permute-start.44 = (bf16[256,1024]{1,0:T(8,128)(2,1)S(1)}, bf16[256,1024]{1,0:T(8,128)(2,1)S(1)}, u32[]{:S(2)}, u32[]{:S(2)}) collective-permute-start(bf16[256,1024]{1,0:T(8,128)(2,1)S(1)} %get-tuple-element.256), channel_id=1, source_target_pairs={{0,16},{1,17},{2,18},{3,19},{4,20},{5,21},{6,22},{7,23},{8,24},{9,... | collective-permute-start | bytes 1572872 | tf_op jit(solution)/shard_map/ppermute | solution.py:290
  228.4 16.0 %collective-permute-start.33 = (bf16[256,768]{1,0:T(8,128)(2,1)S(1)}, bf16[256,768]{1,0:T(8,128)(2,1)S(1)}, u32[]{:S(2)}, u32[]{:S(2)}) collective-permute-start(bf16[256,768]{1,0:T(8,128)(2,1)S(1)} %get-tuple-element.174), channel_id=1, source_target_pairs={{0,2},{1,3},{2,0},{3,1},{4,6},{5,7},{6,4},{7,5},{8,10},{9,11},{10,... | collective-permute-start | bytes 1179656 | tf_op jit(solution)/shard_map/ppermute | solution.py:290
  228.6 15.8 %collective-permute-start.45 = (bf16[128,1024]{1,0:T(8,128)(2,1)S(1)}, bf16[128,1024]{1,0:T(8,128)(2,1)S(1)}, u32[]{:S(2)}, u32[]{:S(2)}) collective-permute-start(bf16[128,1024]{1,0:T(8,128)(2,1)S(1)} %get-tuple-element.203), channel_id=1, source_target_pairs={{0,4},{1,5},{2,6},{3,7},{4,0},{5,1},{6,2},{7,3},{8,12},{9,13},{10,... | collective-permute-start | bytes 786440 | tf_op jit(solution)/shard_map/ppermute | solution.py:290
  247.1 18.0 %collective-permute-start.47 = (bf16[160,1024]{1,0:T(8,128)(2,1)S(1)}, bf16[160,1024]{1,0:T(8,128)(2,1)S(1)}, u32[]{:S(2)}, u32[]{:S(2)}) collective-permute-start(bf16[160,1024]{1,0:T(8,128)(2,1)S(1)} %get-tuple-element.206), channel_id=1, source_target_pairs={{0,2},{1,3},{2,0},{3,1},{4,6},{5,7},{6,4},{7,5},{8,10},{9,11},{10,... | collective-permute-start | bytes 983048 | tf_op jit(solution)/shard_map/ppermute | solution.py:290
  248.0 17.1 %collective-permute-start.46 = (bf16[128,768]{1,0:T(8,128)(2,1)S(1)}, bf16[128,768]{1,0:T(8,128)(2,1)S(1)}, u32[]{:S(2)}, u32[]{:S(2)}) collective-permute-start(bf16[128,768]{1,0:T(8,128)(2,1)S(1)} %get-tuple-element.209), channel_id=1, source_target_pairs={{0,4},{1,5},{2,6},{3,7},{4,0},{5,1},{6,2},{7,3},{8,12},{9,13},{10,... | collective-permute-start | bytes 589832 | tf_op jit(solution)/shard_map/ppermute | solution.py:290
  249.4 15.6 %collective-permute-start.48 = (bf16[128,1024]{1,0:T(8,128)(2,1)S(1)}, bf16[128,1024]{1,0:T(8,128)(2,1)S(1)}, u32[]{:S(2)}, u32[]{:S(2)}) collective-permute-start(bf16[128,1024]{1,0:T(8,128)(2,1)S(1)} %get-tuple-element.211), channel_id=1, source_target_pairs={{0,2},{1,3},{2,0},{3,1},{4,6},{5,7},{6,4},{7,5},{8,10},{9,11},{10,... | collective-permute-start | bytes 786440 | tf_op jit(solution)/shard_map/ppermute | solution.py:290
  258.3 23.5 %collective-permute-start.53 = (bf16[256,1024]{1,0:T(8,128)(2,1)S(1)}, bf16[256,1024]{1,0:T(8,128)(2,1)S(1)}, u32[]{:S(2)}, u32[]{:S(2)}) collective-permute-start(bf16[256,1024]{1,0:T(8,128)(2,1)S(1)} %shard_map.280.near_ref), channel_id=1, source_target_pairs={{0,8},{1,9},{2,10},{3,11},{4,12},{5,13},{6,14},{7,15},{8,0},{9,1},... | collective-permute-start | bytes 1572872 | tf_op jit(solution)/shard_map/ppermute | solution.py:290
  265.1 16.6 %collective-permute-start.51 = (bf16[128,768]{1,0:T(8,128)(2,1)S(1)}, bf16[128,768]{1,0:T(8,128)(2,1)S(1)}, u32[]{:S(2)}, u32[]{:S(2)}) collective-permute-start(bf16[128,768]{1,0:T(8,128)(2,1)S(1)} %shard_map.278.own_ref), channel_id=1, source_target_pairs={{0,16},{1,17},{2,18},{3,19},{4,20},{5,21},{6,22},{7,23},{8,24},{9,... | collective-permute-start | bytes 589832 | tf_op jit(solution)/shard_map/ppermute | solution.py:290
  (77 other events, 599.4 us)

commit v4 on v3

--- a/solution.py
+++ b/solution.py
@@ -487,6 +487,14 @@
     )
     whole_near = place.exchange_z(whole_own)
 
+    express = jnp.log1p(counts.astype(f32)).astype(bf16)
+    numbers = jnp.stack([coords[0], coords[1], segment_ids], axis=-1)
+    beside = jnp.concatenate([numbers // SPLIT, numbers % SPLIT], axis=-1).astype(bf16)
+    beside = jnp.pad(beside, ((0, 0), (0, 0), (0, 122)))
+    pair = place.by_parity(
+        jnp.concatenate([express, logit_grad, after(beside, whole_own)], axis=-1)
+    )
+    own_cells = place.regroup(*pair)
     def up_columns(up_ref, out_ref, first, x):
         y, core, _, _ = coordinates()
         for number in range(nz):
@@ -495,42 +503,45 @@
                 :, pl.ds(pl.multiple_of(at * lanes, lanes), lanes)
             ]
 
-    def qkv_columns(qkv_ref, out_ref, core, x, y):
-        at_rows = pl.ds(pl.multiple_of(y * half, 16), half)
+    def qkv_columns(qkv_ref, out_ref, row, core, x, first, count):
         for at in range(3 * nz):
-            part = own_part(qkv_ref[at_rows, at * 4 * head : (at + 1) * 4 * head], core, x, head)
-            out_ref[:half, at * head : (at + 1) * head] = part
+            columns = slice(at * 4 * head, (at + 1) * 4 * head)
+            part = own_part(
+                qkv_ref[pl.ds(pl.multiple_of(first, 16), count), columns], core, x, head
+            )
+            out_ref[row : row + count, at * head : (at + 1) * head] = part
 
     def theirs_kernel(qkv_ref, up_ref, out_ref):
+        _, core, _, x = coordinates()
+        qkv_columns(qkv_ref, out_ref, 0, core, 1 - x, 0, block)
+        up_columns(up_ref, out_ref, block, 1 - x)
+        out_ref[block:, up_half:] = jnp.zeros((block, three - up_half), bf16)
+
+    theirs = in_vmem(
+        theirs_kernel, [((2 * block, three), bf16)], after(qkv_weight, *pair), up_weight
+    )
+    theirs = place.swap_x(theirs)
+
+    def qkv_kernel(qkv_ref, theirs_ref, out_weight_ref, own_ref, other_ref):
         y, core, _, x = coordinates()
-        qkv_columns(qkv_ref, out_ref, core, 1 - x, y)
-        up_columns(up_ref, out_ref, half, 1 - x)
-        out_ref[half:, up_half:] = jnp.zeros((block, three - up_half), bf16)
-
-    theirs = in_vmem(
-        theirs_kernel, [((half + block, three), bf16)], after(qkv_weight, whole_own), up_weight
-    )
-    theirs = place.swap_x(theirs)
-
-    def qkv_kernel(qkv_ref, theirs_ref, out_weight_ref, out_ref):
-        y, core, _, x = coordinates()
-        qkv_columns(qkv_ref, out_ref, core, x, y)
-        out_ref[half:, :three] = theirs_ref[:half, :]
-        part = rows_at(out_weight_ref, core * half + y * quarter, quarter)
-        for j in range(4):
-            out_ref[j * quarter : (j + 1) * quarter, three:] = part[
-                :, j * slice_width : (j + 1) * slice_width
-            ]
-
-    qkv_own = in_vmem(qkv_kernel, [((block, width), bf16)], qkv_weight, theirs, out_weight)
+        for out_ref, there in ((own_ref, y), (other_ref, 1 - y)):
+            qkv_columns(qkv_ref, out_ref, 0, core, x, there * half, half)
+            out_ref[half:, :three] = rows_at(theirs_ref, there * half, half)
+            part = rows_at(out_weight_ref, core * half + there * quarter, quarter)
+            for j in range(4):
+                out_ref[j * quarter : (j + 1) * quarter, three:] = part[
+                    :, j * slice_width : (j + 1) * slice_width
+                ]
+
+    qkv_own, qkv_own_far = in_vmem(
+        qkv_kernel, [((block, width), bf16)] * 2, qkv_weight, theirs, out_weight
+    )
     qkv_own = after(qkv_own, whole_near)
-    near = [qkv_own] + [place.shift_z(qkv_own, k) for k in range(1, nz)]
-    qkv_pieces = near + [place.swap_y(part) for part in near]
 
     def up_kernel(up_ref, theirs_ref, down_ref, out_ref):
         y, core, _, x = coordinates()
         up_columns(up_ref, out_ref, 0, x)
-        out_ref[:block, up_half:] = theirs_ref[half:, :up_half]
+        out_ref[:block, up_half:] = theirs_ref[block:, :up_half]
         out_ref[block:, :] = rows_at(down_ref, (2 * core + y) * many, many)
 
     up_own = in_vmem(
@@ -538,24 +549,28 @@
     )
     up_near, up_far = [up_own], [place.swap_y(up_own)]
     for k in range(1, nz):
-        up_near.append(place.shift_z(after(up_near[-1], up_far[0], near[1]), 1))
+        up_near.append(place.shift_z(after(up_near[-1], whole_near), 1))
         if k < nz - 1:
             up_far.append(place.swap_y(up_near[-1]))
     up_far.append(place.shift_z(up_far[-1], 1))
-
-    whole_far = place.swap_x(after(whole_near, qkv_pieces[nz]))
-
-    express = jnp.log1p(counts.astype(f32)).astype(bf16)
-    numbers = jnp.stack([coords[0], coords[1], segment_ids], axis=-1)
-    beside = jnp.concatenate([numbers // SPLIT, numbers % SPLIT], axis=-1).astype(bf16)
-    beside = jnp.pad(beside, ((0, 0), (0, 0), (0, 122)))
-    pair = place.by_parity(jnp.concatenate([express, logit_grad, beside], axis=-1))
-    near_cells = jnp.concatenate(
-        place.regroup(*(after(part, theirs) for part in pair)), axis=0
-    )
+    near = [qkv_own, place.shift_z(qkv_own, 1)]
+    near += [place.shift_z(after(qkv_own, up_near[1]), k) for k in range(2, nz)]
+
+    def two_kernel(one_ref, two_ref, out_ref):
+        out_ref[:block, :] = one_ref[...]
+        out_ref[block:, :] = two_ref[...]
+
+    far_one = place.swap_y(near[1])
+    far_two = place.swap_y(in_vmem(two_kernel, [((2 * block, width), bf16)], *near[2:]))
+    qkv_pieces = (*near, qkv_own_far, far_one, far_two)
+
+    whole_far = place.swap_x(whole_near)
+
+    near_cells = jnp.concatenate(after(own_cells, near[1]), axis=0)
     near_cells = jnp.concatenate(
         [near_cells, after(
                 place.swap_x(near_cells), up_far[0], *near[1:], up_near[1], whole_far,
+                up_far[1], far_one,
             )], axis=0
     )
     far_cells = place.swap_core(near_cells)
@@ -579,6 +594,8 @@
         enc_half_kernel, [((genes // 2, width), bf16), ((16, width), f32)], whole_near, whole_far
     )
     enc_far = place.swap_core(enc_half)
+
+    b_dec_row = vectors[0:1]
 
     def both_cores(near_ref, far_ref, out_ref):
         _, core, _, _ = coordinates()
@@ -619,20 +636,20 @@
     )
 
     def attend_kernel(normed_ref, *refs):
-        pieces, refs = refs[: 2 * nz], refs[2 * nz :]
+        pieces, refs = refs[: nz + 3], refs[nz + 3 :]
         column_ref, row_ref, w_ref, w_out_ref, qkv_ref, out_ref, own_ref, send_ref = refs
         y, _, z, x = coordinates()
-        for dy in range(2):
-            for k in range(nz):
-                ref = pieces[dy * nz + k]
-                there = (z - k) % nz
-                for dx in range(2):
-                    row = (2 * there + (x ^ dx)) * block + (y ^ dy) * half
-                    put(w_ref, row, 0, ref[dx * half : (dx + 1) * half, :three])
-                for j in range(4):
-                    row = there * half + (y ^ dy) * quarter
-                    part = ref[j * quarter : (j + 1) * quarter, three:]
-                    put(w_out_ref, row, j * slice_width, part)
+        parts = [(0, k, pieces[k], 0) for k in range(nz)]
+        parts += [(1, k, pieces[nz + min(k, 2)], max(k - 2, 0) * block) for k in range(nz)]
+        for dy, k, ref, first in parts:
+            there = (z - k) % nz
+            for dx in range(2):
+                row = (2 * there + (x ^ dx)) * block + (y ^ dy) * half
+                put(w_ref, row, 0, ref[first + dx * half : first + (dx + 1) * half, :three])
+            for j in range(4):
+                row = there * half + (y ^ dy) * quarter
+                part = ref[first + j * quarter : first + (j + 1) * quarter, three:]
+                put(w_out_ref, row, j * slice_width, part)
         qkv_ref[...] = dot(normed_ref[...], w_ref[...]).astype(bf16)
         allowed = column_ref[...] == row_ref[...]
         for number in range(heads):
@@ -647,7 +664,7 @@
         attend_kernel,
         [((width, three), bf16), ((slice_width, width), bf16), ((rows, three), bf16),
          ((rows, slice_width), bf16), half_f32, half_bf16],
-        after(normed1, up_near[2], up_far[1]), *qkv_pieces, segment, segment_row,
+        after(normed1, up_near[2]), *qkv_pieces, segment, segment_row,
         flops=4 * square + 4 * pairs * head, exps=pairs,
     )
 
@@ -661,7 +678,7 @@
         other = jnp.concatenate([other_ref[own_rows:, :], other_ref[:own_rows, :]], axis=0)
         return mine_ref[...].astype(f32) + other.astype(f32)
 
-    mine = add(own, after(place.swap_core(send), up_far[1], up_near[3], up_far[2]))
+    mine = add(own, after(place.swap_core(send), up_near[3], up_far[2]))
 
     def second_kernel(hidden_ref, mine_ref, other_ref, vectors_ref, out_ref, normed_ref):
         hidden = hidden_ref[...] + sum_x(mine_ref, other_ref)
@@ -876,53 +893,64 @@
     )
     qkv_send = inner(normed1_send, grad_qkv).astype(bf16)
     qkv_other = place.swap_y(qkv_send)
-    up_one = sum_halve(up_mine, up_other_low, after(up_other_high, grad_qkv))
-    down_two.append(add_halve(down_one[1][0], after(down_other, grad_qkv)))
-    down_sum = [add(down_two[0][0], after(down_two_other, grad_qkv))]
+    up_other_high, down_other, down_two_other, ahead_other = after(
+        (up_other_high, down_other, down_two_other, ahead_other), grad_qkv
+    )
     mine = add(
-        own, after(
-            place.swap_core(send), qkv_send, up_one[1], ahead_other, down_two[1][1], down_sum[0]
-        ),
-    )
+        own, after(place.swap_core(send), qkv_send, up_other_high, down_other, down_two_other, ahead_other)
+    )
+    up_one = sum_halve(up_mine, up_other_low, after(up_other_high, mine))
+    down_two.append(add_halve(down_one[1][0], after(down_other, mine)))
+    down_sum = [add(down_two[0][0], after(down_two_other, mine))]
     other = place.swap_x(mine)
-    down_two_other = place.swap_z(after(down_two[1][1], mine), 2)
+    down_two_other = place.swap_z(down_two[1][1], 2)
     up_one_other = place.swap_z(up_one[1], 1)
 
     qkv_mine = inner(normed1_mine, grad_qkv).astype(bf16)
     grad_w_out = inner(context, grad_attn).astype(bf16)
 
-    def logits_kernel(hidden_ref, mine_ref, other_ref, dec_ref, vectors_ref, one_ref, two_ref, own_ref, send_ref):
-        _, core, _, x = coordinates()
-        hidden = (hidden_ref[...] + sum_x(mine_ref, other_ref)).astype(bf16)
-        logits = (dot(hidden[:own_rows, :], dec_ref[...]) + vectors_ref[0:1, :]).astype(bf16)
-        one_ref[...] = logits[:cells, :]
-        two_ref[...] = logits[cells:, :]
-        for k in range(nz):
-            group = hidden[:, 2 * k * block : (2 * k + 2) * block]
-            at = slice(k * half, (k + 1) * half)
-            own_ref[:, at] = own_part(group, core, x, half)
-            send_ref[:, at] = own_part(group, 1 - core, x, half)
-
-    cells_bf16, part_bf16 = ((cells, genes), bf16), ((half_rows, slice_width), bf16)
-    one, two, hidden2_own, hidden2_send = in_vmem(
-        logits_kernel, [cells_bf16, cells_bf16, part_bf16, part_bf16],
-        hidden1, ahead, after(ahead_other, mine), w_dec, vectors, flops=square,
-    )
-    hidden2_far = place.swap_core(hidden2_send)
-    grad_w_dec = inner(hidden2_own, near_cells[:, genes : 2 * genes])
-    grad_w_dec += inner(hidden2_far, far_cells[:, genes : 2 * genes])
-    grad_w_dec = grad_w_dec.astype(bf16)
-    few_mine = jnp.where(place.y == 0, grad_w_out, grad_w_dec)
-    few_send = jnp.where(place.y == 0, grad_w_dec, grad_w_out)
-    few_other = place.swap_y(few_send)
-
-    other = after(other, qkv_mine, few_send, qkv_other, up_one_other, down_two_other)
+    other = after(other, qkv_mine, qkv_other, up_one_other, down_two_other)
     qkv_one = sum_halve(qkv_mine, qkv_other)
     qkv_one_other = place.swap_z(qkv_one[1], 1)
     up_two = add_halve(up_one[0], after(up_one_other, other))
     up_two_other = place.swap_z(up_two[1], 2)
     near_one = in_vmem(first_back_kernel, [message], hidden0, mine, other, grad_h1, vectors)
     far_one = place.swap_core(near_one)
+
+    def hidden_kernel(hidden_ref, mine_ref, other_ref, low_ref, own_ref, send_ref):
+        _, core, _, x = coordinates()
+        hidden = (hidden_ref[...] + sum_x(mine_ref, other_ref)).astype(bf16)
+        low_ref[...] = hidden[:own_rows, :]
+        for k in range(nz):
+            group = hidden[:, 2 * k * block : (2 * k + 2) * block]
+            at = slice(k * half, (k + 1) * half)
+            own_ref[:, at] = own_part(group, core, x, half)
+            send_ref[:, at] = own_part(group, 1 - core, x, half)
+
+    part_bf16 = ((half_rows, slice_width), bf16)
+    hidden2, hidden2_own, hidden2_send = in_vmem(
+        hidden_kernel, [((own_rows, width), bf16), part_bf16, part_bf16],
+        hidden1, ahead, after(ahead_other, near_one),
+    )
+    hidden2_far = place.swap_core(hidden2_send)
+
+    def few_rows_kernel(own_ref, far_ref, near_cells_ref, far_cells_ref, out_grad_ref, mine_ref, send_ref):
+        y, _, _, _ = coordinates()
+        columns = slice(genes, 2 * genes)
+        grad = inner(own_ref[...], near_cells_ref[:, columns])
+        grad = (grad + inner(far_ref[...], far_cells_ref[:, columns])).astype(bf16)
+        mine_ref[...] = jnp.where(y == 0, out_grad_ref[...], grad)
+        send_ref[...] = jnp.where(y == 0, grad, out_grad_ref[...])
+
+    few_shape = ((slice_width, genes), bf16)
+    few_mine, few_send = in_vmem(
+        few_rows_kernel, [few_shape, few_shape],
+        hidden2_own, hidden2_far, near_cells, far_cells, grad_w_out, flops=square,
+    )
+    few_other = place.swap_y(few_send)
+    logits = (dot(hidden2, w_dec) + b_dec_row).astype(bf16)
+    one, two = logits[:cells], logits[cells:]
+
     input_grad = times_t(near_one[:own_rows], w_enc).astype(bf16)
 
     def last_kernel(near_ref, far_ref, one_ref, one_far_ref, two_ref, two_far_ref, bias_ref, *refs):
@@ -992,7 +1020,6 @@
     qkv_other, up_both, down_far, last_two_other, few_two_other, one, two = lax.optimization_barrier(
         (qkv_other, up_both, down_far, last_two_other, few_two_other, one, two)
     )
-    logits = place.regroup(one, two)
     last = add(last_two[0], last_two_other)
     last_other = place.swap_y(last)
 
@@ -1017,7 +1044,6 @@
         )
 
     out_enc = halves(out_enc, place.swap_core(out_enc))
-    out_down = halves(down_sum, down_far)
 
     up_both = jnp.concatenate([up_mine, up_both], axis=0)
 
@@ -1029,16 +1055,24 @@
                     part = ref[dx * block : (dx + 1) * block, 2 * k * lanes : 2 * (k + 1) * lanes]
                     put(out_ref, 0, ((2 * k + (x ^ dx)) * 2 + (core ^ dc)) * 2 * lanes, part)
 
-    out_up = in_vmem(up_out_kernel, [((block, ff), f32)], up_both, place.swap_core(up_both))
 
     qkv_mine, qkv_send = by_x(qkv_sum, qkv_other, three)
-    qkv_both = jnp.concatenate([qkv_mine, place.swap_x(qkv_send)], axis=0)
+    qkv_there = place.swap_x(qkv_send)
+    qkv_both = jnp.concatenate([qkv_mine, qkv_there], axis=0)
+    out_down = halves(down_sum, after(down_far, qkv_there))
+    up_far_both = after(place.swap_core(up_both), qkv_there)
+    out_up = in_vmem(up_out_kernel, [((block, ff), f32)], up_both, up_far_both)
     few_sum = add(few_two[0], few_two_other)
     pair = place.regroup(
-        *(after(input_grad[i * cells : (i + 1) * cells], qkv_other) for i in range(2))
-    )
-    input_grad = jnp.stack(place.by_parity(pair))
-    logits = jnp.stack(place.by_parity(logits))
+        *(
+            jnp.concatenate(
+                [part, after(input_grad[i * cells : (i + 1) * cells], qkv_other)], axis=1
+            )
+            for i, part in enumerate((one, two))
+        )
+    )
+    pair = jnp.stack(place.by_parity(pair))
+    logits, input_grad = pair[:, :, :genes], pair[:, :, genes:]
 
     def few_kernel(own_ref, other_ref, out_ref):
         y, _, _, _ = coordinates()

time: 316 us -> 280 us (0.89)
  starting transfers between devices: 86.8 us -> 76.9 us
  local copies, waits for them, and re-layouts: 18.2 us -> 9.07 us
  Pallas kernels: 43.8 us -> 36.5 us
  waiting for transfers between devices: 142 us -> 138 us
    ppermute x67 -> x63, starting transfers between devices: 81.3 us -> 71.4 us  [send(): lax.ppermute(value, AXES, [(flat(p), flat(move(*p))) for p in everywhere])]
    unnamed x86 -> x28, local copies, waits for them, and re-layouts: 15.6 us -> 5.85 us
    pallas_call x47 -> x49, Pallas kernels: 43.8 us -> 36.5 us  [in_vmem(): pl.pallas_call(kernel, out_shape=shapes, in_specs=[whole] * len(operands)...]
    ppermute x67 -> x63, waiting for transfers between devices: 133 us -> 129 us  [send(): lax.ppermute(value, AXES, [(flat(p), flat(move(*p))) for p in everywhere])]
  transfers between devices with their start and end apart: 68 -> 64, of which waited for: 27 -> 26; matrix products, arithmetic and copies ran while one was open for 7% -> 6% of each run, Pallas kernels for 10% -> 9%
where the time goes in v4:
time: 280 us; the launch traced here: 276 us
  waiting for transfers between devices  138 us (49%)
  starting transfers between devices  76.9 us (27%)
  Pallas kernels  36.5 us (13%)
  local copies, waits for them, and re-layouts  9.07 us (3%)
  matrix products  8.16 us (3%)
  other arithmetic  5.06 us (2%)
    ppermute x63, waiting for transfers between devices, send(): lax.ppermute(value, AXES, [(flat(p), flat(move(*p))) for p in everywhere])  129 us
    ppermute x63, starting transfers between devices, send(): lax.ppermute(value, AXES, [(flat(p), flat(move(*p))) for p in everywhere])  71.4 us
    pallas_call x49, Pallas kernels, in_vmem(): pl.pallas_call(kernel, out_shape=shapes, in_specs=[whole] * len(operands)...  36.5 us
    all_to_all x1, waiting for transfers between devices, exchange_z(): return lax.all_to_all(value, 'z', split_axis=0, concat_axis=0, tiled=True)  9.25 us
    unnamed x28, local copies, waits for them, and re-layouts  5.85 us
  transfers between devices with their start and end apart: 64, of which 26 were waited for; matrix products, arithmetic and copies ran while one was open for 6% of the time, Pallas kernels for 9%

profile of v4, /device:TPU:1, one launch (start us, length us, event | category | flops | bytes accessed | tf_op | source)
XLA Modules:
  0.0 275.6 jit_solution(4247151246073503569)
XLA Ops:
  4.3 5.6 %all-to-all-start = ((bf16[4,112,1024]{2,1,0:T(8,128)(2,1)}), bf16[4,112,1024]{2,1,0:T(8,128)(2,1)S(1)}, u32[]{:S(2)}, u32[]{:S(2)}) async-start(bf16[4,112,1024]{2,1,0:T(8,128)(2,1)} %bitcast.10), calls=%async_computation | async-start | bytes 1835008 | tf_op jit(solution)/shard_map/all_to_all | solution.py:309
  14.4 5.7 %collective-permute-start = (bf16[64,2176]{1,0:T(8,128)(2,1)}, bf16[64,2176]{1,0:T(8,128)(2,1)}, u32[]{:S(2)}, u32[]{:S(2)}) collective-permute-start(bf16[64,2176]{1,0:T(8,128)(2,1)} %get-tuple-element.276), channel_id=1, source_target_pairs={{0,0},{1,1},{2,2},{3,3},{4,8},{5,9},{6,10},{7,11},{8,4},{9,5},{10,... | collective-permute-start | bytes 835592 | tf_op jit(solution)/shard_map/ppermute | solution.py:290
  21.1 1.9 collective-permute-done.2.theirs_ref
  24.5 9.2 %all-to-all-done = bf16[4,112,1024]{2,1,0:T(8,128)(2,1)S(1)} async-done(((bf16[4,112,1024]{2,1,0:T(8,128)(2,1)}), bf16[4,112,1024]{2,1,0:T(8,128)(2,1)S(1)}, u32[]{:S(2)}, u32[]{:S(2)}) %all-to-all-start) | async-done | bytes 917536 | tf_op jit(solution)/shard_map/all_to_all | solution.py:309
  33.7 2.4 collective-permute-start.3
  38.8 20.1 %collective-permute-done = bf16[64,2176]{1,0:T(8,128)(2,1)} collective-permute-done((bf16[64,2176]{1,0:T(8,128)(2,1)}, bf16[64,2176]{1,0:T(8,128)(2,1)}, u32[]{:S(2)}, u32[]{:S(2)}) %collective-permute-start) | collective-permute-done | bytes 278560 | tf_op jit(solution)/shard_map/ppermute | solution.py:290
  64.7 4.5 %collective-permute-done.11.refs_5_ = bf16[128,1024]{1,0:T(8,128)(2,1)S(1)} collective-permute-done((bf16[128,1024]{1,0:T(8,128)(2,1)S(1)}, bf16[128,1024]{1,0:T(8,128)(2,1)S(1)}, u32[]{:S(2)}, u32[]{:S(2)}) %collective-permute-start.11) | collective-permute-done | bytes 262176 | tf_op jit(solution)/shard_map/ppermute | solution.py:290
  70.4 4.4 %collective-permute-done.7.one_ref.refs_2_ = bf16[128,1024]{1,0:T(8,128)(2,1)S(1)} collective-permute-done((bf16[128,1024]{1,0:T(8,128)(2,1)S(1)}, bf16[128,1024]{1,0:T(8,128)(2,1)S(1)}, u32[]{:S(2)}, u32[]{:S(2)}) %collective-permute-start.7) | collective-permute-done | bytes 262176 | tf_op jit(solution)/shard_map/ppermute | solution.py:290
  74.8 4.2 %collective-permute-done.8.two_ref.refs_3_ = bf16[128,1024]{1,0:T(8,128)(2,1)S(1)} collective-permute-done((bf16[128,1024]{1,0:T(8,128)(2,1)S(1)}, bf16[128,1024]{1,0:T(8,128)(2,1)S(1)}, u32[]{:S(2)}, u32[]{:S(2)}) %collective-permute-start.8) | collective-permute-done | bytes 262176 | tf_op jit(solution)/shard_map/ppermute | solution.py:290
  79.2 3.5 %collective-permute-start.14 = (bf16[256,1024]{1,0:T(8,128)(2,1)S(1)}, bf16[256,1024]{1,0:T(8,128)(2,1)S(1)}, u32[]{:S(2)}, u32[]{:S(2)}) collective-permute-start(bf16[256,1024]{1,0:T(8,128)(2,1)S(1)} %collective-permute-done.6.refs_1_), channel_id=1, source_target_pairs={{0,2},{1,3},{2,4},{3,5},{4,6},{5,7},{6,0},{7,1},{8,10},{9,11},{10,... | collective-permute-start | bytes 1572872 | tf_op jit(solution)/shard_map/ppermute | solution.py:290
  85.1 11.0 %collective-permute-done.14.refs_2_ = bf16[256,1024]{1,0:T(8,128)(2,1)S(1)} collective-permute-done((bf16[256,1024]{1,0:T(8,128)(2,1)S(1)}, bf16[256,1024]{1,0:T(8,128)(2,1)S(1)}, u32[]{:S(2)}, u32[]{:S(2)}) %collective-permute-start.14) | collective-permute-done | bytes 524320 | tf_op jit(solution)/shard_map/ppermute | solution.py:290
  101.7 2.1 shard_map.251
  104.1 3.9 %shard_map.253 = (bf16[1024,768]{1,0:T(8,128)(2,1)S(1)}, bf16[256,1024]{1,0:T(8,128)(2,1)S(1)}, bf16[512,768]{1,0:T(8,128)(2,1)S(1)}, bf16[512,256]{1,0:T(8,128)...) custom-call(bf16[512,1024]{1,0:T(8,128)(2,1)S(1)} %get-tuple-element.153.normed_ref, ...), custom_call_target="tpu_custom_call" | custom-call | bytes 1024 | tf_op jit(solution)/shard_map/pallas_call | solution.py:368
  112.3 10.7 %collective-permute-done.22.far_ref = bf16[256,1024]{1,0:T(8,128)(2,1)S(1)} collective-permute-done((bf16[256,1024]{1,0:T(8,128)(2,1)S(1)}, bf16[256,1024]{1,0:T(8,128)(2,1)S(1)}, u32[]{:S(2)}, u32[]{:S(2)}) %collective-permute-start.22) | collective-permute-done | bytes 524320 | tf_op jit(solution)/shard_map/ppermute | solution.py:290
  128.3 6.4 %shard_map.259 = (bf16[512,1024]{1,0:T(8,128)(2,1)S(1)}, bf16[512,1024]{1,0:T(8,128)(2,1)S(1)}, f32[256,1024]{1,0:T(8,128)S(1)}, bf16[256,1024]{1,0:T(8,128)(2,1...) custom-call(bf16[256,1024]{1,0:T(8,128)(2,1)S(1)} %get-tuple-element, ...), custom_call_target="tpu_custom_call" | custom-call | bytes 1024 | tf_op jit(solution)/shard_map/pallas_call | solution.py:368
  141.0 8.9 %collective-permute-done.28.other_ref = bf16[256,1024]{1,0:T(8,128)(2,1)S(1)} collective-permute-done((bf16[256,1024]{1,0:T(8,128)(2,1)S(1)}, bf16[256,1024]{1,0:T(8,128)(2,1)S(1)}, u32[]{:S(2)}, u32[]{:S(2)}) %collective-permute-start.28) | collective-permute-done | bytes 524320 | tf_op jit(solution)/shard_map/ppermute | solution.py:290
  150.1 1.8 collective-permute-done.27.refs_1_
  153.2 1.9 collective-permute-start.29
  158.8 6.1 %shard_map.264 = (bf16[512,768]{1,0:T(8,128)(2,1)S(1)}, f32[256,1024]{1,0:T(8,128)S(1)}, bf16[256,1024]{1,0:T(8,128)(2,1)S(1)}, bf16[512,1024]{1,0:T(8,128)(2,1)S(1)}) custom-call(bf16[272,1024]{1,0:T(8,128)(2,1)S(1)} %get-tuple-element.180.near_ref.two_ref, bf16[272,1024]{1,0:T(8,128)(2,1)S(1)} %collective-permute-done.29.far_ref.two_far_ref, ...), custom_call_target="tpu_custom_call" | custom-call | bytes 1024 | tf_op jit(solution)/shard_map/pallas_call | solution.py:368
  166.7 7.2 %collective-permute-done.35.other_ref = bf16[128,1024]{1,0:T(8,128)(2,1)S(1)} collective-permute-done((bf16[128,1024]{1,0:T(8,128)(2,1)S(1)}, bf16[128,1024]{1,0:T(8,128)(2,1)S(1)}, u32[]{:S(2)}, u32[]{:S(2)}) %collective-permute-start.35) | collective-permute-done | bytes 262176 | tf_op jit(solution)/shard_map/ppermute | solution.py:290
  175.6 2.5 collective-permute-start.38
  179.2 12.6 %collective-permute-done.30.refs_1_ = bf16[512,768]{1,0:T(8,128)(2,1)S(1)} collective-permute-done((bf16[512,768]{1,0:T(8,128)(2,1)S(1)}, bf16[512,768]{1,0:T(8,128)(2,1)S(1)}, u32[]{:S(2)}, u32[]{:S(2)}) %collective-permute-start.30) | collective-permute-done | bytes 786464 | tf_op jit(solution)/shard_map/ppermute | solution.py:290
  195.1 2.4 collective-permute-start.40
  204.3 13.3 %collective-permute-done.31.other_ref = bf16[256,768]{1,0:T(8,128)(2,1)S(1)} collective-permute-done((bf16[256,768]{1,0:T(8,128)(2,1)S(1)}, bf16[256,768]{1,0:T(8,128)(2,1)S(1)}, u32[]{:S(2)}, u32[]{:S(2)}) %collective-permute-start.31) | collective-permute-done | bytes 393248 | tf_op jit(solution)/shard_map/ppermute | solution.py:290
  219.8 2.0 collective-permute-start.45
  226.1 5.0 %collective-permute-done.47.other_ref = bf16[256,1024]{1,0:T(8,128)(2,1)S(1)} collective-permute-done((bf16[256,1024]{1,0:T(8,128)(2,1)S(1)}, bf16[256,1024]{1,0:T(8,128)(2,1)S(1)}, u32[]{:S(2)}, u32[]{:S(2)}) %collective-permute-start.47) | collective-permute-done | bytes 524320 | tf_op jit(solution)/shard_map/ppermute | solution.py:290
  231.2 4.1 %collective-permute-start.51 = (bf16[256,1024]{1,0:T(8,128)(2,1)S(1)}, bf16[256,1024]{1,0:T(8,128)(2,1)S(1)}, u32[]{:S(2)}, u32[]{:S(2)}) collective-permute-start(bf16[256,1024]{1,0:T(8,128)(2,1)S(1)} %shard_map.282.near_ref), channel_id=1, source_target_pairs={{0,8},{1,9},{2,10},{3,11},{4,12},{5,13},{6,14},{7,15},{8,0},{9,1},... | collective-permute-start | bytes 1572872 | tf_op jit(solution)/shard_map/ppermute | solution.py:290
  239.4 1.9 collective-permute-start.52
  242.5 12.4 %collective-permute-done.53.other_ref = bf16[64,1024]{1,0:T(8,128)(2,1)S(1)} collective-permute-done((bf16[64,1024]{1,0:T(8,128)(2,1)S(1)}, bf16[64,1024]{1,0:T(8,128)(2,1)S(1)}, u32[]{:S(2)}, u32[]{:S(2)}) %collective-permute-start.53) | collective-permute-done | bytes 131104 | tf_op jit(solution)/shard_map/ppermute | solution.py:290
  254.9 2.8 %collective-permute-start.55 = (bf16[64,2048]{1,0:T(8,128)(2,1)S(1)}, bf16[64,2048]{1,0:T(8,128)(2,1)S(1)}, u32[]{:S(2)}, u32[]{:S(2)}) collective-permute-start(bf16[64,2048]{1,0:T(8,128)(2,1)S(1)} %pad_maximum_fusion.6), channel_id=1, source_target_pairs={{0,2},{1,3},{2,0},{3,1},{4,10},{5,11},{6,8},{7,9},{8,6},{9,7},{10,... | collective-permute-start | bytes 786440 | tf_op jit(solution)/shard_map/ppermute | solution.py:290
  257.8 1.9 collective-permute-start.54
  262.7 3.7 %collective-permute-done.60.other_ref = bf16[64,1024]{1,0:T(8,128)(2,1)S(1)} collective-permute-done((bf16[64,1024]{1,0:T(8,128)(2,1)S(1)}, bf16[64,1024]{1,0:T(8,128)(2,1)S(1)}, u32[]{:S(2)}, u32[]{:S(2)}) %collective-permute-start.60) | collective-permute-done | bytes 131104 | tf_op jit(solution)/shard_map/ppermute | solution.py:290
  (220 shorter events, 87.9 us)
Async XLA Ops:
  4.3 29.4 %all-to-all-start = ((bf16[4,112,1024]{2,1,0:T(8,128)(2,1)}), bf16[4,112,1024]{2,1,0:T(8,128)(2,1)S(1)}, u32[]{:S(2)}, u32[]{:S(2)}) async-start(bf16[4,112,1024]{2,1,0:T(8,128)(2,1)} %bitcast.10), calls=%async_computation | async-start | bytes 1835008 | tf_op jit(solution)/shard_map/all_to_all | solution.py:309
  14.4 44.5 %collective-permute-start = (bf16[64,2176]{1,0:T(8,128)(2,1)}, bf16[64,2176]{1,0:T(8,128)(2,1)}, u32[]{:S(2)}, u32[]{:S(2)}) collective-permute-start(bf16[64,2176]{1,0:T(8,128)(2,1)} %get-tuple-element.276), channel_id=1, source_target_pairs={{0,0},{1,1},{2,2},{3,3},{4,8},{5,9},{6,10},{7,11},{8,4},{9,5},{10,... | collective-permute-start | bytes 835592 | tf_op jit(solution)/shard_map/ppermute | solution.py:290
  20.1 40.1 %collective-permute-start.1 = (bf16[64,2176]{1,0:T(8,128)(2,1)}, bf16[64,2176]{1,0:T(8,128)(2,1)}, u32[]{:S(2)}, u32[]{:S(2)}) collective-permute-start(bf16[64,2176]{1,0:T(8,128)(2,1)} %get-tuple-element.275), channel_id=1, source_target_pairs={{0,2},{1,3},{2,0},{3,1},{4,10},{5,11},{6,8},{7,9},{8,6},{9,7},{10,... | collective-permute-start | bytes 835592 | tf_op jit(solution)/shard_map/ppermute | solution.py:290
  33.7 26.4 %collective-permute-start.3 = (bf16[128,1024]{1,0:T(8,128)(2,1)S(1)}, bf16[128,1024]{1,0:T(8,128)(2,1)S(1)}, u32[]{:S(2)}, u32[]{:S(2)}) collective-permute-start(bf16[128,1024]{1,0:T(8,128)(2,1)S(1)} %get-tuple-element.145.refs_0_), channel_id=1, source_target_pairs={{0,2},{1,3},{2,4},{3,5},{4,6},{5,7},{6,0},{7,1},{8,10},{9,11},{10,... | collective-permute-start | bytes 786440 | tf_op jit(solution)/shard_map/ppermute | solution.py:290
  37.5 25.4 %collective-permute-start.6 = (bf16[256,1024]{1,0:T(8,128)(2,1)S(1)}, bf16[256,1024]{1,0:T(8,128)(2,1)S(1)}, u32[]{:S(2)}, u32[]{:S(2)}) collective-permute-start(bf16[256,1024]{1,0:T(8,128)(2,1)S(1)} %shard_map.249.refs_0_), channel_id=1, source_target_pairs={{0,2},{1,3},{2,4},{3,5},{4,6},{5,7},{6,0},{7,1},{8,10},{9,11},{10,... | collective-permute-start | bytes 1572872 | tf_op jit(solution)/shard_map/ppermute | solution.py:290
  37.5 26.5 %collective-permute-start.5 = (bf16[256,1024]{1,0:T(8,128)(2,1)S(1)}, bf16[256,1024]{1,0:T(8,128)(2,1)S(1)}, u32[]{:S(2)}, u32[]{:S(2)}) collective-permute-start(bf16[256,1024]{1,0:T(8,128)(2,1)S(1)} %shard_map.249.refs_0_), channel_id=1, source_target_pairs={{0,16},{1,17},{2,18},{3,19},{4,20},{5,21},{6,22},{7,23},{8,24},{9,... | collective-permute-start | bytes 1572872 | tf_op jit(solution)/shard_map/ppermute | solution.py:290
  59.0 20.1 %collective-permute-start.9 = (bf16[448,1024]{1,0:T(8,128)(2,1)S(1)}, bf16[448,1024]{1,0:T(8,128)(2,1)S(1)}, u32[]{:S(2)}, u32[]{:S(2)}) collective-permute-start(bf16[448,1024]{1,0:T(8,128)(2,1)S(1)} %bitcast.47), channel_id=1, source_target_pairs={{0,1},{1,0},{2,3},{3,2},{4,5},{5,4},{6,7},{7,6},{8,9},{9,8},{10,11... | collective-permute-start | bytes 2752520 | tf_op jit(solution)/shard_map/ppermute | solution.py:290
  61.3 17.7 %collective-permute-start.4 = (bf16[128,2176]{1,0:T(8,128)(2,1)S(1)}, bf16[128,2176]{1,0:T(8,128)(2,1)S(1)}, u32[]{:S(2)}, u32[]{:S(2)}) collective-permute-start(bf16[128,2176]{1,0:T(8,128)(2,1)S(1)} %pad_maximum_fusion.2), channel_id=1, source_target_pairs={{0,1},{1,0},{2,3},{3,2},{4,5},{5,4},{6,7},{7,6},{8,9},{9,8},{10,11... | collective-permute-start | bytes 1671176 | tf_op jit(solution)/shard_map/ppermute | solution.py:290
  62.8 16.2 %collective-permute-start.10 = (bf16[256,1024]{1,0:T(8,128)(2,1)S(1)}, bf16[256,1024]{1,0:T(8,128)(2,1)S(1)}, u32[]{:S(2)}, u32[]{:S(2)}) collective-permute-start(bf16[256,1024]{1,0:T(8,128)(2,1)S(1)} %collective-permute-done.6.refs_1_), channel_id=1, source_target_pairs={{0,16},{1,17},{2,18},{3,19},{4,20},{5,21},{6,22},{7,23},{8,24},{9,... | collective-permute-start | bytes 1572872 | tf_op jit(solution)/shard_map/ppermute | solution.py:290
  79.1 18.4 %collective-permute-start.12 = (bf16[256,2176]{1,0:T(8,128)(2,1)S(1)}, bf16[256,2176]{1,0:T(8,128)(2,1)S(1)}, u32[]{:S(2)}, u32[]{:S(2)}) collective-permute-start(bf16[256,2176]{1,0:T(8,128)(2,1)S(1)} %constant_dynamic-update-slice_fusion.near_ref.near_cells_ref), channel_id=1, source_target_pairs={{0,8},{1,9},{2,10},{3,11},{4,12},{5,13},{6,14},{7,15},{8,0},{9,1},... | collective-permute-start | bytes 3342344 | tf_op jit(solution)/shard_map/ppermute | solution.py:290
  79.2 16.9 %collective-permute-start.14 = (bf16[256,1024]{1,0:T(8,128)(2,1)S(1)}, bf16[256,1024]{1,0:T(8,128)(2,1)S(1)}, u32[]{:S(2)}, u32[]{:S(2)}) collective-permute-start(bf16[256,1024]{1,0:T(8,128)(2,1)S(1)} %collective-permute-done.6.refs_1_), channel_id=1, source_target_pairs={{0,2},{1,3},{2,4},{3,5},{4,6},{5,7},{6,0},{7,1},{8,10},{9,11},{10,... | collective-permute-start | bytes 1572872 | tf_op jit(solution)/shard_map/ppermute | solution.py:290
  83.0 21.1 %collective-permute-start.15 = (bf16[256,1024]{1,0:T(8,128)(2,1)S(1)}, bf16[256,1024]{1,0:T(8,128)(2,1)S(1)}, u32[]{:S(2)}, u32[]{:S(2)}) collective-permute-start(bf16[256,1024]{1,0:T(8,128)(2,1)S(1)} %shard_map.252), channel_id=1, source_target_pairs={{0,16},{1,17},{2,18},{3,19},{4,20},{5,21},{6,22},{7,23},{8,24},{9,... | collective-permute-start | bytes 1572872 | tf_op jit(solution)/shard_map/ppermute | solution.py:290
  84.4 17.3 %collective-permute-start.13 = (bf16[512,1024]{1,0:T(8,128)(2,1)S(1)}, bf16[512,1024]{1,0:T(8,128)(2,1)S(1)}, u32[]{:S(2)}, u32[]{:S(2)}) collective-permute-start(bf16[512,1024]{1,0:T(8,128)(2,1)S(1)} %get-tuple-element.147.enc_near_ref), channel_id=1, source_target_pairs={{0,8},{1,9},{2,10},{3,11},{4,12},{5,13},{6,14},{7,15},{8,0},{9,1},... | collective-permute-start | bytes 3145736 | tf_op jit(solution)/shard_map/ppermute | solution.py:290
  96.1 14.4 %collective-permute-start.17 = (bf16[256,1024]{1,0:T(8,128)(2,1)S(1)}, bf16[256,1024]{1,0:T(8,128)(2,1)S(1)}, u32[]{:S(2)}, u32[]{:S(2)}) collective-permute-start(bf16[256,1024]{1,0:T(8,128)(2,1)S(1)} %collective-permute-done.14.refs_2_), channel_id=1, source_target_pairs={{0,2},{1,3},{2,4},{3,5},{4,6},{5,7},{6,0},{7,1},{8,10},{9,11},{10,... | collective-permute-start | bytes 1572872 | tf_op jit(solution)/shard_map/ppermute | solution.py:290
  109.8 14.7 %collective-permute-start.20 = (bf16[256,1024]{1,0:T(8,128)(2,1)S(1)}, bf16[256,1024]{1,0:T(8,128)(2,1)S(1)}, u32[]{:S(2)}, u32[]{:S(2)}) collective-permute-start(bf16[256,1024]{1,0:T(8,128)(2,1)S(1)} %collective-permute-done.18.refs_6_), channel_id=1, source_target_pairs={{0,2},{1,3},{2,4},{3,5},{4,6},{5,7},{6,0},{7,1},{8,10},{9,11},{10,... | collective-permute-start | bytes 1572872 | tf_op jit(solution)/shard_map/ppermute | solution.py:290
  155.1 19.2 %collective-permute-start.33 = (bf16[256,1024]{1,0:T(8,128)(2,1)S(1)}, bf16[256,1024]{1,0:T(8,128)(2,1)S(1)}, u32[]{:S(2)}, u32[]{:S(2)}) collective-permute-start(bf16[256,1024]{1,0:T(8,128)(2,1)S(1)} %get-tuple-element.189), channel_id=1, source_target_pairs={{0,16},{1,17},{2,18},{3,19},{4,20},{5,21},{6,22},{7,23},{8,24},{9,... | collective-permute-start | bytes 1572872 | tf_op jit(solution)/shard_map/ppermute | solution.py:290
  155.9 18.8 %collective-permute-start.34 = (bf16[256,1024]{1,0:T(8,128)(2,1)S(1)}, bf16[256,1024]{1,0:T(8,128)(2,1)S(1)}, u32[]{:S(2)}, u32[]{:S(2)}) collective-permute-start(bf16[256,1024]{1,0:T(8,128)(2,1)S(1)} %get-tuple-element.191), channel_id=1, source_target_pairs={{0,2},{1,3},{2,0},{3,1},{4,6},{5,7},{6,4},{7,5},{8,10},{9,11},{10,... | collective-permute-start | bytes 1572872 | tf_op jit(solution)/shard_map/ppermute | solution.py:290
  157.5 16.5 %collective-permute-start.35 = (bf16[128,1024]{1,0:T(8,128)(2,1)S(1)}, bf16[128,1024]{1,0:T(8,128)(2,1)S(1)}, u32[]{:S(2)}, u32[]{:S(2)}) collective-permute-start(bf16[128,1024]{1,0:T(8,128)(2,1)S(1)} %get-tuple-element.194), channel_id=1, source_target_pairs={{0,4},{1,5},{2,6},{3,7},{4,0},{5,1},{6,2},{7,3},{8,12},{9,13},{10,... | collective-permute-start | bytes 786440 | tf_op jit(solution)/shard_map/ppermute | solution.py:290
  158.5 16.2 %collective-permute-start.36 = (bf16[256,1024]{1,0:T(8,128)(2,1)S(1)}, bf16[256,1024]{1,0:T(8,128)(2,1)S(1)}, u32[]{:S(2)}, u32[]{:S(2)}) collective-permute-start(bf16[256,1024]{1,0:T(8,128)(2,1)S(1)} %shard_map.261.mine_ref), channel_id=1, source_target_pairs={{0,1},{1,0},{2,3},{3,2},{4,5},{5,4},{6,7},{7,6},{8,9},{9,8},{10,11... | collective-permute-start | bytes 1572872 | tf_op jit(solution)/shard_map/ppermute | solution.py:290
  173.9 17.9 %collective-permute-start.30 = (bf16[512,768]{1,0:T(8,128)(2,1)S(1)}, bf16[512,768]{1,0:T(8,128)(2,1)S(1)}, u32[]{:S(2)}, u32[]{:S(2)}) collective-permute-start(bf16[512,768]{1,0:T(8,128)(2,1)S(1)} %convolution_convert_fusion.3), channel_id=1, source_target_pairs={{0,16},{1,17},{2,18},{3,19},{4,20},{5,21},{6,22},{7,23},{8,24},{9,... | collective-permute-start | bytes 2359304 | tf_op jit(solution)/shard_map/ppermute | solution.py:290
  174.9 18.4 %collective-permute-start.37 = (bf16[256,1024]{1,0:T(8,128)(2,1)S(1)}, bf16[256,1024]{1,0:T(8,128)(2,1)S(1)}, u32[]{:S(2)}, u32[]{:S(2)}) collective-permute-start(bf16[256,1024]{1,0:T(8,128)(2,1)S(1)} %shard_map.267.refs_1_), channel_id=1, source_target_pairs={{0,1},{1,0},{2,3},{3,2},{4,5},{5,4},{6,7},{7,6},{8,9},{9,8},{10,11... | collective-permute-start | bytes 1572872 | tf_op jit(solution)/shard_map/ppermute | solution.py:290
  175.6 18.7 %collective-permute-start.38 = (bf16[256,1024]{1,0:T(8,128)(2,1)S(1)}, bf16[256,1024]{1,0:T(8,128)(2,1)S(1)}, u32[]{:S(2)}, u32[]{:S(2)}) collective-permute-start(bf16[256,1024]{1,0:T(8,128)(2,1)S(1)} %get-tuple-element.202), channel_id=1, source_target_pairs={{0,2},{1,3},{2,0},{3,1},{4,6},{5,7},{6,4},{7,5},{8,10},{9,11},{10,... | collective-permute-start | bytes 1572872 | tf_op jit(solution)/shard_map/ppermute | solution.py:290
  178.3 15.0 %collective-permute-start.39 = (bf16[128,1024]{1,0:T(8,128)(2,1)S(1)}, bf16[128,1024]{1,0:T(8,128)(2,1)S(1)}, u32[]{:S(2)}, u32[]{:S(2)}) collective-permute-start(bf16[128,1024]{1,0:T(8,128)(2,1)S(1)} %get-tuple-element.205), channel_id=1, source_target_pairs={{0,4},{1,5},{2,6},{3,7},{4,0},{5,1},{6,2},{7,3},{8,12},{9,13},{10,... | collective-permute-start | bytes 786440 | tf_op jit(solution)/shard_map/ppermute | solution.py:290
  195.1 22.5 %collective-permute-start.40 = (bf16[272,1024]{1,0:T(8,128)(2,1)S(1)}, bf16[272,1024]{1,0:T(8,128)(2,1)S(1)}, u32[]{:S(2)}, u32[]{:S(2)}) collective-permute-start(bf16[272,1024]{1,0:T(8,128)(2,1)S(1)} %shard_map.270.one_ref), channel_id=1, source_target_pairs={{0,8},{1,9},{2,10},{3,11},{4,12},{5,13},{6,14},{7,15},{8,0},{9,1},... | collective-permute-start | bytes 1671176 | tf_op jit(solution)/shard_map/ppermute | solution.py:290
  199.9 17.7 %collective-permute-start.42 = (bf16[256,1024]{1,0:T(8,128)(2,1)S(1)}, bf16[256,1024]{1,0:T(8,128)(2,1)S(1)}, u32[]{:S(2)}, u32[]{:S(2)}) collective-permute-start(bf16[256,1024]{1,0:T(8,128)(2,1)S(1)} %get-tuple-element.213), channel_id=1, source_target_pairs={{0,16},{1,17},{2,18},{3,19},{4,20},{5,21},{6,22},{7,23},{8,24},{9,... | collective-permute-start | bytes 1572872 | tf_op jit(solution)/shard_map/ppermute | solution.py:290
  201.6 16.0 %collective-permute-start.31 = (bf16[256,768]{1,0:T(8,128)(2,1)S(1)}, bf16[256,768]{1,0:T(8,128)(2,1)S(1)}, u32[]{:S(2)}, u32[]{:S(2)}) collective-permute-start(bf16[256,768]{1,0:T(8,128)(2,1)S(1)} %get-tuple-element.186), channel_id=1, source_target_pairs={{0,2},{1,3},{2,0},{3,1},{4,6},{5,7},{6,4},{7,5},{8,10},{9,11},{10,... | collective-permute-start | bytes 1179656 | tf_op jit(solution)/shard_map/ppermute | solution.py:290
  219.8 18.3 %collective-permute-start.45 = (bf16[160,1024]{1,0:T(8,128)(2,1)S(1)}, bf16[160,1024]{1,0:T(8,128)(2,1)S(1)}, u32[]{:S(2)}, u32[]{:S(2)}) collective-permute-start(bf16[160,1024]{1,0:T(8,128)(2,1)S(1)} %get-tuple-element.219), channel_id=1, source_target_pairs={{0,2},{1,3},{2,0},{3,1},{4,6},{5,7},{6,4},{7,5},{8,10},{9,11},{10,... | collective-permute-start | bytes 983048 | tf_op jit(solution)/shard_map/ppermute | solution.py:290
  222.1 16.0 %collective-permute-start.46 = (bf16[128,1024]{1,0:T(8,128)(2,1)S(1)}, bf16[128,1024]{1,0:T(8,128)(2,1)S(1)}, u32[]{:S(2)}, u32[]{:S(2)}) collective-permute-start(bf16[128,1024]{1,0:T(8,128)(2,1)S(1)} %get-tuple-element.225), channel_id=1, source_target_pairs={{0,2},{1,3},{2,0},{3,1},{4,6},{5,7},{6,4},{7,5},{8,10},{9,11},{10,... | collective-permute-start | bytes 786440 | tf_op jit(solution)/shard_map/ppermute | solution.py:290
  222.2 14.5 %collective-permute-start.48 = (bf16[128,1024]{1,0:T(8,128)(2,1)S(1)}, bf16[128,1024]{1,0:T(8,128)(2,1)S(1)}, u32[]{:S(2)}, u32[]{:S(2)}) collective-permute-start(bf16[128,1024]{1,0:T(8,128)(2,1)S(1)} %shard_map.279.own_ref), channel_id=1, source_target_pairs={{0,16},{1,17},{2,18},{3,19},{4,20},{5,21},{6,22},{7,23},{8,24},{9,... | collective-permute-start | bytes 786440 | tf_op jit(solution)/shard_map/ppermute | solution.py:290
  231.2 23.6 %collective-permute-start.51 = (bf16[256,1024]{1,0:T(8,128)(2,1)S(1)}, bf16[256,1024]{1,0:T(8,128)(2,1)S(1)}, u32[]{:S(2)}, u32[]{:S(2)}) collective-permute-start(bf16[256,1024]{1,0:T(8,128)(2,1)S(1)} %shard_map.282.near_ref), channel_id=1, source_target_pairs={{0,8},{1,9},{2,10},{3,11},{4,12},{5,13},{6,14},{7,15},{8,0},{9,1},... | collective-permute-start | bytes 1572872 | tf_op jit(solution)/shard_map/ppermute | solution.py:290
  238.1 16.7 %collective-permute-start.49 = (bf16[128,768]{1,0:T(8,128)(2,1)S(1)}, bf16[128,768]{1,0:T(8,128)(2,1)S(1)}, u32[]{:S(2)}, u32[]{:S(2)}) collective-permute-start(bf16[128,768]{1,0:T(8,128)(2,1)S(1)} %shard_map.280.own_ref), channel_id=1, source_target_pairs={{0,16},{1,17},{2,18},{3,19},{4,20},{5,21},{6,22},{7,23},{8,24},{9,... | collective-permute-start | bytes 589832 | tf_op jit(solution)/shard_map/ppermute | solution.py:290
  239.4 15.4 %collective-permute-start.52 = (bf16[80,1024]{1,0:T(8,128)(2,1)S(1)}, bf16[80,1024]{1,0:T(8,128)(2,1)S(1)}, u32[]{:S(2)}, u32[]{:S(2)}) collective-permute-start(bf16[80,1024]{1,0:T(8,128)(2,1)S(1)} %get-tuple-element.236), channel_id=1, source_target_pairs={{0,4},{1,5},{2,6},{3,7},{4,0},{5,1},{6,2},{7,3},{8,12},{9,13},{10,... | collective-permute-start | bytes 491528 | tf_op jit(solution)/shard_map/ppermute | solution.py:290
  (44 other events, 342.3 us)

commit v5 on v4

--- a/solution.py
+++ b/solution.py
@@ -909,7 +909,7 @@
     qkv_mine = inner(normed1_mine, grad_qkv).astype(bf16)
     grad_w_out = inner(context, grad_attn).astype(bf16)
 
-    other = after(other, qkv_mine, qkv_other, up_one_other, down_two_other)
+    other = after(other, qkv_mine, down_two_other)
     qkv_one = sum_halve(qkv_mine, qkv_other)
     qkv_one_other = place.swap_z(qkv_one[1], 1)
     up_two = add_halve(up_one[0], after(up_one_other, other))
@@ -953,7 +953,11 @@
 
     input_grad = times_t(near_one[:own_rows], w_enc).astype(bf16)
 
-    def last_kernel(near_ref, far_ref, one_ref, one_far_ref, two_ref, two_far_ref, bias_ref, *refs):
+    tall_last = 2 * half + 16
+
+    def last_kernel(
+        near_ref, far_ref, one_ref, one_far_ref, two_ref, two_far_ref, bias_ref, few_ref, few_other_ref, *refs
+    ):
         own_ref, send_ref, slice_ref, grad_ref, sums_ref = refs
         _, core, z, x = coordinates()
         for number, ref in enumerate((near_ref, far_ref)):
@@ -973,28 +977,35 @@
         for ref, low in ((own_ref, z % 2), (send_ref, 1 - z % 2)):
             ref[...] = jnp.zeros(ref.shape, bf16)
             for high in range(2):
-                there, first = 2 * high + low, high * (half + 16)
+                there, first = 2 * high + low, high * tall_last
                 ref[first : first + half, :] = rows_at(grad_ref, there * half, half).astype(bf16)
                 column = pl.multiple_of((2 * there + x) * block, block)
                 part = sums_ref[:, pl.ds(column, block)].astype(bf16)
                 ref[first + half : first + half + 8, :block] = part
+                few = [rows_at(r, there * half, half).astype(f32) for r in (few_ref, few_other_ref)]
+                ref[first + half + 16 : first + tall_last, :] = (few[0] + few[1]).astype(bf16)
 
     last_one = in_vmem(
-        last_kernel, [((2 * (half + 16), width), bf16)] * 2,
-        near_cells, far_cells, near_one, after(far_one, few_other, qkv_one_other, up_two_other),
-        near_two, far_two, bias_sums, flops=square,
+        last_kernel, [((2 * tall_last, width), bf16)] * 2,
+        near_cells, far_cells, near_one, after(far_one, qkv_one_other, up_two_other),
+        near_two, far_two, bias_sums, few_mine, few_other, flops=square,
         scratch=[((rows, slice_width), bf16), ((slice_width, width), f32), ((8, width), f32)],
     )
     last_one_other = place.swap_z(last_one[1], 1)
     qkv_two = add_halve(qkv_one[0], after(qkv_one_other, last_one[1]))
     qkv_two_other = place.swap_z(qkv_two[1], 2)
-    up_sum = add(up_two[0], after(up_two_other, last_one[1]))
-    up_other = place.swap_y(up_sum)
-    down_sum.append(add(down_two[1][0], after(down_two_other, last_one[1])))
-    down_sum = jnp.concatenate(down_sum, axis=0)
-    down_other = place.swap_y(down_sum)
-    few_one = sum_halve(few_mine, after(few_other, last_one[1]))
-    few_one_other = place.swap_z(few_one[1], 1)
+
+    def feed_sum_kernel(down_ref, one_ref, one_other_ref, two_ref, two_other_ref, out_ref):
+        out_ref[:many, :] = down_ref[...]
+        for row, ref, other_ref in ((many, one_ref, one_other_ref), (2 * many, two_ref, two_other_ref)):
+            total = ref[...].astype(f32) + other_ref[...].astype(f32)
+            out_ref[row : row + ref.shape[0], :] = total.astype(bf16)
+
+    feed_sum = in_vmem(
+        feed_sum_kernel, [((2 * many + block, width), bf16)],
+        down_sum[0], down_two[1][0], down_two_other, up_two[0], after(up_two_other, last_one[1]),
+    )
+    feed_other = place.swap_y(feed_sum)
 
     def by_x_kernel(own_ref, other_ref, mine_ref, send_ref):
         y, _, _, x = coordinates()
@@ -1005,33 +1016,28 @@
     def by_x(own, other, width):
         return in_vmem(by_x_kernel, [((block, width), bf16)] * 2, own, other)
 
+    last_two = add_halve(last_one[0], after(last_one_other, feed_other, qkv_two_other))
+    last_two_other = place.swap_z(last_two[1], 2)
     qkv_sum = add(
-        qkv_two[0], after(qkv_two_other, last_one_other, few_one_other, down_other, up_other)
+        qkv_two[0], after(qkv_two_other, last_two[1])
+    )
+
+    def feed_split_kernel(own_ref, other_ref, down_ref, mine_ref, send_ref):
+        y, _, _, x = coordinates()
+        total = own_ref[: 2 * many, :].astype(f32) + other_ref[: 2 * many, :].astype(f32)
+        down_ref[...] = total.astype(bf16)
+        own, other = own_ref[2 * many :, :], other_ref[2 * many :, :]
+        mine_ref[...] = jnp.where(y == x, own, other)
+        send_ref[...] = jnp.where(y == x, other, own)
+
+    block_bf16 = ((block, width), bf16)
+    down_sum, up_mine, up_send = in_vmem(
+        feed_split_kernel, [((2 * many, width), bf16), block_bf16, block_bf16],
+        feed_sum, after(feed_other, last_two[1]),
     )
     qkv_other = place.swap_y(qkv_sum)
-    up_mine, up_send = by_x(up_sum, up_other, ff_slice)
-    up_both = place.swap_x(up_send)
-    down_sum = add(down_sum, down_other)
+    up_there = place.swap_x(up_send)
     down_far = place.swap_core(down_sum)
-    last_two = add_halve(last_one[0], after(last_one_other, qkv_sum))
-    last_two_other = place.swap_z(last_two[1], 2)
-    few_two = add_halve(few_one[0], after(few_one_other, qkv_sum))
-    few_two_other = place.swap_z(few_two[1], 2)
-    qkv_other, up_both, down_far, last_two_other, few_two_other, one, two = lax.optimization_barrier(
-        (qkv_other, up_both, down_far, last_two_other, few_two_other, one, two)
-    )
-    last = add(last_two[0], last_two_other)
-    last_other = place.swap_y(last)
-
-    def last_add_kernel(one_ref, other_ref, out_ref, sums_ref):
-        total = one_ref[...].astype(f32) + other_ref[...].astype(f32)
-        out_ref[...] = total[:half, :].astype(bf16)
-        sums_ref[...] = total[half : half + 8, :block]
-
-    out_enc, sums = in_vmem(
-        last_add_kernel, [((half, width), bf16), ((8, block), f32)], last, last_other
-    )
-
     def halves_kernel(near_ref, far_ref, out_ref):
         _, core, _, _ = coordinates()
         count = near_ref.shape[0]
@@ -1043,9 +1049,6 @@
             halves_kernel, [((2 * near.shape[0], near.shape[1]), f32)], near, far
         )
 
-    out_enc = halves(out_enc, place.swap_core(out_enc))
-
-    up_both = jnp.concatenate([up_mine, up_both], axis=0)
 
     def up_out_kernel(near_ref, far_ref, out_ref):
         _, core, _, x = coordinates()
@@ -1055,14 +1058,43 @@
                     part = ref[dx * block : (dx + 1) * block, 2 * k * lanes : 2 * (k + 1) * lanes]
                     put(out_ref, 0, ((2 * k + (x ^ dx)) * 2 + (core ^ dc)) * 2 * lanes, part)
 
+    qkv_other, last_two_other, one, two, up_there, down_far = lax.optimization_barrier(
+        (qkv_other, last_two_other, one, two, up_there, down_far)
+    )
+    up_both = jnp.concatenate([up_mine, up_there], axis=0)
+    out_down = halves(down_sum, down_far)
+    out_up = in_vmem(
+        up_out_kernel, [((block, ff), f32)], up_both, place.swap_core(up_both)
+    )
+    last = add(last_two[0], last_two_other)
+    last_other = place.swap_y(last)
+
+    def last_add_kernel(one_ref, other_ref, out_ref, sums_ref):
+        y, _, _, _ = coordinates()
+        total = one_ref[: half + 16, :].astype(f32) + other_ref[: half + 16, :].astype(f32)
+        out_ref[:half, :] = total[:half, :].astype(bf16)
+        sums_ref[...] = total[half : half + 8, :block]
+        own, other = one_ref[half + 16 :, :], other_ref[half + 16 :, :]
+        out_ref[half : 2 * half, :] = jnp.where(y == 0, own, other)
+        out_ref[2 * half :, :] = jnp.where(y == 0, other, own)
+
+    last, sums = in_vmem(
+        last_add_kernel, [((3 * half, width), bf16), ((8, block), f32)], last, last_other
+    )
+
+    def last_out_kernel(near_ref, far_ref, *out_refs):
+        _, core, _, _ = coordinates()
+        for dc, ref in enumerate((near_ref, far_ref)):
+            for part, out_ref in enumerate(out_refs):
+                put(out_ref, (core ^ dc) * half, 0, ref[part * half : (part + 1) * half, :])
+
+    out_enc, out_out, out_dec = in_vmem(
+        last_out_kernel, [((block, width), f32)] * 3, last, place.swap_core(last)
+    )
 
     qkv_mine, qkv_send = by_x(qkv_sum, qkv_other, three)
     qkv_there = place.swap_x(qkv_send)
     qkv_both = jnp.concatenate([qkv_mine, qkv_there], axis=0)
-    out_down = halves(down_sum, after(down_far, qkv_there))
-    up_far_both = after(place.swap_core(up_both), qkv_there)
-    out_up = in_vmem(up_out_kernel, [((block, ff), f32)], up_both, up_far_both)
-    few_sum = add(few_two[0], few_two_other)
     pair = place.regroup(
         *(
             jnp.concatenate(
@@ -1073,23 +1105,6 @@
     )
     pair = jnp.stack(place.by_parity(pair))
     logits, input_grad = pair[:, :, :genes], pair[:, :, genes:]
-
-    def few_kernel(own_ref, other_ref, out_ref):
-        y, _, _, _ = coordinates()
-        put(out_ref, y * half, 0, own_ref[...])
-        put(out_ref, (1 - y) * half, 0, other_ref[...])
-
-    few = in_vmem(few_kernel, [((block, genes), bf16)], few_sum, place.swap_y(few_sum))
-
-    def few_out_kernel(near_ref, far_ref, out_ref, dec_ref):
-        _, core, _, _ = coordinates()
-        for dc, ref in enumerate((near_ref, far_ref)):
-            put(out_ref, (core ^ dc) * half, 0, ref[:half, :])
-            put(dec_ref, (core ^ dc) * half, 0, ref[half:, :])
-
-    out_out, out_dec = in_vmem(
-        few_out_kernel, [((block, width), f32), ((block, genes), f32)], few, place.swap_core(few)
-    )
 
     def qkv_out_kernel(near_ref, far_ref, out_ref):
         _, core, _, x = coordinates()

time: 280 us -> 275 us (0.982)
  starting transfers between devices: 76.9 us -> 70.4 us
  waiting for transfers between devices: 138 us -> 142 us
    ppermute x63 -> x58, starting transfers between devices: 71.4 us -> 64.8 us  [send(): lax.ppermute(value, AXES, [(flat(p), flat(move(*p))) for p in everywhere])]
    ppermute x63 -> x58, waiting for transfers between devices: 129 us -> 132 us  [send(): lax.ppermute(value, AXES, [(flat(p), flat(move(*p))) for p in everywhere])]
    pallas_call x49 -> x42, Pallas kernels: 36.5 us -> 35.4 us  [in_vmem(): pl.pallas_call(kernel, out_shape=shapes, in_specs=[whole] * len(operands)...]
  transfers between devices with their start and end apart: 64 -> 59, of which waited for: 26 -> 27; matrix products, arithmetic and copies ran while one was open for 6% -> 6% of each run, Pallas kernels for 9% -> 9%
where the time goes in v5:
time: 275 us; the launch traced here: 271 us
  waiting for transfers between devices  142 us (52%)
  starting transfers between devices  70.4 us (26%)
  Pallas kernels  35.4 us (13%)
  local copies, waits for them, and re-layouts  9.07 us (3%)
  matrix products  8.2 us (3%)
  other arithmetic  5.03 us (2%)
    ppermute x58, waiting for transfers between devices, send(): lax.ppermute(value, AXES, [(flat(p), flat(move(*p))) for p in everywhere])  132 us
    ppermute x58, starting transfers between devices, send(): lax.ppermute(value, AXES, [(flat(p), flat(move(*p))) for p in everywhere])  64.8 us
    pallas_call x42, Pallas kernels, in_vmem(): pl.pallas_call(kernel, out_shape=shapes, in_specs=[whole] * len(operands)...  35.4 us
    all_to_all x1, waiting for transfers between devices, exchange_z(): return lax.all_to_all(value, 'z', split_axis=0, concat_axis=0, tiled=True)  9.25 us
    unnamed x28, local copies, waits for them, and re-layouts  5.85 us
    all_to_all x1, starting transfers between devices, exchange_z(): return lax.all_to_all(value, 'z', split_axis=0, concat_axis=0, tiled=True)  5.55 us
  transfers between devices with their start and end apart: 59, of which 27 were waited for; matrix products, arithmetic and copies ran while one was open for 6% of the time, Pallas kernels for 9%

profile of v5, /device:TPU:1, one launch (start us, length us, event | category | flops | bytes accessed | tf_op | source)
XLA Modules:
  0.0 271.4 jit_solution(5575278469663400029)
XLA Ops:
  4.3 5.6 %all-to-all-start = ((bf16[4,112,1024]{2,1,0:T(8,128)(2,1)}), bf16[4,112,1024]{2,1,0:T(8,128)(2,1)S(1)}, u32[]{:S(2)}, u32[]{:S(2)}) async-start(bf16[4,112,1024]{2,1,0:T(8,128)(2,1)} %bitcast.10), calls=%async_computation | async-start | bytes 1835008 | tf_op jit(solution)/shard_map/all_to_all | solution.py:309
  14.4 5.7 %collective-permute-start = (bf16[64,2176]{1,0:T(8,128)(2,1)}, bf16[64,2176]{1,0:T(8,128)(2,1)}, u32[]{:S(2)}, u32[]{:S(2)}) collective-permute-start(bf16[64,2176]{1,0:T(8,128)(2,1)} %get-tuple-element.262), channel_id=1, source_target_pairs={{0,0},{1,1},{2,2},{3,3},{4,8},{5,9},{6,10},{7,11},{8,4},{9,5},{10,... | collective-permute-start | bytes 835592 | tf_op jit(solution)/shard_map/ppermute | solution.py:290
  21.1 1.9 collective-permute-done.2.theirs_ref
  24.5 9.2 %all-to-all-done = bf16[4,112,1024]{2,1,0:T(8,128)(2,1)S(1)} async-done(((bf16[4,112,1024]{2,1,0:T(8,128)(2,1)}), bf16[4,112,1024]{2,1,0:T(8,128)(2,1)S(1)}, u32[]{:S(2)}, u32[]{:S(2)}) %all-to-all-start) | async-done | bytes 917536 | tf_op jit(solution)/shard_map/all_to_all | solution.py:309
  33.7 2.4 collective-permute-start.3
  38.8 20.1 %collective-permute-done = bf16[64,2176]{1,0:T(8,128)(2,1)} collective-permute-done((bf16[64,2176]{1,0:T(8,128)(2,1)}, bf16[64,2176]{1,0:T(8,128)(2,1)}, u32[]{:S(2)}, u32[]{:S(2)}) %collective-permute-start) | collective-permute-done | bytes 278560 | tf_op jit(solution)/shard_map/ppermute | solution.py:290
  64.7 4.5 %collective-permute-done.11.refs_5_ = bf16[128,1024]{1,0:T(8,128)(2,1)S(1)} collective-permute-done((bf16[128,1024]{1,0:T(8,128)(2,1)S(1)}, bf16[128,1024]{1,0:T(8,128)(2,1)S(1)}, u32[]{:S(2)}, u32[]{:S(2)}) %collective-permute-start.11) | collective-permute-done | bytes 262176 | tf_op jit(solution)/shard_map/ppermute | solution.py:290
  70.4 4.4 %collective-permute-done.7.one_ref.refs_2_ = bf16[128,1024]{1,0:T(8,128)(2,1)S(1)} collective-permute-done((bf16[128,1024]{1,0:T(8,128)(2,1)S(1)}, bf16[128,1024]{1,0:T(8,128)(2,1)S(1)}, u32[]{:S(2)}, u32[]{:S(2)}) %collective-permute-start.7) | collective-permute-done | bytes 262176 | tf_op jit(solution)/shard_map/ppermute | solution.py:290
  74.8 4.2 %collective-permute-done.8.two_ref.refs_3_ = bf16[128,1024]{1,0:T(8,128)(2,1)S(1)} collective-permute-done((bf16[128,1024]{1,0:T(8,128)(2,1)S(1)}, bf16[128,1024]{1,0:T(8,128)(2,1)S(1)}, u32[]{:S(2)}, u32[]{:S(2)}) %collective-permute-start.8) | collective-permute-done | bytes 262176 | tf_op jit(solution)/shard_map/ppermute | solution.py:290
  79.2 3.5 %collective-permute-start.14 = (bf16[256,1024]{1,0:T(8,128)(2,1)S(1)}, bf16[256,1024]{1,0:T(8,128)(2,1)S(1)}, u32[]{:S(2)}, u32[]{:S(2)}) collective-permute-start(bf16[256,1024]{1,0:T(8,128)(2,1)S(1)} %collective-permute-done.6.refs_1_), channel_id=1, source_target_pairs={{0,2},{1,3},{2,4},{3,5},{4,6},{5,7},{6,0},{7,1},{8,10},{9,11},{10,... | collective-permute-start | bytes 1572872 | tf_op jit(solution)/shard_map/ppermute | solution.py:290
  85.1 11.0 %collective-permute-done.14.refs_2_ = bf16[256,1024]{1,0:T(8,128)(2,1)S(1)} collective-permute-done((bf16[256,1024]{1,0:T(8,128)(2,1)S(1)}, bf16[256,1024]{1,0:T(8,128)(2,1)S(1)}, u32[]{:S(2)}, u32[]{:S(2)}) %collective-permute-start.14) | collective-permute-done | bytes 524320 | tf_op jit(solution)/shard_map/ppermute | solution.py:290
  101.7 2.0 shard_map.251
  104.0 3.9 %shard_map.253 = (bf16[1024,768]{1,0:T(8,128)(2,1)S(1)}, bf16[256,1024]{1,0:T(8,128)(2,1)S(1)}, bf16[512,768]{1,0:T(8,128)(2,1)S(1)}, bf16[512,256]{1,0:T(8,128)...) custom-call(bf16[512,1024]{1,0:T(8,128)(2,1)S(1)} %get-tuple-element.146.normed_ref, ...), custom_call_target="tpu_custom_call" | custom-call | bytes 1024 | tf_op jit(solution)/shard_map/pallas_call | solution.py:368
  112.3 10.7 %collective-permute-done.22.far_ref = bf16[256,1024]{1,0:T(8,128)(2,1)S(1)} collective-permute-done((bf16[256,1024]{1,0:T(8,128)(2,1)S(1)}, bf16[256,1024]{1,0:T(8,128)(2,1)S(1)}, u32[]{:S(2)}, u32[]{:S(2)}) %collective-permute-start.22) | collective-permute-done | bytes 524320 | tf_op jit(solution)/shard_map/ppermute | solution.py:290
  128.1 6.3 %shard_map.259 = (bf16[512,1024]{1,0:T(8,128)(2,1)S(1)}, bf16[512,1024]{1,0:T(8,128)(2,1)S(1)}, f32[256,1024]{1,0:T(8,128)S(1)}, bf16[256,1024]{1,0:T(8,128)(2,1...) custom-call(bf16[256,1024]{1,0:T(8,128)(2,1)S(1)} %get-tuple-element, ...), custom_call_target="tpu_custom_call" | custom-call | bytes 1024 | tf_op jit(solution)/shard_map/pallas_call | solution.py:368
  140.9 8.8 %collective-permute-done.28.other_ref = bf16[256,1024]{1,0:T(8,128)(2,1)S(1)} collective-permute-done((bf16[256,1024]{1,0:T(8,128)(2,1)S(1)}, bf16[256,1024]{1,0:T(8,128)(2,1)S(1)}, u32[]{:S(2)}, u32[]{:S(2)}) %collective-permute-start.28) | collective-permute-done | bytes 524320 | tf_op jit(solution)/shard_map/ppermute | solution.py:290
  153.0 1.9 collective-permute-start.29
  158.6 6.0 %shard_map.264 = (bf16[512,768]{1,0:T(8,128)(2,1)S(1)}, f32[256,1024]{1,0:T(8,128)S(1)}, bf16[256,1024]{1,0:T(8,128)(2,1)S(1)}, bf16[512,1024]{1,0:T(8,128)(2,1)S(1)}) custom-call(bf16[272,1024]{1,0:T(8,128)(2,1)S(1)} %get-tuple-element.173.near_ref.two_ref, bf16[272,1024]{1,0:T(8,128)(2,1)S(1)} %collective-permute-done.29.far_ref.two_far_ref, ...), custom_call_target="tpu_custom_call" | custom-call | bytes 1024 | tf_op jit(solution)/shard_map/pallas_call | solution.py:368
  165.9 7.8 %collective-permute-done.35.other_ref = bf16[128,1024]{1,0:T(8,128)(2,1)S(1)} collective-permute-done((bf16[128,1024]{1,0:T(8,128)(2,1)S(1)}, bf16[128,1024]{1,0:T(8,128)(2,1)S(1)}, u32[]{:S(2)}, u32[]{:S(2)}) %collective-permute-start.35) | collective-permute-done | bytes 262176 | tf_op jit(solution)/shard_map/ppermute | solution.py:290
  176.3 2.0 collective-permute-start.38
  180.5 9.0 %collective-permute-done.38.one_other_ref = bf16[128,1024]{1,0:T(8,128)(2,1)S(1)} collective-permute-done((bf16[128,1024]{1,0:T(8,128)(2,1)S(1)}, bf16[128,1024]{1,0:T(8,128)(2,1)S(1)}, u32[]{:S(2)}, u32[]{:S(2)}) %collective-permute-start.38) | collective-permute-done | bytes 262176 | tf_op jit(solution)/shard_map/ppermute | solution.py:290
  190.5 2.3 collective-permute-start.39
  196.5 2.4 collective-permute-start.41
  199.0 13.0 %collective-permute-done.31.other_ref = bf16[256,768]{1,0:T(8,128)(2,1)S(1)} collective-permute-done((bf16[256,768]{1,0:T(8,128)(2,1)S(1)}, bf16[256,768]{1,0:T(8,128)(2,1)S(1)}, u32[]{:S(2)}, u32[]{:S(2)}) %collective-permute-start.31) | collective-permute-done | bytes 393248 | tf_op jit(solution)/shard_map/ppermute | solution.py:290
  218.7 12.8 %collective-permute-done.44.other_ref = bf16[128,768]{1,0:T(8,128)(2,1)S(1)} collective-permute-done((bf16[128,768]{1,0:T(8,128)(2,1)S(1)}, bf16[128,768]{1,0:T(8,128)(2,1)S(1)}, u32[]{:S(2)}, u32[]{:S(2)}) %collective-permute-start.44) | collective-permute-done | bytes 196640 | tf_op jit(solution)/shard_map/ppermute | solution.py:290
  232.6 2.3 collective-permute-start.50
  235.0 2.4 collective-permute-start.48
  238.9 4.8 %collective-permute-done.47.other_ref = bf16[128,768]{1,0:T(8,128)(2,1)S(1)} collective-permute-done((bf16[128,768]{1,0:T(8,128)(2,1)S(1)}, bf16[128,768]{1,0:T(8,128)(2,1)S(1)}, u32[]{:S(2)}, u32[]{:S(2)}) %collective-permute-start.47) | collective-permute-done | bytes 196640 | tf_op jit(solution)/shard_map/ppermute | solution.py:290
  244.9 6.0 %collective-permute-done.48.other_ref = bf16[144,1024]{1,0:T(8,128)(2,1)S(1)} collective-permute-done((bf16[144,1024]{1,0:T(8,128)(2,1)S(1)}, bf16[144,1024]{1,0:T(8,128)(2,1)S(1)}, u32[]{:S(2)}, u32[]{:S(2)}) %collective-permute-start.48) | collective-permute-done | bytes 294944 | tf_op jit(solution)/shard_map/ppermute | solution.py:290
  251.0 3.1 %collective-permute-start.52 = (bf16[64,2048]{1,0:T(8,128)(2,1)S(1)}, bf16[64,2048]{1,0:T(8,128)(2,1)S(1)}, u32[]{:S(2)}, u32[]{:S(2)}) collective-permute-start(bf16[64,2048]{1,0:T(8,128)(2,1)S(1)} %pad_maximum_fusion.5), channel_id=1, source_target_pairs={{0,2},{1,3},{2,0},{3,1},{4,10},{5,11},{6,8},{7,9},{8,6},{9,7},{10,... | collective-permute-start | bytes 786440 | tf_op jit(solution)/shard_map/ppermute | solution.py:290
  254.1 1.9 collective-permute-start.51
  262.0 3.5 %collective-permute-done.51 = bf16[64,2048]{1,0:T(8,128)(2,1)S(1)} collective-permute-done((bf16[64,2048]{1,0:T(8,128)(2,1)S(1)}, bf16[64,2048]{1,0:T(8,128)(2,1)S(1)}, u32[]{:S(2)}, u32[]{:S(2)}) %collective-permute-start.51) | collective-permute-done | bytes 262176 | tf_op jit(solution)/shard_map/ppermute | solution.py:290
  (202 shorter events, 84.1 us)
Async XLA Ops:
  4.3 29.4 %all-to-all-start = ((bf16[4,112,1024]{2,1,0:T(8,128)(2,1)}), bf16[4,112,1024]{2,1,0:T(8,128)(2,1)S(1)}, u32[]{:S(2)}, u32[]{:S(2)}) async-start(bf16[4,112,1024]{2,1,0:T(8,128)(2,1)} %bitcast.10), calls=%async_computation | async-start | bytes 1835008 | tf_op jit(solution)/shard_map/all_to_all | solution.py:309
  14.4 44.5 %collective-permute-start = (bf16[64,2176]{1,0:T(8,128)(2,1)}, bf16[64,2176]{1,0:T(8,128)(2,1)}, u32[]{:S(2)}, u32[]{:S(2)}) collective-permute-start(bf16[64,2176]{1,0:T(8,128)(2,1)} %get-tuple-element.262), channel_id=1, source_target_pairs={{0,0},{1,1},{2,2},{3,3},{4,8},{5,9},{6,10},{7,11},{8,4},{9,5},{10,... | collective-permute-start | bytes 835592 | tf_op jit(solution)/shard_map/ppermute | solution.py:290
  20.1 40.1 %collective-permute-start.1 = (bf16[64,2176]{1,0:T(8,128)(2,1)}, bf16[64,2176]{1,0:T(8,128)(2,1)}, u32[]{:S(2)}, u32[]{:S(2)}) collective-permute-start(bf16[64,2176]{1,0:T(8,128)(2,1)} %get-tuple-element.261), channel_id=1, source_target_pairs={{0,2},{1,3},{2,0},{3,1},{4,10},{5,11},{6,8},{7,9},{8,6},{9,7},{10,... | collective-permute-start | bytes 835592 | tf_op jit(solution)/shard_map/ppermute | solution.py:290
  33.7 26.4 %collective-permute-start.3 = (bf16[128,1024]{1,0:T(8,128)(2,1)S(1)}, bf16[128,1024]{1,0:T(8,128)(2,1)S(1)}, u32[]{:S(2)}, u32[]{:S(2)}) collective-permute-start(bf16[128,1024]{1,0:T(8,128)(2,1)S(1)} %get-tuple-element.138.refs_0_), channel_id=1, source_target_pairs={{0,2},{1,3},{2,4},{3,5},{4,6},{5,7},{6,0},{7,1},{8,10},{9,11},{10,... | collective-permute-start | bytes 786440 | tf_op jit(solution)/shard_map/ppermute | solution.py:290
  37.5 25.4 %collective-permute-start.6 = (bf16[256,1024]{1,0:T(8,128)(2,1)S(1)}, bf16[256,1024]{1,0:T(8,128)(2,1)S(1)}, u32[]{:S(2)}, u32[]{:S(2)}) collective-permute-start(bf16[256,1024]{1,0:T(8,128)(2,1)S(1)} %shard_map.249.refs_0_), channel_id=1, source_target_pairs={{0,2},{1,3},{2,4},{3,5},{4,6},{5,7},{6,0},{7,1},{8,10},{9,11},{10,... | collective-permute-start | bytes 1572872 | tf_op jit(solution)/shard_map/ppermute | solution.py:290
  37.5 26.5 %collective-permute-start.5 = (bf16[256,1024]{1,0:T(8,128)(2,1)S(1)}, bf16[256,1024]{1,0:T(8,128)(2,1)S(1)}, u32[]{:S(2)}, u32[]{:S(2)}) collective-permute-start(bf16[256,1024]{1,0:T(8,128)(2,1)S(1)} %shard_map.249.refs_0_), channel_id=1, source_target_pairs={{0,16},{1,17},{2,18},{3,19},{4,20},{5,21},{6,22},{7,23},{8,24},{9,... | collective-permute-start | bytes 1572872 | tf_op jit(solution)/shard_map/ppermute | solution.py:290
  59.0 20.1 %collective-permute-start.9 = (bf16[448,1024]{1,0:T(8,128)(2,1)S(1)}, bf16[448,1024]{1,0:T(8,128)(2,1)S(1)}, u32[]{:S(2)}, u32[]{:S(2)}) collective-permute-start(bf16[448,1024]{1,0:T(8,128)(2,1)S(1)} %bitcast.47), channel_id=1, source_target_pairs={{0,1},{1,0},{2,3},{3,2},{4,5},{5,4},{6,7},{7,6},{8,9},{9,8},{10,11... | collective-permute-start | bytes 2752520 | tf_op jit(solution)/shard_map/ppermute | solution.py:290
  61.3 17.7 %collective-permute-start.4 = (bf16[128,2176]{1,0:T(8,128)(2,1)S(1)}, bf16[128,2176]{1,0:T(8,128)(2,1)S(1)}, u32[]{:S(2)}, u32[]{:S(2)}) collective-permute-start(bf16[128,2176]{1,0:T(8,128)(2,1)S(1)} %pad_maximum_fusion.2), channel_id=1, source_target_pairs={{0,1},{1,0},{2,3},{3,2},{4,5},{5,4},{6,7},{7,6},{8,9},{9,8},{10,11... | collective-permute-start | bytes 1671176 | tf_op jit(solution)/shard_map/ppermute | solution.py:290
  62.8 16.2 %collective-permute-start.10 = (bf16[256,1024]{1,0:T(8,128)(2,1)S(1)}, bf16[256,1024]{1,0:T(8,128)(2,1)S(1)}, u32[]{:S(2)}, u32[]{:S(2)}) collective-permute-start(bf16[256,1024]{1,0:T(8,128)(2,1)S(1)} %collective-permute-done.6.refs_1_), channel_id=1, source_target_pairs={{0,16},{1,17},{2,18},{3,19},{4,20},{5,21},{6,22},{7,23},{8,24},{9,... | collective-permute-start | bytes 1572872 | tf_op jit(solution)/shard_map/ppermute | solution.py:290
  79.1 18.4 %collective-permute-start.12 = (bf16[256,2176]{1,0:T(8,128)(2,1)S(1)}, bf16[256,2176]{1,0:T(8,128)(2,1)S(1)}, u32[]{:S(2)}, u32[]{:S(2)}) collective-permute-start(bf16[256,2176]{1,0:T(8,128)(2,1)S(1)} %constant_dynamic-update-slice_fusion.near_ref.near_cells_ref), channel_id=1, source_target_pairs={{0,8},{1,9},{2,10},{3,11},{4,12},{5,13},{6,14},{7,15},{8,0},{9,1},... | collective-permute-start | bytes 3342344 | tf_op jit(solution)/shard_map/ppermute | solution.py:290
  79.2 16.9 %collective-permute-start.14 = (bf16[256,1024]{1,0:T(8,128)(2,1)S(1)}, bf16[256,1024]{1,0:T(8,128)(2,1)S(1)}, u32[]{:S(2)}, u32[]{:S(2)}) collective-permute-start(bf16[256,1024]{1,0:T(8,128)(2,1)S(1)} %collective-permute-done.6.refs_1_), channel_id=1, source_target_pairs={{0,2},{1,3},{2,4},{3,5},{4,6},{5,7},{6,0},{7,1},{8,10},{9,11},{10,... | collective-permute-start | bytes 1572872 | tf_op jit(solution)/shard_map/ppermute | solution.py:290
  83.0 21.0 %collective-permute-start.15 = (bf16[256,1024]{1,0:T(8,128)(2,1)S(1)}, bf16[256,1024]{1,0:T(8,128)(2,1)S(1)}, u32[]{:S(2)}, u32[]{:S(2)}) collective-permute-start(bf16[256,1024]{1,0:T(8,128)(2,1)S(1)} %shard_map.252), channel_id=1, source_target_pairs={{0,16},{1,17},{2,18},{3,19},{4,20},{5,21},{6,22},{7,23},{8,24},{9,... | collective-permute-start | bytes 1572872 | tf_op jit(solution)/shard_map/ppermute | solution.py:290
  84.4 17.4 %collective-permute-start.13 = (bf16[512,1024]{1,0:T(8,128)(2,1)S(1)}, bf16[512,1024]{1,0:T(8,128)(2,1)S(1)}, u32[]{:S(2)}, u32[]{:S(2)}) collective-permute-start(bf16[512,1024]{1,0:T(8,128)(2,1)S(1)} %get-tuple-element.140.enc_near_ref), channel_id=1, source_target_pairs={{0,8},{1,9},{2,10},{3,11},{4,12},{5,13},{6,14},{7,15},{8,0},{9,1},... | collective-permute-start | bytes 3145736 | tf_op jit(solution)/shard_map/ppermute | solution.py:290
  96.1 14.4 %collective-permute-start.17 = (bf16[256,1024]{1,0:T(8,128)(2,1)S(1)}, bf16[256,1024]{1,0:T(8,128)(2,1)S(1)}, u32[]{:S(2)}, u32[]{:S(2)}) collective-permute-start(bf16[256,1024]{1,0:T(8,128)(2,1)S(1)} %collective-permute-done.14.refs_2_), channel_id=1, source_target_pairs={{0,2},{1,3},{2,4},{3,5},{4,6},{5,7},{6,0},{7,1},{8,10},{9,11},{10,... | collective-permute-start | bytes 1572872 | tf_op jit(solution)/shard_map/ppermute | solution.py:290
  109.4 13.6 %collective-permute-start.22 = (bf16[256,1024]{1,0:T(8,128)(2,1)S(1)}, bf16[256,1024]{1,0:T(8,128)(2,1)S(1)}, u32[]{:S(2)}, u32[]{:S(2)}) collective-permute-start(bf16[256,1024]{1,0:T(8,128)(2,1)S(1)} %shard_map.256.near_ref), channel_id=1, source_target_pairs={{0,16},{1,17},{2,18},{3,19},{4,20},{5,21},{6,22},{7,23},{8,24},{9,... | collective-permute-start | bytes 1572872 | tf_op jit(solution)/shard_map/ppermute | solution.py:290
  109.7 14.6 %collective-permute-start.20 = (bf16[256,1024]{1,0:T(8,128)(2,1)S(1)}, bf16[256,1024]{1,0:T(8,128)(2,1)S(1)}, u32[]{:S(2)}, u32[]{:S(2)}) collective-permute-start(bf16[256,1024]{1,0:T(8,128)(2,1)S(1)} %collective-permute-done.18.refs_6_), channel_id=1, source_target_pairs={{0,2},{1,3},{2,4},{3,5},{4,6},{5,7},{6,0},{7,1},{8,10},{9,11},{10,... | collective-permute-start | bytes 1572872 | tf_op jit(solution)/shard_map/ppermute | solution.py:290
  154.9 18.8 %collective-permute-start.33 = (bf16[256,1024]{1,0:T(8,128)(2,1)S(1)}, bf16[256,1024]{1,0:T(8,128)(2,1)S(1)}, u32[]{:S(2)}, u32[]{:S(2)}) collective-permute-start(bf16[256,1024]{1,0:T(8,128)(2,1)S(1)} %get-tuple-element.182), channel_id=1, source_target_pairs={{0,16},{1,17},{2,18},{3,19},{4,20},{5,21},{6,22},{7,23},{8,24},{9,... | collective-permute-start | bytes 1572872 | tf_op jit(solution)/shard_map/ppermute | solution.py:290
  155.7 18.8 %collective-permute-start.34 = (bf16[256,1024]{1,0:T(8,128)(2,1)S(1)}, bf16[256,1024]{1,0:T(8,128)(2,1)S(1)}, u32[]{:S(2)}, u32[]{:S(2)}) collective-permute-start(bf16[256,1024]{1,0:T(8,128)(2,1)S(1)} %get-tuple-element.184), channel_id=1, source_target_pairs={{0,2},{1,3},{2,0},{3,1},{4,6},{5,7},{6,4},{7,5},{8,10},{9,11},{10,... | collective-permute-start | bytes 1572872 | tf_op jit(solution)/shard_map/ppermute | solution.py:290
  157.2 17.3 %collective-permute-start.36 = (bf16[256,1024]{1,0:T(8,128)(2,1)S(1)}, bf16[256,1024]{1,0:T(8,128)(2,1)S(1)}, u32[]{:S(2)}, u32[]{:S(2)}) collective-permute-start(bf16[256,1024]{1,0:T(8,128)(2,1)S(1)} %shard_map.261.mine_ref), channel_id=1, source_target_pairs={{0,1},{1,0},{2,3},{3,2},{4,5},{5,4},{6,7},{7,6},{8,9},{9,8},{10,11... | collective-permute-start | bytes 1572872 | tf_op jit(solution)/shard_map/ppermute | solution.py:290
  157.6 16.2 %collective-permute-start.35 = (bf16[128,1024]{1,0:T(8,128)(2,1)S(1)}, bf16[128,1024]{1,0:T(8,128)(2,1)S(1)}, u32[]{:S(2)}, u32[]{:S(2)}) collective-permute-start(bf16[128,1024]{1,0:T(8,128)(2,1)S(1)} %get-tuple-element.187), channel_id=1, source_target_pairs={{0,4},{1,5},{2,6},{3,7},{4,0},{5,1},{6,2},{7,3},{8,12},{9,13},{10,... | collective-permute-start | bytes 786440 | tf_op jit(solution)/shard_map/ppermute | solution.py:290
  175.2 14.3 %collective-permute-start.37 = (bf16[256,1024]{1,0:T(8,128)(2,1)S(1)}, bf16[256,1024]{1,0:T(8,128)(2,1)S(1)}, u32[]{:S(2)}, u32[]{:S(2)}) collective-permute-start(bf16[256,1024]{1,0:T(8,128)(2,1)S(1)} %shard_map.267.refs_1_), channel_id=1, source_target_pairs={{0,1},{1,0},{2,3},{3,2},{4,5},{5,4},{6,7},{7,6},{8,9},{9,8},{10,11... | collective-permute-start | bytes 1572872 | tf_op jit(solution)/shard_map/ppermute | solution.py:290
  175.6 20.4 %collective-permute-start.30 = (bf16[512,768]{1,0:T(8,128)(2,1)S(1)}, bf16[512,768]{1,0:T(8,128)(2,1)S(1)}, u32[]{:S(2)}, u32[]{:S(2)}) collective-permute-start(bf16[512,768]{1,0:T(8,128)(2,1)S(1)} %convolution_convert_fusion.3), channel_id=1, source_target_pairs={{0,16},{1,17},{2,18},{3,19},{4,20},{5,21},{6,22},{7,23},{8,24},{9,... | collective-permute-start | bytes 2359304 | tf_op jit(solution)/shard_map/ppermute | solution.py:290
  179.4 16.9 %collective-permute-start.40 = (bf16[256,1024]{1,0:T(8,128)(2,1)S(1)}, bf16[256,1024]{1,0:T(8,128)(2,1)S(1)}, u32[]{:S(2)}, u32[]{:S(2)}) collective-permute-start(bf16[256,1024]{1,0:T(8,128)(2,1)S(1)} %get-tuple-element.201), channel_id=1, source_target_pairs={{0,2},{1,3},{2,0},{3,1},{4,6},{5,7},{6,4},{7,5},{8,10},{9,11},{10,... | collective-permute-start | bytes 1572872 | tf_op jit(solution)/shard_map/ppermute | solution.py:290
  190.5 21.6 %collective-permute-start.39 = (bf16[272,1024]{1,0:T(8,128)(2,1)S(1)}, bf16[272,1024]{1,0:T(8,128)(2,1)S(1)}, u32[]{:S(2)}, u32[]{:S(2)}) collective-permute-start(bf16[272,1024]{1,0:T(8,128)(2,1)S(1)} %shard_map.269.one_ref), channel_id=1, source_target_pairs={{0,8},{1,9},{2,10},{3,11},{4,12},{5,13},{6,14},{7,15},{8,0},{9,1},... | collective-permute-start | bytes 1671176 | tf_op jit(solution)/shard_map/ppermute | solution.py:290
  195.1 17.0 %collective-permute-start.43 = (bf16[256,1024]{1,0:T(8,128)(2,1)S(1)}, bf16[256,1024]{1,0:T(8,128)(2,1)S(1)}, u32[]{:S(2)}, u32[]{:S(2)}) collective-permute-start(bf16[256,1024]{1,0:T(8,128)(2,1)S(1)} %get-tuple-element.212), channel_id=1, source_target_pairs={{0,16},{1,17},{2,18},{3,19},{4,20},{5,21},{6,22},{7,23},{8,24},{9,... | collective-permute-start | bytes 1572872 | tf_op jit(solution)/shard_map/ppermute | solution.py:290
  196.3 15.8 %collective-permute-start.31 = (bf16[256,768]{1,0:T(8,128)(2,1)S(1)}, bf16[256,768]{1,0:T(8,128)(2,1)S(1)}, u32[]{:S(2)}, u32[]{:S(2)}) collective-permute-start(bf16[256,768]{1,0:T(8,128)(2,1)S(1)} %get-tuple-element.179), channel_id=1, source_target_pairs={{0,2},{1,3},{2,0},{3,1},{4,6},{5,7},{6,4},{7,5},{8,10},{9,11},{10,... | collective-permute-start | bytes 1179656 | tf_op jit(solution)/shard_map/ppermute | solution.py:290
  196.5 15.5 %collective-permute-start.41 = (bf16[128,1024]{1,0:T(8,128)(2,1)S(1)}, bf16[128,1024]{1,0:T(8,128)(2,1)S(1)}, u32[]{:S(2)}, u32[]{:S(2)}) collective-permute-start(bf16[128,1024]{1,0:T(8,128)(2,1)S(1)} %get-tuple-element.203), channel_id=1, source_target_pairs={{0,4},{1,5},{2,6},{3,7},{4,0},{5,1},{6,2},{7,3},{8,12},{9,13},{10,... | collective-permute-start | bytes 786440 | tf_op jit(solution)/shard_map/ppermute | solution.py:290
  213.5 18.8 %collective-permute-start.46 = (bf16[384,1024]{1,0:T(8,128)(2,1)S(1)}, bf16[384,1024]{1,0:T(8,128)(2,1)S(1)}, u32[]{:S(2)}, u32[]{:S(2)}) collective-permute-start(bf16[384,1024]{1,0:T(8,128)(2,1)S(1)} %shard_map.277.own_ref), channel_id=1, source_target_pairs={{0,16},{1,17},{2,18},{3,19},{4,20},{5,21},{6,22},{7,23},{8,24},{9,... | collective-permute-start | bytes 2359304 | tf_op jit(solution)/shard_map/ppermute | solution.py:290
  214.2 18.0 %collective-permute-start.45 = (bf16[288,1024]{1,0:T(8,128)(2,1)S(1)}, bf16[288,1024]{1,0:T(8,128)(2,1)S(1)}, u32[]{:S(2)}, u32[]{:S(2)}) collective-permute-start(bf16[288,1024]{1,0:T(8,128)(2,1)S(1)} %get-tuple-element.213), channel_id=1, source_target_pairs={{0,2},{1,3},{2,0},{3,1},{4,6},{5,7},{6,4},{7,5},{8,10},{9,11},{10,... | collective-permute-start | bytes 1769480 | tf_op jit(solution)/shard_map/ppermute | solution.py:290
  216.6 14.9 %collective-permute-start.44 = (bf16[128,768]{1,0:T(8,128)(2,1)S(1)}, bf16[128,768]{1,0:T(8,128)(2,1)S(1)}, u32[]{:S(2)}, u32[]{:S(2)}) collective-permute-start(bf16[128,768]{1,0:T(8,128)(2,1)S(1)} %get-tuple-element.216), channel_id=1, source_target_pairs={{0,4},{1,5},{2,6},{3,7},{4,0},{5,1},{6,2},{7,3},{8,12},{9,13},{10,... | collective-permute-start | bytes 589832 | tf_op jit(solution)/shard_map/ppermute | solution.py:290
  232.6 18.3 %collective-permute-start.50 = (bf16[256,1024]{1,0:T(8,128)(2,1)S(1)}, bf16[256,1024]{1,0:T(8,128)(2,1)S(1)}, u32[]{:S(2)}, u32[]{:S(2)}) collective-permute-start(bf16[256,1024]{1,0:T(8,128)(2,1)S(1)} %get-tuple-element.230.near_ref), channel_id=1, source_target_pairs={{0,8},{1,9},{2,10},{3,11},{4,12},{5,13},{6,14},{7,15},{8,0},{9,1},... | collective-permute-start | bytes 1572872 | tf_op jit(solution)/shard_map/ppermute | solution.py:290
  235.0 15.9 %collective-permute-start.48 = (bf16[144,1024]{1,0:T(8,128)(2,1)S(1)}, bf16[144,1024]{1,0:T(8,128)(2,1)S(1)}, u32[]{:S(2)}, u32[]{:S(2)}) collective-permute-start(bf16[144,1024]{1,0:T(8,128)(2,1)S(1)} %get-tuple-element.224), channel_id=1, source_target_pairs={{0,4},{1,5},{2,6},{3,7},{4,0},{5,1},{6,2},{7,3},{8,12},{9,13},{10,... | collective-permute-start | bytes 884744 | tf_op jit(solution)/shard_map/ppermute | solution.py:290
  (39 other events, 291.9 us)

commit v6 on v5

--- a/solution.py
+++ b/solution.py
@@ -1103,8 +1103,18 @@
             for i, part in enumerate((one, two))
         )
     )
-    pair = jnp.stack(place.by_parity(pair))
-    logits, input_grad = pair[:, :, :genes], pair[:, :, genes:]
+
+    def results_kernel(one_ref, two_ref, logits_ref, grad_ref):
+        _, _, z, _ = coordinates()
+        one, two = one_ref[...], two_ref[...]
+        for number, part in enumerate(
+            (jnp.where(z % 2 == 0, one, two), jnp.where(z % 2 == 0, two, one))
+        ):
+            at = slice(number * cells, (number + 1) * cells)
+            logits_ref[at, :], grad_ref[at, :] = part[:, :genes], part[:, genes:]
+
+    results = in_vmem(results_kernel, [((own_rows, genes), bf16)] * 2, *pair)
+    logits, input_grad = (result.reshape(seqs, cells, genes) for result in results)
 
     def qkv_out_kernel(near_ref, far_ref, out_ref):
         _, core, _, x = coordinates()

time: 275 us -> 276 us (level)
    pallas_call x42 -> x43, Pallas kernels: 35.4 us -> 36.3 us  [in_vmem(): pl.pallas_call(kernel, out_shape=shapes, in_specs=[whole] * len(operands)...]
where the time goes in v6:
time: 276 us; the launch traced here: 271 us
  waiting for transfers between devices  141 us (51%)
  starting transfers between devices  70.4 us (26%)
  Pallas kernels  36.3 us (13%)
  local copies, waits for them, and re-layouts  9.07 us (3%)
  matrix products  8.2 us (3%)
  other arithmetic  4.16 us (2%)
    ppermute x58, waiting for transfers between devices, send(): lax.ppermute(value, AXES, [(flat(p), flat(move(*p))) for p in everywhere])  132 us
    ppermute x58, starting transfers between devices, send(): lax.ppermute(value, AXES, [(flat(p), flat(move(*p))) for p in everywhere])  64.8 us
    pallas_call x43, Pallas kernels, in_vmem(): pl.pallas_call(kernel, out_shape=shapes, in_specs=[whole] * len(operands)...  36.3 us
    all_to_all x1, waiting for transfers between devices, exchange_z(): return lax.all_to_all(value, 'z', split_axis=0, concat_axis=0, tiled=True)  9.25 us
    unnamed x28, local copies, waits for them, and re-layouts  5.85 us
    all_to_all x1, starting transfers between devices, exchange_z(): return lax.all_to_all(value, 'z', split_axis=0, concat_axis=0, tiled=True)  5.55 us
  transfers between devices with their start and end apart: 59, of which 27 were waited for; matrix products, arithmetic and copies ran while one was open for 6% of the time, Pallas kernels for 9%

profile of v6, /device:TPU:1, one launch (start us, length us, event | category | flops | bytes accessed | tf_op | source)
XLA Modules:
  0.0 271.0 jit_solution(8358033977082670912)
XLA Ops:
  4.3 5.6 %all-to-all-start = ((bf16[4,112,1024]{2,1,0:T(8,128)(2,1)}), bf16[4,112,1024]{2,1,0:T(8,128)(2,1)S(1)}, u32[]{:S(2)}, u32[]{:S(2)}) async-start(bf16[4,112,1024]{2,1,0:T(8,128)(2,1)} %bitcast.10), calls=%async_computation | async-start | bytes 1835008 | tf_op jit(solution)/shard_map/all_to_all | solution.py:309
  14.4 5.7 %collective-permute-start = (bf16[64,2176]{1,0:T(8,128)(2,1)}, bf16[64,2176]{1,0:T(8,128)(2,1)}, u32[]{:S(2)}, u32[]{:S(2)}) collective-permute-start(bf16[64,2176]{1,0:T(8,128)(2,1)} %get-tuple-element.266), channel_id=1, source_target_pairs={{0,0},{1,1},{2,2},{3,3},{4,8},{5,9},{6,10},{7,11},{8,4},{9,5},{10,... | collective-permute-start | bytes 835592 | tf_op jit(solution)/shard_map/ppermute | solution.py:290
  21.1 1.9 collective-permute-done.2.theirs_ref
  24.5 9.2 %all-to-all-done = bf16[4,112,1024]{2,1,0:T(8,128)(2,1)S(1)} async-done(((bf16[4,112,1024]{2,1,0:T(8,128)(2,1)}), bf16[4,112,1024]{2,1,0:T(8,128)(2,1)S(1)}, u32[]{:S(2)}, u32[]{:S(2)}) %all-to-all-start) | async-done | bytes 917536 | tf_op jit(solution)/shard_map/all_to_all | solution.py:309
  33.7 2.4 collective-permute-start.3
  38.8 20.1 %collective-permute-done = bf16[64,2176]{1,0:T(8,128)(2,1)} collective-permute-done((bf16[64,2176]{1,0:T(8,128)(2,1)}, bf16[64,2176]{1,0:T(8,128)(2,1)}, u32[]{:S(2)}, u32[]{:S(2)}) %collective-permute-start) | collective-permute-done | bytes 278560 | tf_op jit(solution)/shard_map/ppermute | solution.py:290
  64.7 4.5 %collective-permute-done.11.refs_5_ = bf16[128,1024]{1,0:T(8,128)(2,1)S(1)} collective-permute-done((bf16[128,1024]{1,0:T(8,128)(2,1)S(1)}, bf16[128,1024]{1,0:T(8,128)(2,1)S(1)}, u32[]{:S(2)}, u32[]{:S(2)}) %collective-permute-start.11) | collective-permute-done | bytes 262176 | tf_op jit(solution)/shard_map/ppermute | solution.py:290
  70.4 4.4 %collective-permute-done.7.one_ref.refs_2_ = bf16[128,1024]{1,0:T(8,128)(2,1)S(1)} collective-permute-done((bf16[128,1024]{1,0:T(8,128)(2,1)S(1)}, bf16[128,1024]{1,0:T(8,128)(2,1)S(1)}, u32[]{:S(2)}, u32[]{:S(2)}) %collective-permute-start.7) | collective-permute-done | bytes 262176 | tf_op jit(solution)/shard_map/ppermute | solution.py:290
  74.8 4.2 %collective-permute-done.8.two_ref.refs_3_ = bf16[128,1024]{1,0:T(8,128)(2,1)S(1)} collective-permute-done((bf16[128,1024]{1,0:T(8,128)(2,1)S(1)}, bf16[128,1024]{1,0:T(8,128)(2,1)S(1)}, u32[]{:S(2)}, u32[]{:S(2)}) %collective-permute-start.8) | collective-permute-done | bytes 262176 | tf_op jit(solution)/shard_map/ppermute | solution.py:290
  79.2 3.5 %collective-permute-start.14 = (bf16[256,1024]{1,0:T(8,128)(2,1)S(1)}, bf16[256,1024]{1,0:T(8,128)(2,1)S(1)}, u32[]{:S(2)}, u32[]{:S(2)}) collective-permute-start(bf16[256,1024]{1,0:T(8,128)(2,1)S(1)} %collective-permute-done.6.refs_1_), channel_id=1, source_target_pairs={{0,2},{1,3},{2,4},{3,5},{4,6},{5,7},{6,0},{7,1},{8,10},{9,11},{10,... | collective-permute-start | bytes 1572872 | tf_op jit(solution)/shard_map/ppermute | solution.py:290
  85.1 11.0 %collective-permute-done.14.refs_2_ = bf16[256,1024]{1,0:T(8,128)(2,1)S(1)} collective-permute-done((bf16[256,1024]{1,0:T(8,128)(2,1)S(1)}, bf16[256,1024]{1,0:T(8,128)(2,1)S(1)}, u32[]{:S(2)}, u32[]{:S(2)}) %collective-permute-start.14) | collective-permute-done | bytes 524320 | tf_op jit(solution)/shard_map/ppermute | solution.py:290
  101.7 2.0 shard_map.251
  104.0 3.9 %shard_map.253 = (bf16[1024,768]{1,0:T(8,128)(2,1)S(1)}, bf16[256,1024]{1,0:T(8,128)(2,1)S(1)}, bf16[512,768]{1,0:T(8,128)(2,1)S(1)}, bf16[512,256]{1,0:T(8,128)...) custom-call(bf16[512,1024]{1,0:T(8,128)(2,1)S(1)} %get-tuple-element.148.normed_ref, ...), custom_call_target="tpu_custom_call" | custom-call | bytes 1024 | tf_op jit(solution)/shard_map/pallas_call | solution.py:368
  112.3 10.7 %collective-permute-done.22.far_ref = bf16[256,1024]{1,0:T(8,128)(2,1)S(1)} collective-permute-done((bf16[256,1024]{1,0:T(8,128)(2,1)S(1)}, bf16[256,1024]{1,0:T(8,128)(2,1)S(1)}, u32[]{:S(2)}, u32[]{:S(2)}) %collective-permute-start.22) | collective-permute-done | bytes 524320 | tf_op jit(solution)/shard_map/ppermute | solution.py:290
  128.1 6.3 %shard_map.259 = (bf16[512,1024]{1,0:T(8,128)(2,1)S(1)}, bf16[512,1024]{1,0:T(8,128)(2,1)S(1)}, f32[256,1024]{1,0:T(8,128)S(1)}, bf16[256,1024]{1,0:T(8,128)(2,1...) custom-call(bf16[256,1024]{1,0:T(8,128)(2,1)S(1)} %get-tuple-element, ...), custom_call_target="tpu_custom_call" | custom-call | bytes 1024 | tf_op jit(solution)/shard_map/pallas_call | solution.py:368
  140.9 8.8 %collective-permute-done.28.other_ref = bf16[256,1024]{1,0:T(8,128)(2,1)S(1)} collective-permute-done((bf16[256,1024]{1,0:T(8,128)(2,1)S(1)}, bf16[256,1024]{1,0:T(8,128)(2,1)S(1)}, u32[]{:S(2)}, u32[]{:S(2)}) %collective-permute-start.28) | collective-permute-done | bytes 524320 | tf_op jit(solution)/shard_map/ppermute | solution.py:290
  153.0 1.9 collective-permute-start.29
  158.6 6.0 %shard_map.264 = (bf16[512,768]{1,0:T(8,128)(2,1)S(1)}, f32[256,1024]{1,0:T(8,128)S(1)}, bf16[256,1024]{1,0:T(8,128)(2,1)S(1)}, bf16[512,1024]{1,0:T(8,128)(2,1)S(1)}) custom-call(bf16[272,1024]{1,0:T(8,128)(2,1)S(1)} %get-tuple-element.175.near_ref.two_ref, bf16[272,1024]{1,0:T(8,128)(2,1)S(1)} %collective-permute-done.29.far_ref.two_far_ref, ...), custom_call_target="tpu_custom_call" | custom-call | bytes 1024 | tf_op jit(solution)/shard_map/pallas_call | solution.py:368
  165.9 7.8 %collective-permute-done.35.other_ref = bf16[128,1024]{1,0:T(8,128)(2,1)S(1)} collective-permute-done((bf16[128,1024]{1,0:T(8,128)(2,1)S(1)}, bf16[128,1024]{1,0:T(8,128)(2,1)S(1)}, u32[]{:S(2)}, u32[]{:S(2)}) %collective-permute-start.35) | collective-permute-done | bytes 262176 | tf_op jit(solution)/shard_map/ppermute | solution.py:290
  176.3 2.0 collective-permute-start.38
  180.5 9.0 %collective-permute-done.38.one_other_ref = bf16[128,1024]{1,0:T(8,128)(2,1)S(1)} collective-permute-done((bf16[128,1024]{1,0:T(8,128)(2,1)S(1)}, bf16[128,1024]{1,0:T(8,128)(2,1)S(1)}, u32[]{:S(2)}, u32[]{:S(2)}) %collective-permute-start.38) | collective-permute-done | bytes 262176 | tf_op jit(solution)/shard_map/ppermute | solution.py:290
  190.5 2.3 collective-permute-start.39
  196.5 2.4 collective-permute-start.41
  199.0 13.0 %collective-permute-done.31.other_ref = bf16[256,768]{1,0:T(8,128)(2,1)S(1)} collective-permute-done((bf16[256,768]{1,0:T(8,128)(2,1)S(1)}, bf16[256,768]{1,0:T(8,128)(2,1)S(1)}, u32[]{:S(2)}, u32[]{:S(2)}) %collective-permute-start.31) | collective-permute-done | bytes 393248 | tf_op jit(solution)/shard_map/ppermute | solution.py:290
  218.7 12.8 %collective-permute-done.44.other_ref = bf16[128,768]{1,0:T(8,128)(2,1)S(1)} collective-permute-done((bf16[128,768]{1,0:T(8,128)(2,1)S(1)}, bf16[128,768]{1,0:T(8,128)(2,1)S(1)}, u32[]{:S(2)}, u32[]{:S(2)}) %collective-permute-start.44) | collective-permute-done | bytes 196640 | tf_op jit(solution)/shard_map/ppermute | solution.py:290
  232.6 2.3 collective-permute-start.50
  235.0 2.4 collective-permute-start.48
  238.9 4.8 %collective-permute-done.47.other_ref = bf16[128,768]{1,0:T(8,128)(2,1)S(1)} collective-permute-done((bf16[128,768]{1,0:T(8,128)(2,1)S(1)}, bf16[128,768]{1,0:T(8,128)(2,1)S(1)}, u32[]{:S(2)}, u32[]{:S(2)}) %collective-permute-start.47) | collective-permute-done | bytes 196640 | tf_op jit(solution)/shard_map/ppermute | solution.py:290
  244.9 6.0 %collective-permute-done.48.other_ref = bf16[144,1024]{1,0:T(8,128)(2,1)S(1)} collective-permute-done((bf16[144,1024]{1,0:T(8,128)(2,1)S(1)}, bf16[144,1024]{1,0:T(8,128)(2,1)S(1)}, u32[]{:S(2)}, u32[]{:S(2)}) %collective-permute-start.48) | collective-permute-done | bytes 294944 | tf_op jit(solution)/shard_map/ppermute | solution.py:290
  251.0 1.9 collective-permute-start.51
  252.9 3.1 %collective-permute-start.52 = (bf16[64,2048]{1,0:T(8,128)(2,1)S(1)}, bf16[64,2048]{1,0:T(8,128)(2,1)S(1)}, u32[]{:S(2)}, u32[]{:S(2)}) collective-permute-start(bf16[64,2048]{1,0:T(8,128)(2,1)S(1)} %pad_maximum_fusion.4), channel_id=1, source_target_pairs={{0,2},{1,3},{2,0},{3,1},{4,10},{5,11},{6,8},{7,9},{8,6},{9,7},{10,... | collective-permute-start | bytes 786440 | tf_op jit(solution)/shard_map/ppermute | solution.py:290
  257.7 3.2 %collective-permute-done.55 = bf16[128,768]{1,0:T(8,128)(2,1)S(1)} collective-permute-done((bf16[128,768]{1,0:T(8,128)(2,1)S(1)}, bf16[128,768]{1,0:T(8,128)(2,1)S(1)}, u32[]{:S(2)}, u32[]{:S(2)}) %collective-permute-start.55) | collective-permute-done | bytes 196640 | tf_op jit(solution)/shard_map/ppermute | solution.py:290
  (201 shorter events, 84.0 us)
Async XLA Ops:
  4.3 29.4 %all-to-all-start = ((bf16[4,112,1024]{2,1,0:T(8,128)(2,1)}), bf16[4,112,1024]{2,1,0:T(8,128)(2,1)S(1)}, u32[]{:S(2)}, u32[]{:S(2)}) async-start(bf16[4,112,1024]{2,1,0:T(8,128)(2,1)} %bitcast.10), calls=%async_computation | async-start | bytes 1835008 | tf_op jit(solution)/shard_map/all_to_all | solution.py:309
  14.4 44.5 %collective-permute-start = (bf16[64,2176]{1,0:T(8,128)(2,1)}, bf16[64,2176]{1,0:T(8,128)(2,1)}, u32[]{:S(2)}, u32[]{:S(2)}) collective-permute-start(bf16[64,2176]{1,0:T(8,128)(2,1)} %get-tuple-element.266), channel_id=1, source_target_pairs={{0,0},{1,1},{2,2},{3,3},{4,8},{5,9},{6,10},{7,11},{8,4},{9,5},{10,... | collective-permute-start | bytes 835592 | tf_op jit(solution)/shard_map/ppermute | solution.py:290
  20.1 40.1 %collective-permute-start.1 = (bf16[64,2176]{1,0:T(8,128)(2,1)}, bf16[64,2176]{1,0:T(8,128)(2,1)}, u32[]{:S(2)}, u32[]{:S(2)}) collective-permute-start(bf16[64,2176]{1,0:T(8,128)(2,1)} %get-tuple-element.265), channel_id=1, source_target_pairs={{0,2},{1,3},{2,0},{3,1},{4,10},{5,11},{6,8},{7,9},{8,6},{9,7},{10,... | collective-permute-start | bytes 835592 | tf_op jit(solution)/shard_map/ppermute | solution.py:290
  33.7 26.4 %collective-permute-start.3 = (bf16[128,1024]{1,0:T(8,128)(2,1)S(1)}, bf16[128,1024]{1,0:T(8,128)(2,1)S(1)}, u32[]{:S(2)}, u32[]{:S(2)}) collective-permute-start(bf16[128,1024]{1,0:T(8,128)(2,1)S(1)} %get-tuple-element.140.refs_0_), channel_id=1, source_target_pairs={{0,2},{1,3},{2,4},{3,5},{4,6},{5,7},{6,0},{7,1},{8,10},{9,11},{10,... | collective-permute-start | bytes 786440 | tf_op jit(solution)/shard_map/ppermute | solution.py:290
  37.5 25.4 %collective-permute-start.6 = (bf16[256,1024]{1,0:T(8,128)(2,1)S(1)}, bf16[256,1024]{1,0:T(8,128)(2,1)S(1)}, u32[]{:S(2)}, u32[]{:S(2)}) collective-permute-start(bf16[256,1024]{1,0:T(8,128)(2,1)S(1)} %shard_map.249.refs_0_), channel_id=1, source_target_pairs={{0,2},{1,3},{2,4},{3,5},{4,6},{5,7},{6,0},{7,1},{8,10},{9,11},{10,... | collective-permute-start | bytes 1572872 | tf_op jit(solution)/shard_map/ppermute | solution.py:290
  37.5 26.5 %collective-permute-start.5 = (bf16[256,1024]{1,0:T(8,128)(2,1)S(1)}, bf16[256,1024]{1,0:T(8,128)(2,1)S(1)}, u32[]{:S(2)}, u32[]{:S(2)}) collective-permute-start(bf16[256,1024]{1,0:T(8,128)(2,1)S(1)} %shard_map.249.refs_0_), channel_id=1, source_target_pairs={{0,16},{1,17},{2,18},{3,19},{4,20},{5,21},{6,22},{7,23},{8,24},{9,... | collective-permute-start | bytes 1572872 | tf_op jit(solution)/shard_map/ppermute | solution.py:290
  59.0 20.1 %collective-permute-start.9 = (bf16[448,1024]{1,0:T(8,128)(2,1)S(1)}, bf16[448,1024]{1,0:T(8,128)(2,1)S(1)}, u32[]{:S(2)}, u32[]{:S(2)}) collective-permute-start(bf16[448,1024]{1,0:T(8,128)(2,1)S(1)} %bitcast.45), channel_id=1, source_target_pairs={{0,1},{1,0},{2,3},{3,2},{4,5},{5,4},{6,7},{7,6},{8,9},{9,8},{10,11... | collective-permute-start | bytes 2752520 | tf_op jit(solution)/shard_map/ppermute | solution.py:290
  61.3 17.7 %collective-permute-start.4 = (bf16[128,2176]{1,0:T(8,128)(2,1)S(1)}, bf16[128,2176]{1,0:T(8,128)(2,1)S(1)}, u32[]{:S(2)}, u32[]{:S(2)}) collective-permute-start(bf16[128,2176]{1,0:T(8,128)(2,1)S(1)} %pad_maximum_fusion.2), channel_id=1, source_target_pairs={{0,1},{1,0},{2,3},{3,2},{4,5},{5,4},{6,7},{7,6},{8,9},{9,8},{10,11... | collective-permute-start | bytes 1671176 | tf_op jit(solution)/shard_map/ppermute | solution.py:290
  62.8 16.2 %collective-permute-start.10 = (bf16[256,1024]{1,0:T(8,128)(2,1)S(1)}, bf16[256,1024]{1,0:T(8,128)(2,1)S(1)}, u32[]{:S(2)}, u32[]{:S(2)}) collective-permute-start(bf16[256,1024]{1,0:T(8,128)(2,1)S(1)} %collective-permute-done.6.refs_1_), channel_id=1, source_target_pairs={{0,16},{1,17},{2,18},{3,19},{4,20},{5,21},{6,22},{7,23},{8,24},{9,... | collective-permute-start | bytes 1572872 | tf_op jit(solution)/shard_map/ppermute | solution.py:290
  79.1 18.4 %collective-permute-start.12 = (bf16[256,2176]{1,0:T(8,128)(2,1)S(1)}, bf16[256,2176]{1,0:T(8,128)(2,1)S(1)}, u32[]{:S(2)}, u32[]{:S(2)}) collective-permute-start(bf16[256,2176]{1,0:T(8,128)(2,1)S(1)} %constant_dynamic-update-slice_fusion.near_ref.near_cells_ref), channel_id=1, source_target_pairs={{0,8},{1,9},{2,10},{3,11},{4,12},{5,13},{6,14},{7,15},{8,0},{9,1},... | collective-permute-start | bytes 3342344 | tf_op jit(solution)/shard_map/ppermute | solution.py:290
  79.2 16.9 %collective-permute-start.14 = (bf16[256,1024]{1,0:T(8,128)(2,1)S(1)}, bf16[256,1024]{1,0:T(8,128)(2,1)S(1)}, u32[]{:S(2)}, u32[]{:S(2)}) collective-permute-start(bf16[256,1024]{1,0:T(8,128)(2,1)S(1)} %collective-permute-done.6.refs_1_), channel_id=1, source_target_pairs={{0,2},{1,3},{2,4},{3,5},{4,6},{5,7},{6,0},{7,1},{8,10},{9,11},{10,... | collective-permute-start | bytes 1572872 | tf_op jit(solution)/shard_map/ppermute | solution.py:290
  83.0 21.0 %collective-permute-start.15 = (bf16[256,1024]{1,0:T(8,128)(2,1)S(1)}, bf16[256,1024]{1,0:T(8,128)(2,1)S(1)}, u32[]{:S(2)}, u32[]{:S(2)}) collective-permute-start(bf16[256,1024]{1,0:T(8,128)(2,1)S(1)} %shard_map.252), channel_id=1, source_target_pairs={{0,16},{1,17},{2,18},{3,19},{4,20},{5,21},{6,22},{7,23},{8,24},{9,... | collective-permute-start | bytes 1572872 | tf_op jit(solution)/shard_map/ppermute | solution.py:290
  84.4 17.4 %collective-permute-start.13 = (bf16[512,1024]{1,0:T(8,128)(2,1)S(1)}, bf16[512,1024]{1,0:T(8,128)(2,1)S(1)}, u32[]{:S(2)}, u32[]{:S(2)}) collective-permute-start(bf16[512,1024]{1,0:T(8,128)(2,1)S(1)} %get-tuple-element.142.enc_near_ref), channel_id=1, source_target_pairs={{0,8},{1,9},{2,10},{3,11},{4,12},{5,13},{6,14},{7,15},{8,0},{9,1},... | collective-permute-start | bytes 3145736 | tf_op jit(solution)/shard_map/ppermute | solution.py:290
  96.1 14.4 %collective-permute-start.17 = (bf16[256,1024]{1,0:T(8,128)(2,1)S(1)}, bf16[256,1024]{1,0:T(8,128)(2,1)S(1)}, u32[]{:S(2)}, u32[]{:S(2)}) collective-permute-start(bf16[256,1024]{1,0:T(8,128)(2,1)S(1)} %collective-permute-done.14.refs_2_), channel_id=1, source_target_pairs={{0,2},{1,3},{2,4},{3,5},{4,6},{5,7},{6,0},{7,1},{8,10},{9,11},{10,... | collective-permute-start | bytes 1572872 | tf_op jit(solution)/shard_map/ppermute | solution.py:290
  109.7 14.6 %collective-permute-start.20 = (bf16[256,1024]{1,0:T(8,128)(2,1)S(1)}, bf16[256,1024]{1,0:T(8,128)(2,1)S(1)}, u32[]{:S(2)}, u32[]{:S(2)}) collective-permute-start(bf16[256,1024]{1,0:T(8,128)(2,1)S(1)} %collective-permute-done.18.refs_6_), channel_id=1, source_target_pairs={{0,2},{1,3},{2,4},{3,5},{4,6},{5,7},{6,0},{7,1},{8,10},{9,11},{10,... | collective-permute-start | bytes 1572872 | tf_op jit(solution)/shard_map/ppermute | solution.py:290
  154.9 18.8 %collective-permute-start.33 = (bf16[256,1024]{1,0:T(8,128)(2,1)S(1)}, bf16[256,1024]{1,0:T(8,128)(2,1)S(1)}, u32[]{:S(2)}, u32[]{:S(2)}) collective-permute-start(bf16[256,1024]{1,0:T(8,128)(2,1)S(1)} %get-tuple-element.184), channel_id=1, source_target_pairs={{0,16},{1,17},{2,18},{3,19},{4,20},{5,21},{6,22},{7,23},{8,24},{9,... | collective-permute-start | bytes 1572872 | tf_op jit(solution)/shard_map/ppermute | solution.py:290
  155.7 18.8 %collective-permute-start.34 = (bf16[256,1024]{1,0:T(8,128)(2,1)S(1)}, bf16[256,1024]{1,0:T(8,128)(2,1)S(1)}, u32[]{:S(2)}, u32[]{:S(2)}) collective-permute-start(bf16[256,1024]{1,0:T(8,128)(2,1)S(1)} %get-tuple-element.186), channel_id=1, source_target_pairs={{0,2},{1,3},{2,0},{3,1},{4,6},{5,7},{6,4},{7,5},{8,10},{9,11},{10,... | collective-permute-start | bytes 1572872 | tf_op jit(solution)/shard_map/ppermute | solution.py:290
  157.2 17.3 %collective-permute-start.36 = (bf16[256,1024]{1,0:T(8,128)(2,1)S(1)}, bf16[256,1024]{1,0:T(8,128)(2,1)S(1)}, u32[]{:S(2)}, u32[]{:S(2)}) collective-permute-start(bf16[256,1024]{1,0:T(8,128)(2,1)S(1)} %shard_map.261.mine_ref), channel_id=1, source_target_pairs={{0,1},{1,0},{2,3},{3,2},{4,5},{5,4},{6,7},{7,6},{8,9},{9,8},{10,11... | collective-permute-start | bytes 1572872 | tf_op jit(solution)/shard_map/ppermute | solution.py:290
  157.6 16.2 %collective-permute-start.35 = (bf16[128,1024]{1,0:T(8,128)(2,1)S(1)}, bf16[128,1024]{1,0:T(8,128)(2,1)S(1)}, u32[]{:S(2)}, u32[]{:S(2)}) collective-permute-start(bf16[128,1024]{1,0:T(8,128)(2,1)S(1)} %get-tuple-element.189), channel_id=1, source_target_pairs={{0,4},{1,5},{2,6},{3,7},{4,0},{5,1},{6,2},{7,3},{8,12},{9,13},{10,... | collective-permute-start | bytes 786440 | tf_op jit(solution)/shard_map/ppermute | solution.py:290
  175.2 14.3 %collective-permute-start.37 = (bf16[256,1024]{1,0:T(8,128)(2,1)S(1)}, bf16[256,1024]{1,0:T(8,128)(2,1)S(1)}, u32[]{:S(2)}, u32[]{:S(2)}) collective-permute-start(bf16[256,1024]{1,0:T(8,128)(2,1)S(1)} %shard_map.267.refs_1_), channel_id=1, source_target_pairs={{0,1},{1,0},{2,3},{3,2},{4,5},{5,4},{6,7},{7,6},{8,9},{9,8},{10,11... | collective-permute-start | bytes 1572872 | tf_op jit(solution)/shard_map/ppermute | solution.py:290
  175.6 20.4 %collective-permute-start.30 = (bf16[512,768]{1,0:T(8,128)(2,1)S(1)}, bf16[512,768]{1,0:T(8,128)(2,1)S(1)}, u32[]{:S(2)}, u32[]{:S(2)}) collective-permute-start(bf16[512,768]{1,0:T(8,128)(2,1)S(1)} %convolution_convert_fusion.3), channel_id=1, source_target_pairs={{0,16},{1,17},{2,18},{3,19},{4,20},{5,21},{6,22},{7,23},{8,24},{9,... | collective-permute-start | bytes 2359304 | tf_op jit(solution)/shard_map/ppermute | solution.py:290
  179.4 16.9 %collective-permute-start.40 = (bf16[256,1024]{1,0:T(8,128)(2,1)S(1)}, bf16[256,1024]{1,0:T(8,128)(2,1)S(1)}, u32[]{:S(2)}, u32[]{:S(2)}) collective-permute-start(bf16[256,1024]{1,0:T(8,128)(2,1)S(1)} %get-tuple-element.203), channel_id=1, source_target_pairs={{0,2},{1,3},{2,0},{3,1},{4,6},{5,7},{6,4},{7,5},{8,10},{9,11},{10,... | collective-permute-start | bytes 1572872 | tf_op jit(solution)/shard_map/ppermute | solution.py:290
  190.5 21.6 %collective-permute-start.39 = (bf16[272,1024]{1,0:T(8,128)(2,1)S(1)}, bf16[272,1024]{1,0:T(8,128)(2,1)S(1)}, u32[]{:S(2)}, u32[]{:S(2)}) collective-permute-start(bf16[272,1024]{1,0:T(8,128)(2,1)S(1)} %shard_map.269.one_ref), channel_id=1, source_target_pairs={{0,8},{1,9},{2,10},{3,11},{4,12},{5,13},{6,14},{7,15},{8,0},{9,1},... | collective-permute-start | bytes 1671176 | tf_op jit(solution)/shard_map/ppermute | solution.py:290
  195.1 17.0 %collective-permute-start.43 = (bf16[256,1024]{1,0:T(8,128)(2,1)S(1)}, bf16[256,1024]{1,0:T(8,128)(2,1)S(1)}, u32[]{:S(2)}, u32[]{:S(2)}) collective-permute-start(bf16[256,1024]{1,0:T(8,128)(2,1)S(1)} %get-tuple-element.214), channel_id=1, source_target_pairs={{0,16},{1,17},{2,18},{3,19},{4,20},{5,21},{6,22},{7,23},{8,24},{9,... | collective-permute-start | bytes 1572872 | tf_op jit(solution)/shard_map/ppermute | solution.py:290
  196.3 15.8 %collective-permute-start.31 = (bf16[256,768]{1,0:T(8,128)(2,1)S(1)}, bf16[256,768]{1,0:T(8,128)(2,1)S(1)}, u32[]{:S(2)}, u32[]{:S(2)}) collective-permute-start(bf16[256,768]{1,0:T(8,128)(2,1)S(1)} %get-tuple-element.181), channel_id=1, source_target_pairs={{0,2},{1,3},{2,0},{3,1},{4,6},{5,7},{6,4},{7,5},{8,10},{9,11},{10,... | collective-permute-start | bytes 1179656 | tf_op jit(solution)/shard_map/ppermute | solution.py:290
  196.5 15.5 %collective-permute-start.41 = (bf16[128,1024]{1,0:T(8,128)(2,1)S(1)}, bf16[128,1024]{1,0:T(8,128)(2,1)S(1)}, u32[]{:S(2)}, u32[]{:S(2)}) collective-permute-start(bf16[128,1024]{1,0:T(8,128)(2,1)S(1)} %get-tuple-element.205), channel_id=1, source_target_pairs={{0,4},{1,5},{2,6},{3,7},{4,0},{5,1},{6,2},{7,3},{8,12},{9,13},{10,... | collective-permute-start | bytes 786440 | tf_op jit(solution)/shard_map/ppermute | solution.py:290
  213.5 18.8 %collective-permute-start.46 = (bf16[384,1024]{1,0:T(8,128)(2,1)S(1)}, bf16[384,1024]{1,0:T(8,128)(2,1)S(1)}, u32[]{:S(2)}, u32[]{:S(2)}) collective-permute-start(bf16[384,1024]{1,0:T(8,128)(2,1)S(1)} %shard_map.277.own_ref), channel_id=1, source_target_pairs={{0,16},{1,17},{2,18},{3,19},{4,20},{5,21},{6,22},{7,23},{8,24},{9,... | collective-permute-start | bytes 2359304 | tf_op jit(solution)/shard_map/ppermute | solution.py:290
  214.2 18.0 %collective-permute-start.45 = (bf16[288,1024]{1,0:T(8,128)(2,1)S(1)}, bf16[288,1024]{1,0:T(8,128)(2,1)S(1)}, u32[]{:S(2)}, u32[]{:S(2)}) collective-permute-start(bf16[288,1024]{1,0:T(8,128)(2,1)S(1)} %get-tuple-element.215), channel_id=1, source_target_pairs={{0,2},{1,3},{2,0},{3,1},{4,6},{5,7},{6,4},{7,5},{8,10},{9,11},{10,... | collective-permute-start | bytes 1769480 | tf_op jit(solution)/shard_map/ppermute | solution.py:290
  216.6 14.9 %collective-permute-start.44 = (bf16[128,768]{1,0:T(8,128)(2,1)S(1)}, bf16[128,768]{1,0:T(8,128)(2,1)S(1)}, u32[]{:S(2)}, u32[]{:S(2)}) collective-permute-start(bf16[128,768]{1,0:T(8,128)(2,1)S(1)} %get-tuple-element.218), channel_id=1, source_target_pairs={{0,4},{1,5},{2,6},{3,7},{4,0},{5,1},{6,2},{7,3},{8,12},{9,13},{10,... | collective-permute-start | bytes 589832 | tf_op jit(solution)/shard_map/ppermute | solution.py:290
  232.6 18.3 %collective-permute-start.50 = (bf16[256,1024]{1,0:T(8,128)(2,1)S(1)}, bf16[256,1024]{1,0:T(8,128)(2,1)S(1)}, u32[]{:S(2)}, u32[]{:S(2)}) collective-permute-start(bf16[256,1024]{1,0:T(8,128)(2,1)S(1)} %get-tuple-element.232.near_ref), channel_id=1, source_target_pairs={{0,8},{1,9},{2,10},{3,11},{4,12},{5,13},{6,14},{7,15},{8,0},{9,1},... | collective-permute-start | bytes 1572872 | tf_op jit(solution)/shard_map/ppermute | solution.py:290
  235.0 15.9 %collective-permute-start.48 = (bf16[144,1024]{1,0:T(8,128)(2,1)S(1)}, bf16[144,1024]{1,0:T(8,128)(2,1)S(1)}, u32[]{:S(2)}, u32[]{:S(2)}) collective-permute-start(bf16[144,1024]{1,0:T(8,128)(2,1)S(1)} %get-tuple-element.226), channel_id=1, source_target_pairs={{0,4},{1,5},{2,6},{3,7},{4,0},{5,1},{6,2},{7,3},{8,12},{9,13},{10,... | collective-permute-start | bytes 884744 | tf_op jit(solution)/shard_map/ppermute | solution.py:290
  251.0 14.2 %collective-permute-start.51 = (bf16[64,2048]{1,0:T(8,128)(2,1)S(1)}, bf16[64,2048]{1,0:T(8,128)(2,1)S(1)}, u32[]{:S(2)}, u32[]{:S(2)}) collective-permute-start(bf16[64,2048]{1,0:T(8,128)(2,1)S(1)} %pad_maximum_fusion.3), channel_id=1, source_target_pairs={{0,0},{1,1},{2,2},{3,3},{4,8},{5,9},{6,10},{7,11},{8,4},{9,5},{10,... | collective-permute-start | bytes 786440 | tf_op jit(solution)/shard_map/ppermute | solution.py:290
  (39 other events, 294.0 us)
